TPU v7x, 32 devices: a whole 2x2x4 slice. The times are simulated.
32 devices in a mesh: rep: 4 (over y, x), shard: 8 (over z, core).
Axes of the slice: x: 2, y: 2, z: 4, core: 2. Of those that a mesh axis runs over, the one named last changes fastest.
Arguments:
- tokens_in: bfloat16 [8, 2048, 1536], P('shard', 'rep'), may hold values from -6 to 6
- lengths: int32 [8], P('shard'), may hold values from 512 to 2048, as said below
- cotangent: bfloat16 [8, 2048, 1536], P('shard', 'rep'), may hold values from -6 to 6
- attn_norm: bfloat16 [1536], P('shard'), may hold values from 0.5 to 1.5
- query_proj: bfloat16 [1536, 1536], P('shard'), may hold values from -0.15625 to 0.15625
- key_proj: bfloat16 [1536, 128], P('shard'), may hold values from -0.15625 to 0.15625
- value_proj: bfloat16 [1536, 128], P('shard'), may hold values from -0.15625 to 0.15625
- attn_out: bfloat16 [1536, 1536], P('shard'), may hold values from -2.5 to 2.5
- first_norm: bfloat16 [1536], P('shard'), may hold values from 0.5 to 1.5
- first_gate: bfloat16 [1536, 4608], P('shard'), may hold values from -0.15625 to 0.15625
- first_up: bfloat16 [1536, 4608], P('shard'), may hold values from -0.15625 to 0.15625
- first_down: bfloat16 [4608, 1536], P('shard'), may hold values from -0.09375 to 0.09375
- mixer_norm: bfloat16 [1536], P('shard'), may hold values from 0.5 to 1.5
- branch_proj: bfloat16 [1536, 2048], P('shard'), may hold values from -0.15625 to 0.15625
- gated_proj: bfloat16 [1536, 2048], P('shard'), may hold values from -0.15625 to 0.15625
- conv_taps: bfloat16 [2048, 4], P('shard'), may hold values from -3 to 3
- rate_gate: bfloat16 [2048, 128], P('shard'), may hold values from -0.5 to 0.5
- input_gate: bfloat16 [2048, 128], P('shard'), may hold values from -0.5 to 0.5
- decay_rate: bfloat16 [2048], P('shard'), may hold values from 9.727478e-05 to 0.019897461
- mixer_out: bfloat16 [2048, 1536], P('shard'), may hold values from -0.25 to 0.25
- second_norm: bfloat16 [1536], P('shard'), may hold values from 0.5 to 1.5
- second_gate: bfloat16 [1536, 4608], P('shard'), may hold values from -0.15625 to 0.15625
- second_up: bfloat16 [1536, 4608], P('shard'), may hold values from -0.15625 to 0.15625
- second_down: bfloat16 [4608, 1536], P('shard'), may hold values from -0.09375 to 0.09375
Outputs:
- out: bfloat16 [8, 2048, 1536], P('shard', 'rep')
- input_grad: bfloat16 [8, 2048, 1536], P('shard', 'rep')
- grad_attn_norm: float32 [1536], P('shard')
- grad_query_proj: float32 [1536, 1536], P('shard')
- grad_key_proj: float32 [1536, 128], P('shard')
- grad_value_proj: float32 [1536, 128], P('shard')
- grad_attn_out: float32 [1536, 1536], P('shard')
- grad_first_norm: float32 [1536], P('shard')
- grad_first_gate: float32 [1536, 4608], P('shard')
- grad_first_up: float32 [1536, 4608], P('shard')
- grad_first_down: float32 [4608, 1536], P('shard')
- grad_mixer_norm: float32 [1536], P('shard')
- grad_branch_proj: float32 [1536, 2048], P('shard')
- grad_gated_proj: float32 [1536, 2048], P('shard')
- grad_conv_taps: float32 [2048, 4], P('shard')
- grad_rate_gate: float32 [2048, 128], P('shard')
- grad_input_gate: float32 [2048, 128], P('shard')
- grad_decay_rate: float32 [2048], P('shard')
- grad_mixer_out: float32 [2048, 1536], P('shard')
- grad_second_norm: float32 [1536], P('shard')
- grad_second_gate: float32 [1536, 4608], P('shard')
- grad_second_up: float32 [1536, 4608], P('shard')
- grad_second_down: float32 [4608, 1536], P('shard')
Inputs may be any that keep to these rules, and one draw needn't show every extreme that they name: `lengths`: valid slots of each sequence; the slots from this length on are padding. One sequence, drawn from the seed, fills all 2048 slots.
All inputs are finite; a program needn't handle non-finite values.
Results may differ from a plain program's by a relative error of at most 0.02.
Values may be sent and summed in bfloat16 or wider, within the bound.
A program may use at most 512 MiB of HBM per device.

v0:
```python
import math

import jax
import jax.numpy as jnp
from jax import lax
from jax.sharding import PartitionSpec as P

WINDOW = 1024


EPSILON = 1e-06


def shifted(x, axis, by):
    size = lax.axis_size(axis)
    pairs = [(i, i + by) for i in range(size) if 0 <= i + by < size]
    return lax.ppermute(x, axis, pairs)


def carried_in(part, axis, combine, identity, reverse):
    count = lax.axis_size(axis)
    place = lax.axis_index(axis)
    ahead = count - 1 - place if reverse else place
    gathered = jax.tree.map(lambda a: lax.all_gather(a, axis), part)
    state = jax.tree.map(lambda a, e: jnp.zeros_like(a) + jnp.asarray(e, a.dtype), part, identity)

    def one(turn, state):
        source = count - 1 - turn if reverse else turn
        return combine(
            state, jax.tree.map(lambda a: lax.dynamic_index_in_dim(a, source, 0, False), gathered)
        )

    return lax.fori_loop(0, ahead, one, state)


def rms_norm(values, norm_gain):
    return (
        values * lax.rsqrt(jnp.mean(values * values, axis=-1, keepdims=True) + EPSILON) * norm_gain
    )


def gelu_tanh(values):
    return jax.nn.gelu(values, approximate=True)


def mlp_middle(gate_pre, up_pre):
    return gelu_tanh(gate_pre) * up_pre


def lru_gates(rate_pre, input_pre, decay_w, conv_out):
    log_coef = -8.0 * jax.nn.sigmoid(rate_pre) * decay_w
    lru_coef = jnp.exp(log_coef)
    lru_drive = jnp.sqrt(-jnp.expm1(2.0 * log_coef)) * jax.nn.sigmoid(input_pre) * conv_out
    return (lru_coef, lru_drive)


def compose(first_pair, second_pair):
    return (first_pair[0] * second_pair[0], second_pair[0] * first_pair[1] + second_pair[1])


def linear_scan(lru_coef, lru_drive):
    return lax.associative_scan(compose, (lru_coef, lru_drive), axis=0)


def matmul(first_op, second_op):
    return jnp.dot(first_op, second_op, preferred_element_type=jnp.float32)


def matmul_left(first_op, second_op):
    return lax.dot_general(
        first_op, second_op, (((0,), (0,)), ((), ())), preferred_element_type=jnp.float32
    )


def matmul_right(first_op, second_op):
    return lax.dot_general(
        first_op, second_op, (((1,), (1,)), ((), ())), preferred_element_type=jnp.float32
    )


def rounded(values):
    return values.astype(jnp.bfloat16).astype(jnp.float32)


def window_scores(query_heads, key_win, start_row):
    row_count = query_heads.shape[0]
    score_scale = 1.0 / math.sqrt(query_heads.shape[2])
    raw_scores = (
        jnp.einsum("thd,kd->htk", query_heads, key_win, preferred_element_type=jnp.float32)
        * score_scale
    )
    row_pos = start_row + jnp.arange(row_count, dtype=jnp.int32)[:, None]
    col_pos = start_row - WINDOW + jnp.arange(key_win.shape[0], dtype=jnp.int32)[None, :]
    allowed = (col_pos <= row_pos) & (col_pos > row_pos - WINDOW) & (col_pos >= 0)
    return jnp.where(allowed[None], raw_scores, -1e30)


def mlp_forward(resid, norm_gain, gate_full, up_full, down_full):
    normed_low = rms_norm(resid, norm_gain).astype(jnp.bfloat16)
    gate_pre = matmul(normed_low, gate_full)
    up_pre = matmul(normed_low, up_full)
    hidden_low = mlp_middle(gate_pre, up_pre).astype(jnp.bfloat16)
    return (resid + matmul(hidden_low, down_full), (normed_low, gate_pre, up_pre, hidden_low))


def mlp_backward(resid, norm_gain, gate_full, up_full, down_full, kept_vals, back_out):
    normed_low, gate_pre, up_pre, hidden_low = kept_vals
    out_low = back_out.astype(jnp.bfloat16)
    grad_down = matmul_left(hidden_low, out_low)
    back_hidden = rounded(matmul_right(out_low, down_full))
    middle_pull = jax.vjp(mlp_middle, gate_pre, up_pre)[1]
    back_gate, back_up = middle_pull(back_hidden)
    gate_low = back_gate.astype(jnp.bfloat16)
    up_low = back_up.astype(jnp.bfloat16)
    grad_gate = matmul_left(normed_low, gate_low)
    grad_up = matmul_left(normed_low, up_low)
    back_normed = matmul_right(gate_low, gate_full) + matmul_right(up_low, up_full)
    norm_pull = jax.vjp(rms_norm, resid, norm_gain)[1]
    back_resid, grad_gain = norm_pull(back_normed)
    return (back_out + back_resid, (grad_gain, grad_gate, grad_up, grad_down))


def on_device(
    tokens_in,
    lengths,
    cotangent,
    attn_norm,
    query_proj,
    key_proj,
    value_proj,
    attn_out,
    first_norm,
    first_gate,
    first_up,
    first_down,
    mixer_norm,
    branch_proj,
    gated_proj,
    conv_taps,
    rate_gate,
    input_gate,
    decay_rate,
    mixer_out,
    second_norm,
    second_gate,
    second_up,
    second_down,
):
    row_count = tokens_in.shape[1]
    model_width = tokens_in.shape[2]
    rep_count = lax.axis_size("rep")
    start_row = lax.axis_index("rep") * row_count
    positions = start_row + jnp.arange(row_count, dtype=jnp.int32)
    valid_mask = (positions < lengths[0]).astype(jnp.float32)[:, None]
    inputs = tokens_in.reshape(row_count, model_width).astype(jnp.float32)
    (
        attn_gain,
        query_full,
        key_full,
        value_full,
        attn_full,
        first_gain,
        first_gate_full,
        first_up_full,
        first_down_full,
    ) = (
        lax.all_gather(attn_norm, "shard", axis=0, tiled=True),
        lax.all_gather(query_proj, "shard", axis=0, tiled=True),
        lax.all_gather(key_proj, "shard", axis=0, tiled=True),
        lax.all_gather(value_proj, "shard", axis=0, tiled=True),
        lax.all_gather(attn_out, "shard", axis=0, tiled=True),
        lax.all_gather(first_norm, "shard", axis=0, tiled=True),
        lax.all_gather(first_gate, "shard", axis=0, tiled=True),
        lax.all_gather(first_up, "shard", axis=0, tiled=True),
        lax.all_gather(first_down, "shard", axis=0, tiled=True),
    )
    gain_attn = attn_gain.astype(jnp.float32)
    gain_first = first_gain.astype(jnp.float32)
    attn_normed = rms_norm(inputs, gain_attn).astype(jnp.bfloat16)
    query_rows = matmul(attn_normed, query_full).astype(jnp.bfloat16)
    key_rows = matmul(attn_normed, key_full).astype(jnp.bfloat16)
    value_rows = matmul(attn_normed, value_full).astype(jnp.bfloat16)
    key_seq, value_seq = (
        lax.all_gather(key_rows, "rep", axis=0, tiled=True),
        lax.all_gather(value_rows, "rep", axis=0, tiled=True),
    )
    head_size = key_rows.shape[1]
    head_count = query_rows.shape[1] // head_size
    front_pad = jnp.zeros((WINDOW, head_size), jnp.bfloat16)
    key_win = lax.dynamic_slice_in_dim(
        jnp.concatenate([front_pad, key_seq], axis=0), start_row, WINDOW + row_count, 0
    )
    value_win = lax.dynamic_slice_in_dim(
        jnp.concatenate([front_pad, value_seq], axis=0), start_row, WINDOW + row_count, 0
    )
    query_heads = query_rows.reshape(row_count, head_count, head_size)
    scores = window_scores(query_heads, key_win, start_row)
    row_peak = jnp.max(scores, axis=-1, keepdims=True)
    exp_scores = jnp.exp(scores - row_peak)
    exp_total = jnp.sum(exp_scores, axis=-1, keepdims=True)
    log_total = row_peak + jnp.log(exp_total)
    probs_low = (exp_scores / exp_total).astype(jnp.bfloat16)
    attended = jnp.einsum("htk,kd->thd", probs_low, value_win, preferred_element_type=jnp.float32)
    attended_low = attended.reshape(row_count, head_count * head_size).astype(jnp.bfloat16)
    resid_one = inputs + matmul(attended_low, attn_full)
    middle, first_kept = mlp_forward(
        resid_one, gain_first, first_gate_full, first_up_full, first_down_full
    )
    (
        mix_gain,
        branch_full,
        gated_full,
        conv_full,
        rate_full,
        input_full,
        decay_full,
        mix_full,
        second_gain,
        second_gate_full,
        second_up_full,
        second_down_full,
    ) = (
        lax.all_gather(mixer_norm, "shard", axis=0, tiled=True),
        lax.all_gather(branch_proj, "shard", axis=0, tiled=True),
        lax.all_gather(gated_proj, "shard", axis=0, tiled=True),
        lax.all_gather(conv_taps, "shard", axis=0, tiled=True),
        lax.all_gather(rate_gate, "shard", axis=0, tiled=True),
        lax.all_gather(input_gate, "shard", axis=0, tiled=True),
        lax.all_gather(decay_rate, "shard", axis=0, tiled=True),
        lax.all_gather(mixer_out, "shard", axis=0, tiled=True),
        lax.all_gather(second_norm, "shard", axis=0, tiled=True),
        lax.all_gather(second_gate, "shard", axis=0, tiled=True),
        lax.all_gather(second_up, "shard", axis=0, tiled=True),
        lax.all_gather(second_down, "shard", axis=0, tiled=True),
    )
    gain_mix = mix_gain.astype(jnp.float32)
    gain_second = second_gain.astype(jnp.float32)
    mix_normed = rms_norm(middle, gain_mix).astype(jnp.bfloat16)
    branch = matmul(mix_normed, branch_full)
    gated_pre = matmul(mix_normed, gated_full)
    lru_width = branch.shape[1]
    block_width = rate_full.shape[1]
    block_count = lru_width // block_width
    conv_w = conv_full.astype(jnp.float32)
    tap_count = conv_w.shape[1]
    tail_rows = shifted(branch[row_count - (tap_count - 1) :], "rep", 1)
    extended = jnp.concatenate([tail_rows, branch], axis=0)
    conv_out = jnp.zeros((row_count, lru_width), jnp.float32)
    for offset in range(tap_count):
        conv_out = (
            conv_out
            + conv_w[:, offset]
            * extended[tap_count - 1 - offset : tap_count - 1 - offset + row_count]
        )
    conv_low = conv_out.astype(jnp.bfloat16).reshape(row_count, block_count, block_width)
    rate_blocks = rate_full.reshape(block_count, block_width, block_width)
    input_blocks = input_full.reshape(block_count, block_width, block_width)
    rate_pre = jnp.einsum(
        "tbi,bij->tbj", conv_low, rate_blocks, preferred_element_type=jnp.float32
    ).reshape(row_count, lru_width)
    input_pre = jnp.einsum(
        "tbi,bij->tbj", conv_low, input_blocks, preferred_element_type=jnp.float32
    ).reshape(row_count, lru_width)
    decay_w = decay_full.astype(jnp.float32)
    lru_coef, lru_drive = lru_gates(rate_pre, input_pre, decay_w, conv_out)
    cum_coef, local_state = linear_scan(lru_coef, lru_drive)
    scan_identity = (jnp.ones((lru_width,), jnp.float32), jnp.zeros((lru_width,), jnp.float32))
    start_state = carried_in((cum_coef[-1], local_state[-1]), "rep", compose, scan_identity, False)[
        1
    ]
    lru_state = local_state + cum_coef * start_state[None, :]
    gated_act = gelu_tanh(gated_pre)
    mix_low = (lru_state * gated_act).astype(jnp.bfloat16)
    resid_two = middle + matmul(mix_low, mix_full)
    final_rows, second_kept = mlp_forward(
        resid_two, gain_second, second_gate_full, second_up_full, second_down_full
    )
    out_tokens = final_rows.astype(jnp.bfloat16).reshape(1, row_count, model_width)
    back_final = cotangent.reshape(row_count, model_width).astype(jnp.float32) * valid_mask
    back_two, second_grads = mlp_backward(
        resid_two,
        gain_second,
        second_gate_full,
        second_up_full,
        second_down_full,
        second_kept,
        back_final,
    )
    mix_back_low = back_two.astype(jnp.bfloat16)
    grad_mix_out = matmul_left(mix_low, mix_back_low)
    back_mixed = rounded(matmul_right(mix_back_low, mix_full))
    back_state = back_mixed * gated_act
    gelu_pull = jax.vjp(gelu_tanh, gated_pre)[1]
    gated_back_low = gelu_pull(back_mixed * lru_state)[0].astype(jnp.bfloat16)
    coef_next = jnp.concatenate([lru_coef[1:], jnp.ones((1, lru_width), jnp.float32)], axis=0)
    rev_prod, rev_local = linear_scan(jnp.flip(coef_next, 0), jnp.flip(back_state, 0))
    later_prod = jnp.flip(rev_prod, 0)
    local_adjoint = jnp.flip(rev_local, 0)
    carry_in = carried_in(
        (cum_coef[-1], lru_coef[0] * local_adjoint[0]), "rep", compose, scan_identity, True
    )[1]
    adjoint = local_adjoint + later_prod * carry_in[None, :]
    prev_state = jnp.concatenate([start_state[None, :], lru_state[:-1]], axis=0)
    gates_pull = jax.vjp(lru_gates, rate_pre, input_pre, decay_w, conv_out)[1]
    back_rate, back_input, grad_decay, back_conv_direct = gates_pull(
        (adjoint * prev_state, adjoint)
    )
    rate_back_low = back_rate.astype(jnp.bfloat16).reshape(row_count, block_count, block_width)
    input_back_low = back_input.astype(jnp.bfloat16).reshape(row_count, block_count, block_width)
    grad_rate = jnp.einsum(
        "tbi,tbj->bij", conv_low, rate_back_low, preferred_element_type=jnp.float32
    ).reshape(lru_width, block_width)
    grad_input = jnp.einsum(
        "tbi,tbj->bij", conv_low, input_back_low, preferred_element_type=jnp.float32
    ).reshape(lru_width, block_width)
    gate_back_conv = jnp.einsum(
        "tbj,bij->tbi", rate_back_low, rate_blocks, preferred_element_type=jnp.float32
    ) + jnp.einsum("tbj,bij->tbi", input_back_low, input_blocks, preferred_element_type=jnp.float32)
    back_conv = back_conv_direct + gate_back_conv.reshape(row_count, lru_width)
    tap_pad = jnp.zeros((tap_count - 1, lru_width), jnp.float32)
    padded_back = jnp.concatenate([tap_pad, back_conv, tap_pad], axis=0)
    back_extended = jnp.zeros((row_count + tap_count - 1, lru_width), jnp.float32)
    tap_grads = []
    for offset in range(tap_count):
        back_extended = (
            back_extended
            + conv_w[:, offset] * padded_back[offset : offset + row_count + tap_count - 1]
        )
        tap_grads.append(
            jnp.sum(
                back_conv * extended[tap_count - 1 - offset : tap_count - 1 - offset + row_count],
                axis=0,
            )
        )
    grad_conv = jnp.stack(tap_grads, axis=1)
    spill_rows = shifted(back_extended[: tap_count - 1], "rep", -1)
    spill_full = jnp.concatenate(
        [jnp.zeros((row_count - (tap_count - 1), lru_width), jnp.float32), spill_rows], axis=0
    )
    branch_back_low = (back_extended[tap_count - 1 :] + spill_full).astype(jnp.bfloat16)
    grad_branch = matmul_left(mix_normed, branch_back_low)
    grad_gated = matmul_left(mix_normed, gated_back_low)
    back_mix_normed = matmul_right(branch_back_low, branch_full) + matmul_right(
        gated_back_low, gated_full
    )
    mix_norm_pull = jax.vjp(rms_norm, middle, gain_mix)[1]
    back_middle_norm, grad_mix_gain = mix_norm_pull(back_mix_normed)
    back_middle = back_two + back_middle_norm
    rec_grads = (
        grad_mix_gain,
        grad_branch,
        grad_gated,
        grad_conv,
        grad_rate,
        grad_input,
        grad_decay,
        grad_mix_out,
        second_grads[0],
        second_grads[1],
        second_grads[2],
        second_grads[3],
    )
    rec_parts = (
        lax.psum_scatter(rec_grads[0], "shard", scatter_dimension=0, tiled=True),
        lax.psum_scatter(rec_grads[1], "shard", scatter_dimension=0, tiled=True),
        lax.psum_scatter(rec_grads[2], "shard", scatter_dimension=0, tiled=True),
        lax.psum_scatter(rec_grads[3], "shard", scatter_dimension=0, tiled=True),
        lax.psum_scatter(rec_grads[4], "shard", scatter_dimension=0, tiled=True),
        lax.psum_scatter(rec_grads[5], "shard", scatter_dimension=0, tiled=True),
        lax.psum_scatter(rec_grads[6], "shard", scatter_dimension=0, tiled=True),
        lax.psum_scatter(rec_grads[7], "shard", scatter_dimension=0, tiled=True),
        lax.psum_scatter(rec_grads[8], "shard", scatter_dimension=0, tiled=True),
        lax.psum_scatter(rec_grads[9], "shard", scatter_dimension=0, tiled=True),
        lax.psum_scatter(rec_grads[10], "shard", scatter_dimension=0, tiled=True),
        lax.psum_scatter(rec_grads[11], "shard", scatter_dimension=0, tiled=True),
    )
    back_one, first_grads = mlp_backward(
        resid_one,
        gain_first,
        first_gate_full,
        first_up_full,
        first_down_full,
        first_kept,
        back_middle,
    )
    attn_back_low = back_one.astype(jnp.bfloat16)
    grad_attn_out = matmul_left(attended_low, attn_back_low)
    back_attended = (
        matmul_right(attn_back_low, attn_full)
        .astype(jnp.bfloat16)
        .reshape(row_count, head_count, head_size)
    )
    attn_probs = jnp.exp(window_scores(query_heads, key_win, start_row) - log_total)
    probs_again = attn_probs.astype(jnp.bfloat16)
    back_probs = jnp.einsum(
        "thd,kd->htk", back_attended, value_win, preferred_element_type=jnp.float32
    )
    prob_dot = jnp.sum(attn_probs * back_probs, axis=-1, keepdims=True)
    scores_back_low = (attn_probs * (back_probs - prob_dot)).astype(jnp.bfloat16)
    score_scale = 1.0 / math.sqrt(head_size)
    back_query = (
        jnp.einsum("htk,kd->thd", scores_back_low, key_win, preferred_element_type=jnp.float32)
        * score_scale
    )
    back_key_win = (
        jnp.einsum("htk,thd->kd", scores_back_low, query_heads, preferred_element_type=jnp.float32)
        * score_scale
    )
    back_value_win = jnp.einsum(
        "htk,thd->kd", probs_again, back_attended, preferred_element_type=jnp.float32
    )
    seq_zeros = jnp.zeros((WINDOW + row_count * rep_count, head_size), jnp.float32)
    key_spread = lax.dynamic_update_slice_in_dim(seq_zeros, back_key_win, start_row, 0)[WINDOW:]
    value_spread = lax.dynamic_update_slice_in_dim(seq_zeros, back_value_win, start_row, 0)[WINDOW:]
    key_back, value_back = (
        lax.psum_scatter(key_spread, "rep", scatter_dimension=0, tiled=True),
        lax.psum_scatter(value_spread, "rep", scatter_dimension=0, tiled=True),
    )
    query_back_low = back_query.reshape(row_count, head_count * head_size).astype(jnp.bfloat16)
    key_back_low = key_back.astype(jnp.bfloat16)
    value_back_low = value_back.astype(jnp.bfloat16)
    grad_query = matmul_left(attn_normed, query_back_low)
    grad_key = matmul_left(attn_normed, key_back_low)
    grad_value = matmul_left(attn_normed, value_back_low)
    back_attn_normed = (
        matmul_right(query_back_low, query_full)
        + matmul_right(key_back_low, key_full)
        + matmul_right(value_back_low, value_full)
    )
    attn_norm_pull = jax.vjp(rms_norm, inputs, gain_attn)[1]
    back_inputs_norm, grad_attn_gain = attn_norm_pull(back_attn_normed)
    input_grad = (
        (back_one + back_inputs_norm).astype(jnp.bfloat16).reshape(1, row_count, model_width)
    )
    attn_grads = (
        grad_attn_gain,
        grad_query,
        grad_key,
        grad_value,
        grad_attn_out,
        first_grads[0],
        first_grads[1],
        first_grads[2],
        first_grads[3],
    )
    attn_parts = (
        lax.psum_scatter(attn_grads[0], "shard", scatter_dimension=0, tiled=True),
        lax.psum_scatter(attn_grads[1], "shard", scatter_dimension=0, tiled=True),
        lax.psum_scatter(attn_grads[2], "shard", scatter_dimension=0, tiled=True),
        lax.psum_scatter(attn_grads[3], "shard", scatter_dimension=0, tiled=True),
        lax.psum_scatter(attn_grads[4], "shard", scatter_dimension=0, tiled=True),
        lax.psum_scatter(attn_grads[5], "shard", scatter_dimension=0, tiled=True),
        lax.psum_scatter(attn_grads[6], "shard", scatter_dimension=0, tiled=True),
        lax.psum_scatter(attn_grads[7], "shard", scatter_dimension=0, tiled=True),
        lax.psum_scatter(attn_grads[8], "shard", scatter_dimension=0, tiled=True),
    )
    totals = lax.psum(
        (
            attn_parts[0],
            attn_parts[1],
            attn_parts[2],
            attn_parts[3],
            attn_parts[4],
            attn_parts[5],
            attn_parts[6],
            attn_parts[7],
            attn_parts[8],
            rec_parts[0],
            rec_parts[1],
            rec_parts[2],
            rec_parts[3],
            rec_parts[4],
            rec_parts[5],
            rec_parts[6],
            rec_parts[7],
            rec_parts[8],
            rec_parts[9],
            rec_parts[10],
            rec_parts[11],
        ),
        "rep",
    )
    return (
        out_tokens,
        input_grad,
        totals[0],
        totals[1],
        totals[2],
        totals[3],
        totals[4],
        totals[5],
        totals[6],
        totals[7],
        totals[8],
        totals[9],
        totals[10],
        totals[11],
        totals[12],
        totals[13],
        totals[14],
        totals[15],
        totals[16],
        totals[17],
        totals[18],
        totals[19],
        totals[20],
    )


def solution(mesh):
    placed = (
        P("shard", "rep", None),
        P("shard"),
        P("shard", "rep", None),
        P("shard"),
        P("shard", None),
        P("shard", None),
        P("shard", None),
        P("shard", None),
        P("shard"),
        P("shard", None),
        P("shard", None),
        P("shard", None),
        P("shard"),
        P("shard", None),
        P("shard", None),
        P("shard", None),
        P("shard", None),
        P("shard", None),
        P("shard"),
        P("shard", None),
        P("shard"),
        P("shard", None),
        P("shard", None),
        P("shard", None),
    )
    return jax.shard_map(
        on_device,
        mesh=mesh,
        in_specs=placed,
        out_specs=(
            P("shard", "rep", None),
            P("shard", "rep", None),
            P("shard"),
            P("shard", None),
            P("shard", None),
            P("shard", None),
            P("shard", None),
            P("shard"),
            P("shard", None),
            P("shard", None),
            P("shard", None),
            P("shard"),
            P("shard", None),
            P("shard", None),
            P("shard", None),
            P("shard", None),
            P("shard", None),
            P("shard"),
            P("shard", None),
            P("shard"),
            P("shard", None),
            P("shard", None),
            P("shard", None),
        ),
        check_vma=False,
    )
```

profile of v0, /device:TPU:0, one launch (start us, length us, event | category | flops | bytes accessed | tf_op | source)
XLA Modules:
  0.0 4876.0 jit_solution(916881686542531051)
XLA Ops:
  17.2 31.6 all-reduce.91
  135.9 18.1 all_gather.94
  234.1 23.2 all-gather.20.cloned.1.call-done
  270.6 116.0 %all-gather.22.cloned.1.call-done = bf16[1536,4608]{1,0:T(8,128)(2,1)} async-done(((bf16[192,4608]{1,0:T(8,128)(2,1)}), bf16[1536,4608]{1,0:T(8,128)(2,1)}) %all-gather.22.cloned.1.call-update) | async-done | bytes 14155792 | tf_op jit(solution)/shard_map/all_gather | solution.py:174
  402.9 113.2 %all-gather.24.cloned.1.call-done = bf16[4608,1536]{1,0:T(8,128)(2,1)} async-done(((bf16[576,1536]{1,0:T(8,128)(2,1)}), bf16[4608,1536]{1,0:T(8,128)(2,1)}) %all-gather.24.cloned.1.call-update) | async-done | bytes 14155792 | tf_op jit(solution)/shard_map/all_gather | solution.py:175
  530.1 50.5 %all-gather.26.cloned.1.call-done = bf16[1536,2048]{1,0:T(8,128)(2,1)} async-done(((bf16[192,2048]{1,0:T(8,128)(2,1)}), bf16[1536,2048]{1,0:T(8,128)(2,1)}) %all-gather.26.cloned.1.call-update) | async-done | bytes 6291472 | tf_op jit(solution)/shard_map/all_gather | solution.py:224
  591.6 118.9 %all-gather.36.cloned.1.call-done = bf16[4608,1536]{1,0:T(8,128)(2,1)} async-done(((bf16[576,1536]{1,0:T(8,128)(2,1)}), bf16[4608,1536]{1,0:T(8,128)(2,1)}) %all-gather.36.cloned.1.call-update) | async-done | bytes 14155792 | tf_op jit(solution)/shard_map/all_gather | solution.py:234
  710.5 25.2 convolution_convert_fusion.1
  1102.7 16.8 multiply_convert_fusion.2
  1141.4 23.9 fusion.24
  1178.7 19.6 multiply_reduce_fusion.5
  1406.2 17.0 slice.706
  1533.0 32.8 rev.9
  1599.5 32.7 rev.10
  1698.3 20.8 fusion.17
  1732.8 19.3 multiply_reduce_fusion.7
  1765.4 27.8 fusion
  1793.2 31.5 fusion.2
  1863.8 28.7 reduce-scatter.23.cloned.1.call-done
  2051.9 74.1 %reduce-scatter.25.cloned.1.call-done = f32[192,1536]{1,0:T(8,128)} async-done(((f32[1536,1536]{1,0:T(8,128)}), f32[192,1536]{1,0:T(8,128)}) %reduce-scatter.25.cloned.1.call-update) | async-done | bytes 1179664 | tf_op jit(solution)/shard_map/reduce_scatter | solution.py:448
  2126.1 100.2 %reduce-scatter.31.cloned.1.call-done = f32[192,1536]{1,0:T(8,128)} async-done(((f32[1536,1536]{1,0:T(8,128)}), f32[192,1536]{1,0:T(8,128)}) %reduce-scatter.31.cloned.1.call-update) | async-done | bytes 1179664 | tf_op jit(solution)/shard_map/reduce_scatter | solution.py:451
  2226.3 129.7 %reduce-scatter.41.cloned.1.call-done = f32[192,2048]{1,0:T(8,128)} async-done(((f32[1536,2048]{1,0:T(8,128)}), f32[192,2048]{1,0:T(8,128)}) %reduce-scatter.41.cloned.1.call-update) | async-done | bytes 1572880 | tf_op jit(solution)/shard_map/reduce_scatter | solution.py:366
  2356.0 129.9 %reduce-scatter.47.cloned.1.call-done = f32[256,1536]{1,0:T(8,128)} async-done(((f32[2048,1536]{1,0:T(8,128)}), f32[256,1536]{1,0:T(8,128)}) %reduce-scatter.47.cloned.1.call-update) | async-done | bytes 1572880 | tf_op jit(solution)/shard_map/reduce_scatter | solution.py:371
  2486.0 129.9 %reduce-scatter.39.cloned.1.call-done = f32[192,2048]{1,0:T(8,128)} async-done(((f32[1536,2048]{1,0:T(8,128)}), f32[192,2048]{1,0:T(8,128)}) %reduce-scatter.39.cloned.1.call-update) | async-done | bytes 1572880 | tf_op jit(solution)/shard_map/reduce_scatter | solution.py:365
  2615.9 277.5 %reduce-scatter.49.cloned.1.call-done = f32[192,4608]{1,0:T(8,128)} async-done(((f32[1536,4608]{1,0:T(8,128)}), f32[192,4608]{1,0:T(8,128)}) %reduce-scatter.49.cloned.1.call-update) | async-done | bytes 3538960 | tf_op jit(solution)/shard_map/reduce_scatter | solution.py:373
  2893.4 277.4 %reduce-scatter.51.cloned.1.call-done = f32[192,4608]{1,0:T(8,128)} async-done(((f32[1536,4608]{1,0:T(8,128)}), f32[192,4608]{1,0:T(8,128)}) %reduce-scatter.51.cloned.1.call-update) | async-done | bytes 3538960 | tf_op jit(solution)/shard_map/reduce_scatter | solution.py:374
  3170.8 277.5 %reduce-scatter.53.cloned.1.call-done = f32[576,1536]{1,0:T(8,128)} async-done(((f32[4608,1536]{1,0:T(8,128)}), f32[576,1536]{1,0:T(8,128)}) %reduce-scatter.53.cloned.1.call-update) | async-done | bytes 3538960 | tf_op jit(solution)/shard_map/reduce_scatter | solution.py:375
  3448.3 277.4 %reduce-scatter.33.cloned.1.call-done = f32[192,4608]{1,0:T(8,128)} async-done(((f32[1536,4608]{1,0:T(8,128)}), f32[192,4608]{1,0:T(8,128)}) %reduce-scatter.33.cloned.1.call-update) | async-done | bytes 3538960 | tf_op jit(solution)/shard_map/reduce_scatter | solution.py:453
  3725.7 277.4 %reduce-scatter.35.cloned.1.call-done = f32[192,4608]{1,0:T(8,128)} async-done(((f32[1536,4608]{1,0:T(8,128)}), f32[192,4608]{1,0:T(8,128)}) %reduce-scatter.35.cloned.1.call-update) | async-done | bytes 3538960 | tf_op jit(solution)/shard_map/reduce_scatter | solution.py:454
  4003.1 277.5 %reduce-scatter.37.cloned.1.call-done = f32[576,1536]{1,0:T(8,128)} async-done(((f32[4608,1536]{1,0:T(8,128)}), f32[576,1536]{1,0:T(8,128)}) %reduce-scatter.37.cloned.1.call-update) | async-done | bytes 3538960 | tf_op jit(solution)/shard_map/reduce_scatter | solution.py:455
  4323.1 27.2 all-reduce.88
  4368.0 472.1 %all-reduce.94.cloned.1.call-done = (f32[192,1536]{1,0:T(8,128)}, f32[192,128]{1,0:T(8,128)}, f32[192,128]{1,0:T(8,128)}, f32[192,1536]{1,0:T(8,128)}, f32[192,4...) async-done(((f32[192,1536]{1,0:T(8,128)}, ...) | async-done | bytes 28770320 | tf_op jit(solution)/shard_map/psum | solution.py:457
  (914 shorter events, 1362.4 us)
Async XLA Ops:
  7.2 163.3 %all-gather.16.cloned.1.call-start = ((), (), s32[]{:S(2)}) async-start(), calls=%async_computation.18 | async-start | bytes 5308416 | tf_op jit(solution)/shard_map/all_gather | solution.py:168
  7.9 218.7 %all-gather.18.cloned.1.call-start = ((), (), s32[]{:S(2)}) async-start(), calls=%async_computation.19 | async-start | bytes 5308416 | tf_op jit(solution)/shard_map/all_gather | solution.py:171
  8.7 248.6 %all-gather.20.cloned.1.call-start = ((), (), s32[]{:S(2)}) async-start(), calls=%async_computation.20 | async-start | bytes 15925248 | tf_op jit(solution)/shard_map/all_gather | solution.py:173
  9.4 377.3 %all-gather.22.cloned.1.call-start = ((), (), s32[]{:S(2)}) async-start(), calls=%async_computation.21 | async-start | bytes 15925248 | tf_op jit(solution)/shard_map/all_gather | solution.py:174
  10.0 506.1 %all-gather.24.cloned.1.call-start = ((), (), s32[]{:S(2)}) async-start(), calls=%async_computation.22 | async-start | bytes 15925248 | tf_op jit(solution)/shard_map/all_gather | solution.py:175
  10.6 569.9 %all-gather.26.cloned.1.call-start = ((), (), s32[]{:S(2)}) async-start(), calls=%async_computation.23 | async-start | bytes 7077888 | tf_op jit(solution)/shard_map/all_gather | solution.py:224
  11.2 699.3 %all-gather.36.cloned.1.call-start = ((), (), s32[]{:S(2)}) async-start(), calls=%async_computation.28 | async-start | bytes 15925248 | tf_op jit(solution)/shard_map/all_gather | solution.py:234
  12.0 1090.1 %all-gather.28.cloned.1.call-start = ((), (), s32[]{:S(2)}) async-start(), calls=%async_computation.24 | async-start | bytes 7077888 | tf_op jit(solution)/shard_map/all_gather | solution.py:225
  12.7 1106.8 %all-gather.30.cloned.1.call-start = ((), (), s32[]{:S(2)}) async-start(), calls=%async_computation.25 | async-start | bytes 7077888 | tf_op jit(solution)/shard_map/all_gather | solution.py:230
  13.5 1114.6 %all-gather.34.cloned.1.call-start = ((), (), s32[]{:S(2)}) async-start(), calls=%async_computation.27 | async-start | bytes 15925248 | tf_op jit(solution)/shard_map/all_gather | solution.py:233
  14.0 1127.4 %all-gather.32.cloned.1.call-start = ((), (), s32[]{:S(2)}) async-start(), calls=%async_computation.26 | async-start | bytes 15925248 | tf_op jit(solution)/shard_map/all_gather | solution.py:232
  14.8 1846.3 %reduce-scatter.21.cloned.1.call-start = ((), (), s32[]{:S(2)}) async-start(), calls=%async_computation.29 | async-start | bytes 1310720 | tf_op jit(solution)/shard_map/reduce_scatter | solution.py:416
  588.1 147.6 %collective-permute-start = (f32[3,2048]{1,0:T(4,128)S(1)}, f32[3,2048]{1,0:T(4,128)S(1)}, u32[]{:S(2)}, u32[]{:S(2)}) collective-permute-start(f32[3,2048]{1,0:T(4,128)S(1)} %slice.803), channel_id=1, source_target_pairs={{0,8},{8,16},{16,24},{1,9},{9,17},{17,25},{2,10},{10,18},{18,26},{... | collective-permute-start | bytes 73736 | tf_op jit(solution)/shard_map/ppermute | solution.py:17
  1684.5 5.8 collective-permute-start.1
  1834.9 57.6 %reduce-scatter.23.cloned.1.call-start = ((), (), s32[]{:S(2)}) async-start(), calls=%async_computation.30 | async-start | bytes 1310720 | tf_op jit(solution)/shard_map/reduce_scatter | solution.py:417
  1851.0 200.8 %reduce-scatter.43.cloned.1.call-start = ((), (), s32[]{:S(2)}) async-start(), calls=%async_computation.40 | async-start | bytes 1179648 | tf_op jit(solution)/shard_map/reduce_scatter | solution.py:368
  1855.0 196.8 %reduce-scatter.45.cloned.1.call-start = ((), (), s32[]{:S(2)}) async-start(), calls=%async_computation.41 | async-start | bytes 1179648 | tf_op jit(solution)/shard_map/reduce_scatter | solution.py:369
  1859.1 192.8 %reduce-scatter.27.cloned.1.call-start = ((), (), s32[]{:S(2)}) async-start(), calls=%async_computation.32 | async-start | bytes 884736 | tf_op jit(solution)/shard_map/reduce_scatter | solution.py:449
  1863.5 188.4 %reduce-scatter.29.cloned.1.call-start = ((), (), s32[]{:S(2)}) async-start(), calls=%async_computation.33 | async-start | bytes 884736 | tf_op jit(solution)/shard_map/reduce_scatter | solution.py:450
  1895.0 231.0 %reduce-scatter.25.cloned.1.call-start = ((), (), s32[]{:S(2)}) async-start(), calls=%async_computation.31 | async-start | bytes 10616832 | tf_op jit(solution)/shard_map/reduce_scatter | solution.py:448
  1911.4 314.9 %reduce-scatter.31.cloned.1.call-start = ((), (), s32[]{:S(2)}) async-start(), calls=%async_computation.34 | async-start | bytes 10616832 | tf_op jit(solution)/shard_map/reduce_scatter | solution.py:451
  1919.8 436.2 %reduce-scatter.41.cloned.1.call-start = ((), (), s32[]{:S(2)}) async-start(), calls=%async_computation.39 | async-start | bytes 14155776 | tf_op jit(solution)/shard_map/reduce_scatter | solution.py:366
  1929.2 556.7 %reduce-scatter.47.cloned.1.call-start = ((), (), s32[]{:S(2)}) async-start(), calls=%async_computation.42 | async-start | bytes 14155776 | tf_op jit(solution)/shard_map/reduce_scatter | solution.py:371
  1939.4 676.5 %reduce-scatter.39.cloned.1.call-start = ((), (), s32[]{:S(2)}) async-start(), calls=%async_computation.38 | async-start | bytes 14155776 | tf_op jit(solution)/shard_map/reduce_scatter | solution.py:365
  1949.5 943.9 %reduce-scatter.49.cloned.1.call-start = ((), (), s32[]{:S(2)}) async-start(), calls=%async_computation.43 | async-start | bytes 31850496 | tf_op jit(solution)/shard_map/reduce_scatter | solution.py:373
  1965.7 1205.0 %reduce-scatter.51.cloned.1.call-start = ((), (), s32[]{:S(2)}) async-start(), calls=%async_computation.44 | async-start | bytes 31850496 | tf_op jit(solution)/shard_map/reduce_scatter | solution.py:374
  1982.4 1465.9 %reduce-scatter.53.cloned.1.call-start = ((), (), s32[]{:S(2)}) async-start(), calls=%async_computation.45 | async-start | bytes 31850496 | tf_op jit(solution)/shard_map/reduce_scatter | solution.py:375
  1999.0 1726.7 %reduce-scatter.33.cloned.1.call-start = ((), (), s32[]{:S(2)}) async-start(), calls=%async_computation.35 | async-start | bytes 31850496 | tf_op jit(solution)/shard_map/reduce_scatter | solution.py:453
  2015.3 1987.8 %reduce-scatter.35.cloned.1.call-start = ((), (), s32[]{:S(2)}) async-start(), calls=%async_computation.36 | async-start | bytes 31850496 | tf_op jit(solution)/shard_map/reduce_scatter | solution.py:454
  2032.1 2248.5 %reduce-scatter.37.cloned.1.call-start = ((), (), s32[]{:S(2)}) async-start(), calls=%async_computation.37 | async-start | bytes 31850496 | tf_op jit(solution)/shard_map/reduce_scatter | solution.py:455
  2049.4 2264.5 %reduce-scatter.55.cloned.1.call-start = ((), (), s32[]{:S(2)}) async-start(), calls=%async_computation.46 | async-start | bytes 1179648
  2051.6 2788.5 %all-reduce.94.cloned.1.call-start = ((), (), s32[]{:S(2)}) async-start(), calls=%async_computation.47 | async-start | bytes 57540608 | tf_op jit(solution)/shard_map/psum | solution.py:457
  (196 other events, 4706.2 us)
Sparse Core Ops, SparseCore 0:
  9.7 57.9 all-gather.15
  69.3 53.6 all-gather.17
  124.6 132.6 all-gather.19
  258.8 127.8 all-gather.21
  388.2 127.8 all-gather.23
  517.5 62.9 all-gather.25
  582.2 128.2 all-gather.35
  712.1 62.9 all-gather.27
  776.8 63.3 all-gather.29
  841.7 128.2 all-gather.33
  971.7 127.8 all-gather.31
  1835.1 25.9 reduce-scatter.20
  1864.8 27.7 reduce-scatter.22
  1895.2 32.1 reduce-scatter.42
  1930.1 30.7 reduce-scatter.44
  1963.5 30.0 reduce-scatter.26
  1996.5 29.7 reduce-scatter.28
  2028.5 97.5 reduce-scatter.24
  2128.4 97.8 reduce-scatter.30
  2228.4 127.5 reduce-scatter.40
  2358.3 127.5 reduce-scatter.46
  2488.3 127.5 reduce-scatter.38
  2618.2 275.1 reduce-scatter.48
  2895.6 275.1 reduce-scatter.50
  3173.1 275.1 reduce-scatter.52
  3450.5 275.1 reduce-scatter.32
  3727.9 275.1 reduce-scatter.34
  4005.4 275.1 reduce-scatter.36
  4283.4 30.4 reduce-scatter.54
  4320.2 519.7 all-reduce.93
where the time goes:
time: 4900 us; the launch traced here: 4880 us
  waiting for transfers between devices  3170 us (65%)
  local copies, waits for them, and re-layouts  712 us (15%)
  matrix products  532 us (11%)
  other arithmetic  224 us (5%)
  blocking collectives  207 us (4%)
    psum x1, waiting for transfers between devices, on_device(): lax.psum((attn_parts[0], attn_parts[1], attn_parts[2], attn_parts[3], att...  472 us
    slice x125, local copies, waits for them, and re-layouts, linear_scan(): return lax.associative_scan(compose, (lru_coef, lru_drive), axis=0)  380 us
    reduce_scatter x1, waiting for transfers between devices, on_device(): lax.psum_scatter(rec_grads[9], 'shard', scatter_dimension=0, tiled=True)  278 us
    reduce_scatter x1, waiting for transfers between devices, on_device(): lax.psum_scatter(rec_grads[11], 'shard', scatter_dimension=0, tiled=True)  278 us
    reduce_scatter x1, waiting for transfers between devices, on_device(): lax.psum_scatter(attn_grads[8], 'shard', scatter_dimension=0, tiled=True)  278 us
    reduce_scatter x1, waiting for transfers between devices, on_device(): lax.psum_scatter(attn_grads[6], 'shard', scatter_dimension=0, tiled=True)  277 us
    reduce_scatter x1, waiting for transfers between devices, on_device(): lax.psum_scatter(rec_grads[10], 'shard', scatter_dimension=0, tiled=True)  277 us
    reduce_scatter x1, waiting for transfers between devices, on_device(): lax.psum_scatter(attn_grads[7], 'shard', scatter_dimension=0, tiled=True)  277 us
  transfers between devices with their start and end apart: 32, of which 21 were waited for; matrix products, arithmetic and copies ran while one was open for 15% of the time, Pallas kernels for 0%

commit v1 on v0

v1 whole, which is shorter than its diff:
```python
import functools
import math

import jax
import jax.numpy as jnp
from jax import lax
from jax.experimental import pallas as pl
from jax.experimental.pallas import tpu as pltpu
from jax.sharding import PartitionSpec as P

WINDOW = 1024
LAG = 1
EPSILON = 1e-06
F32 = jnp.float32
BF16 = jnp.bfloat16


def rms_norm(values, norm_gain):
    return (
        values * lax.rsqrt(jnp.mean(values * values, axis=-1, keepdims=True) + EPSILON) * norm_gain
    )


def gelu_tanh(values):
    return jax.nn.gelu(values, approximate=True)


def mlp_middle(gate_pre, up_pre):
    return gelu_tanh(gate_pre) * up_pre


def lru_gates(rate_pre, input_pre, decay_w, conv_out):
    log_coef = -8.0 * jax.nn.sigmoid(rate_pre) * decay_w
    lru_coef = jnp.exp(log_coef)
    lru_drive = jnp.sqrt(-jnp.expm1(2.0 * log_coef)) * jax.nn.sigmoid(input_pre) * conv_out
    return (lru_coef, lru_drive)


def matmul(first_op, second_op):
    return jnp.dot(first_op, second_op, preferred_element_type=F32)


def matmul_left(first_op, second_op):
    return lax.dot_general(
        first_op, second_op, (((0,), (0,)), ((), ())), preferred_element_type=F32
    )


def matmul_right(first_op, second_op):
    return lax.dot_general(
        first_op, second_op, (((1,), (1,)), ((), ())), preferred_element_type=F32
    )


def rounded(values):
    return values.astype(BF16).astype(F32)


def my_chip():
    return lax.axis_index("shard") // 2


def my_core():
    return lax.rem(lax.axis_index("shard"), 2)


def swap_cores(x):
    count = lax.axis_size("shard")
    return lax.ppermute(x, "shard", [(i, i ^ 1) for i in range(count)])


def shift_rep(x, by):
    size = lax.axis_size("rep")
    return lax.ppermute(x, "rep", [(i, i + by) for i in range(size) if 0 <= i + by < size])


def shift_chip(x, by):
    count = lax.axis_size("shard")
    return lax.ppermute(x, "shard", [(i, (i + 2 * by) % count) for i in range(count)])


def by_core(first, second):
    return jnp.where(my_core() == 0, first, second)


def unit_pieces(columns, unit, parts):
    sub = unit // parts
    chips = columns // unit // 2
    return sub, tuple(
        [(2 * chip + core) * unit + part * sub for part in range(parts) for chip in range(chips)]
        for core in (0, 1)
    )


def column_halves(w, unit, parts=1):
    sub, places = unit_pieces(w.shape[1], unit, parts)
    return tuple(
        jnp.concatenate([w[:, at : at + sub] for at in places[core]], axis=1) for core in (0, 1)
    )


def joined_columns(first, second, unit, parts=1):
    sub, places = unit_pieces(2 * first.shape[1], unit, parts)
    pieces = {}
    for half, starts in zip((first, second), places):
        for i, at in enumerate(starts):
            pieces[at] = half[:, i * sub : (i + 1) * sub]
    return jnp.concatenate([pieces[at] for at in sorted(pieces)], axis=1)


def chip_rows(halves):
    own = by_core(halves[0], halves[1])
    other = swap_cores(by_core(halves[1], halves[0]))
    return jnp.concatenate([by_core(own, other), by_core(other, own)], axis=0)


def rep_masks(flip):
    size = lax.axis_size("rep")
    masks = [1 << i for i in range(size.bit_length() - 1)]
    return masks[::-1] if flip else masks


def swap_rep(x, mask):
    size = lax.axis_size("rep")
    return lax.ppermute(x, "rep", [(i, i ^ mask) for i in range(size)])


MESH_ID = pl.DeviceIdType.MESH


def across(place, mask):
    return place + mask - 2 * mask * lax.rem(place // mask, 2)


def highest(at):
    return 1 << (at.bit_length() - 1)


def lowest(at):
    return at & -at


def gather_kernel(chunks, arrays, chips, reps, *refs):
    ins, outs = refs[:arrays], refs[arrays : 2 * arrays]
    along_send, along_recv, rep_send, rep_recv, local_sem = refs[2 * arrays :]
    shard = lax.axis_index("shard")
    chip, core = shard // 2, lax.rem(shard, 2)
    place = lax.axis_index("rep")
    bits = [1 << i for i in range(reps.bit_length() - 1)]
    everyone = range(1, reps)

    def device_at(chip_at):
        return {"shard": 2 * chip_at + core}

    barrier = pltpu.get_barrier_semaphore()
    for by in (1, chips - 1):
        pl.semaphore_signal(
            barrier,
            inc=1,
            device_id=device_at(lax.rem(chip + by, chips)),
            device_id_type=MESH_ID,
        )
    for bit in bits:
        pl.semaphore_signal(
            barrier, inc=1, device_id={"rep": across(place, bit)}, device_id_type=MESH_ID
        )
    pl.semaphore_wait(barrier, 2 + len(bits))

    def block(c, rep_at, chip_at, half=None):
        array, first, columns, sub, split = chunks[c]
        row = (rep_at * chips + chip_at) * sub if split else chip_at * sub
        if half is not None:
            columns = columns // 2
            first = first + half * columns
        return outs[array].at[pl.ds(pl.multiple_of(row, 16), sub), pl.ds(first, columns)]

    def own(c):
        array, first, columns, sub, split = chunks[c]
        row = pl.multiple_of(place * sub, 16) if split else 0
        return ins[array].at[pl.ds(row, sub), pl.ds(first, columns)]

    def along(c, origin, to, direction):
        here = block(c, place, origin)
        return here, pltpu.make_async_remote_copy(
            src_ref=here,
            dst_ref=here,
            send_sem=along_send.at[c, origin, direction],
            recv_sem=along_recv.at[c, origin],
            device_id=device_at(to),
            device_id_type=MESH_ID,
        )

    def first_along(c, to, direction):
        return pltpu.make_async_remote_copy(
            src_ref=own(c),
            dst_ref=block(c, place, chip),
            send_sem=along_send.at[c, chip, direction],
            recv_sem=along_recv.at[c, chip],
            device_id=device_at(to),
            device_id_type=MESH_ID,
        )

    def hop(c, chip_at, at, half):
        bit = at if half is None else (highest(at) if half == 0 else lowest(at))
        here = block(c, across_all(place, at ^ bit), chip_at, half)
        slot = 2 * at + (half or 0)
        return pltpu.make_async_remote_copy(
            src_ref=here,
            dst_ref=here,
            send_sem=rep_send.at[c, chip_at, slot],
            recv_sem=rep_recv.at[c, chip_at, slot],
            device_id={"rep": across(place, bit)},
            device_id_type=MESH_ID,
        )

    def arrival(c, chip_at, at, half):
        here = block(c, across_all(place, at), chip_at, half)
        slot = 2 * at + (half or 0)
        return pltpu.make_async_remote_copy(
            src_ref=here,
            dst_ref=here,
            send_sem=rep_send.at[c, chip_at, slot],
            recv_sem=rep_recv.at[c, chip_at, slot],
            device_id={"rep": place},
            device_id_type=MESH_ID,
        )

    def across_all(at, offset):
        for bit in bits:
            if offset & bit:
                at = across(at, bit)
        return at

    def halves(at):
        return (None,) if at == lowest(at) else (0, 1)

    def local_copies(c):
        array, first, columns, sub, split = chunks[c]
        copies = []
        for part in range(reps if split else 1):
            copies.append(
                pltpu.make_async_copy(
                    ins[array].at[pl.ds(part * sub, sub), pl.ds(first, columns)],
                    block(c, part, chip),
                    local_sem.at[c, part],
                )
            )
        return copies

    def others(run):
        def one(by, carry):
            run(lax.rem(chip + by, chips))
            return carry

        lax.fori_loop(1, chips, one, 0)

    def begin(c):
        @pl.when(chip < chips - 1)
        def _():
            first_along(c, chip + 1, 0).start()

        @pl.when(chip > 0)
        def _():
            first_along(c, chip - 1, 1).start()

        for copy in local_copies(c):
            copy.start()

    def spread(c, origin):
        if chunks[c][4]:
            for bit in bits:
                hop(c, origin, bit, None).start()

    def arrived(c, by):
        @pl.when(chip - by >= 0)
        def _():
            along(c, chip - by, chip, 0)[1].wait_recv()

            @pl.when(chip < chips - 1)
            def _():
                along(c, chip - by, chip + 1, 0)[1].start()

            spread(c, chip - by)

        @pl.when(chip + by < chips)
        def _():
            along(c, chip + by, chip, 1)[1].wait_recv()

            @pl.when(chip > 0)
            def _():
                along(c, chip + by, chip - 1, 1)[1].start()

            spread(c, chip + by)

    def passed(c, level):
        if not chunks[c][4]:
            return

        def run(origin):
            for at in everyone:
                if at.bit_count() == level:
                    for half in halves(at):
                        arrival(c, origin, at, half).wait_recv()
            for at in everyone:
                if at.bit_count() == level + 1:
                    for half in halves(at):
                        hop(c, origin, at, half).start()

        others(run)

    def end(c):
        @pl.when(chip < chips - 1)
        def _():
            first_along(c, chip + 1, 0).wait_send()

        @pl.when(chip > 0)
        def _():
            first_along(c, chip - 1, 1).wait_send()

        for copy in local_copies(c):
            copy.wait()
        for by in range(1, chips):

            @pl.when((chip - by >= 0) & (chip < chips - 1))
            def _(by=by):
                along(c, chip - by, chip + 1, 0)[1].wait_send()

            @pl.when((chip + by < chips) & (chip > 0))
            def _(by=by):
                along(c, chip + by, chip - 1, 1)[1].wait_send()

        if chunks[c][4]:

            def run(origin):
                for at in everyone:
                    for half in halves(at):
                        hop(c, origin, at, half).wait_send()

            others(run)

    stages = (
        [begin]
        + [functools.partial(arrived, by=by) for by in range(1, chips)]
        + [functools.partial(passed, level=level) for level in range(1, len(bits) + 1)]
        + [end]
    )
    for tick in range(len(chunks) + (len(stages) - 1) * LAG):
        for at, stage in enumerate(stages):
            if 0 <= tick - at * LAG < len(chunks):
                stage(tick - at * LAG)


def gather_all(arrays, splits, widths):
    reps, chips = lax.axis_size("rep"), lax.axis_size("shard") // 2
    if any(split and array.shape[0] // reps % 16 for array, split in zip(arrays, splits)):
        results = []
        for array, split in zip(arrays, splits):
            if split:
                part = array.shape[0] // reps
                array = lax.dynamic_slice_in_dim(array, lax.axis_index("rep") * part, part, 0)
            array = lax.all_gather(
                array,
                "shard",
                axis=0,
                tiled=True,
                axis_index_groups=[list(range(core, 2 * chips, 2)) for core in (0, 1)],
            )
            results.append(lax.all_gather(array, "rep", axis=0, tiled=True) if split else array)
        return results
    chunks = []
    for i, (array, split, wide) in enumerate(zip(arrays, splits, widths)):
        sub = array.shape[0] // reps if split else array.shape[0]
        for first in range(0, array.shape[1], wide):
            chunks.append((i, first, min(wide, array.shape[1] - first), sub, split))
    slots = 2 * reps
    count = len(chunks)
    return pl.pallas_call(
        functools.partial(gather_kernel, chunks, len(arrays), chips, reps),
        in_specs=[pl.BlockSpec(memory_space=pltpu.VMEM)] * len(arrays),
        out_specs=[pl.BlockSpec(memory_space=pl.ANY)] * len(arrays),
        out_shape=[
            jax.ShapeDtypeStruct((a.shape[0] * chips, a.shape[1]), a.dtype) for a in arrays
        ],
        scratch_shapes=[
            pltpu.SemaphoreType.DMA((count, chips, 2)),
            pltpu.SemaphoreType.DMA((count, chips)),
            pltpu.SemaphoreType.DMA((count, chips, slots)),
            pltpu.SemaphoreType.DMA((count, chips, slots)),
            pltpu.SemaphoreType.DMA((count, reps)),
        ],
        compiler_params=pltpu.CompilerParams(
            collective_id=0, has_side_effects=True, vmem_limit_bytes=40 * 1024 * 1024
        ),
    )(*arrays)


def sum_chips(parts):
    chips = lax.axis_size("shard") // 2
    chip = my_chip()
    sub = parts[0].shape[0] // chips

    def rows_of(by):
        at = lax.rem(chip + by, chips) * sub
        return jnp.concatenate(
            [lax.dynamic_slice_in_dim(part, at, sub, 0) for part in parts], axis=1
        )

    total = rows_of(0).astype(F32)
    for by in range(1, chips):
        total = total + shift_chip(rows_of(by), by).astype(F32)
    return total.astype(BF16)


def sum_rep(x):
    middle = x.shape[1] // 2
    halves = [x[:, :middle], x[:, middle:]]
    for flip in (0, 1):
        for mask in rep_masks(flip):
            here = halves[flip]
            halves[flip] = (here.astype(F32) + swap_rep(here, mask).astype(F32)).astype(BF16)
    return jnp.concatenate(halves, axis=1)


def reduce_kernel(chunks, counts, chips, *refs):
    n_left, n_right, n_given, n_out = counts
    n = len(chunks)
    refs = list(refs)

    def take(count):
        taken = refs[:count]
        del refs[:count]
        return taken

    lefts, rights, givens = take(n_left), take(n_right), take(n_given)
    outs, first_in, second_in, chip_in = take(n_out), take(n), take(n), take(n)
    right_buf, big_left, first_out, first_loc, second_out, second_loc = take(6)
    chip_out, chip_loc, own_out = take(3)
    send, recv, chip_send, chip_recv, hop_send, hop_recv, local = take(7)
    shard = lax.axis_index("shard")
    chip, core = shard // 2, lax.rem(shard, 2)
    place = lax.axis_index("rep")
    bits = (1, 2)

    def device_at(chip_at):
        return {"shard": 2 * chip_at + core}

    barrier = pltpu.get_barrier_semaphore()
    for by in range(1, chips):
        pl.semaphore_signal(
            barrier,
            inc=1,
            device_id=device_at(lax.rem(chip + by, chips)),
            device_id_type=MESH_ID,
        )
    for bit in bits:
        pl.semaphore_signal(
            barrier, inc=1, device_id={"rep": across(place, bit)}, device_id_type=MESH_ID
        )
    pl.semaphore_wait(barrier, chips - 1 + len(bits))

    def rep_at(offset):
        at = place
        for bit in bits:
            if offset & bit:
                at = across(at, bit)
        return at

    def masks(c):
        return bits[::-1] if chunks[c]["flip"] else bits

    def rows_of(c):
        return chips * chunks[c]["sub"]

    def right_copy(c):
        k = chunks[c]
        return pltpu.make_async_copy(
            rights[k["right"]].at[:, pl.ds(k["first"], k["wide"])],
            right_buf.at[c % 6, :, pl.ds(0, k["wide"])],
            local.at[c, 0],
        )

    def left_copy(c):
        return pltpu.make_async_copy(lefts[chunks[c]["left"]], big_left, local.at[c, 1])

    def exchange(c, turn):
        k, rows = chunks[c], rows_of(c)
        source, target = ((first_out, first_in), (second_out, second_in))[turn]
        return pltpu.make_async_remote_copy(
            src_ref=source.at[c % 3, :, pl.ds(0, rows), pl.ds(0, k["wide"])],
            dst_ref=target[c],
            send_sem=send.at[c, turn],
            recv_sem=recv.at[c, turn],
            device_id={"rep": across(place, masks(c)[turn])},
            device_id_type=MESH_ID,
        )

    def arrived_copy(c, turn):
        k, rows = chunks[c], rows_of(c)
        source = (first_in, second_in)[turn][c]
        target = (first_loc.at[c % 4], second_loc.at[c % 2])[turn]
        return pltpu.make_async_copy(
            source, target.at[:, pl.ds(0, rows), pl.ds(0, k["wide"])], local.at[c, 2 + turn]
        )

    def tiles(c, run):
        wide = chunks[c]["wide"]
        tile = 256 if wide % 256 == 0 else 128

        def one(i, carry):
            run(pl.ds(pl.multiple_of(i * tile, tile), tile))
            return carry

        lax.fori_loop(0, wide // tile, one, 0)

    def product(c, offset, target, arrivals):
        k, rows = chunks[c], rows_of(c)
        at = rep_at(offset)

        def run(columns):
            if k["given"] is not None:
                total = givens[k["given"]][at, :, columns].astype(F32)
            else:
                left = big_left if k["big"] else lefts[k["left"]]
                total = jnp.dot(
                    left[at], right_buf[c % 6, :, columns], preferred_element_type=F32
                )
            for ref, index in arrivals:
                total = total + ref[index + (pl.ds(0, rows), columns)].astype(F32)
            target[0][target[1] + (pl.ds(0, rows), columns)] = total.astype(BF16)

        tiles(c, run)

    def load(c):
        if chunks[c]["given"] is None:
            right_copy(c).start()
            if chunks[c]["load"]:
                left_copy(c).start()

    def send_first(c):
        if chunks[c]["given"] is None:
            right_copy(c).wait()
            if chunks[c]["load"]:
                left_copy(c).wait()
        one, two = masks(c)
        product(c, one, (first_out, (c % 3, 0)), [])
        product(c, one ^ two, (first_out, (c % 3, 1)), [])
        exchange(c, 0).start()

    def take_first(c):
        exchange(c, 0).wait_recv()
        arrived_copy(c, 0).start()

    def send_second(c):
        arrived_copy(c, 0).wait()
        product(c, masks(c)[1], (second_out, (c % 3, 0)), [(first_loc, (c % 4, 1))])
        exchange(c, 1).start()
        exchange(c, 0).wait_send()

    def take_second(c):
        exchange(c, 1).wait_recv()
        arrived_copy(c, 1).start()

    def to_chip(c, by):
        k = chunks[c]
        at = lax.rem(chip + by, chips)
        row = pl.multiple_of(at * k["sub"], 16)
        return pltpu.make_async_remote_copy(
            src_ref=chip_out.at[c % 3, pl.ds(row, k["sub"]), pl.ds(0, k["wide"])],
            dst_ref=chip_in[c].at[by - 1],
            send_sem=chip_send.at[c, by - 1],
            recv_sem=chip_recv.at[c, by - 1],
            device_id=device_at(at),
            device_id_type=MESH_ID,
        )

    def send_chips(c):
        arrived_copy(c, 1).wait()
        product(
            c, 0, (chip_out, (c % 3,)), [(first_loc, (c % 4, 0)), (second_loc, (c % 2, 0))]
        )
        for by in range(1, chips):
            to_chip(c, by).start()
        exchange(c, 1).wait_send()

    def chips_copy(c):
        k = chunks[c]
        return pltpu.make_async_copy(
            chip_in[c],
            chip_loc.at[c % 2, :, pl.ds(0, k["sub"]), pl.ds(0, k["wide"])],
            local.at[c, 4],
        )

    def take_chips(c):
        for by in range(1, chips):
            to_chip(c, by).wait_recv()
        chips_copy(c).start()

    def out_rows(c, offset, half=None):
        k = chunks[c]
        first, wide = k["place"], k["wide"]
        if half is not None:
            wide = wide // 2
            first = first + half * wide
        row = pl.multiple_of(rep_at(offset) * k["sub"], 16)
        return outs[k["out"]].at[pl.ds(row, k["sub"]), pl.ds(first, wide)]

    def own_rows_of(c):
        k = chunks[c]
        return own_out.at[c % 3, pl.ds(0, k["sub"]), pl.ds(0, k["wide"])]

    def own_copy(c):
        return pltpu.make_async_copy(own_rows_of(c), out_rows(c, 0), local.at[c, 5])

    def hop(c, at, half):
        bit = at if at in bits else (2 if half != 1 else 1)
        here = out_rows(c, at ^ bit, half)
        slot = 2 * at + (half or 0)
        return pltpu.make_async_remote_copy(
            src_ref=own_rows_of(c) if at in bits else here,
            dst_ref=here,
            send_sem=hop_send.at[c, slot],
            recv_sem=hop_recv.at[c, slot],
            device_id={"rep": across(place, bit)},
            device_id_type=MESH_ID,
        )

    def arrival(c, at, half):
        here = out_rows(c, at, half)
        slot = 2 * at + (half or 0)
        return pltpu.make_async_remote_copy(
            src_ref=here,
            dst_ref=here,
            send_sem=hop_send.at[c, slot],
            recv_sem=hop_recv.at[c, slot],
            device_id={"rep": across(place, 1)},
            device_id_type=MESH_ID,
        )

    def far_halves(c):
        return (0, 1) if chunks[c]["wide"] % 256 == 0 else (None,)

    def send_sums(c):
        k = chunks[c]
        chips_copy(c).wait()
        row = pl.multiple_of(chip * k["sub"], 16)

        def run(columns):
            total = chip_out[c % 3, pl.ds(row, k["sub"]), columns].astype(F32)
            for by in range(1, chips):
                total = total + chip_loc[c % 2, by - 1, pl.ds(0, k["sub"]), columns].astype(F32)
            own_out[c % 3, pl.ds(0, k["sub"]), columns] = total.astype(BF16)

        tiles(c, run)
        for bit in bits:
            hop(c, bit, None).start()
        own_copy(c).start()
        for by in range(1, chips):
            to_chip(c, by).wait_send()

    def pass_sums(c):
        for bit in bits:
            arrival(c, bit, None).wait_recv()
        for half in far_halves(c):
            hop(c, 3, half).start()

    def end(c):
        own_copy(c).wait()
        for bit in bits:
            hop(c, bit, None).wait_send()
        for half in far_halves(c):
            arrival(c, 3, half).wait_recv()
            hop(c, 3, half).wait_send()

    stages = [
        load,
        send_first,
        take_first,
        send_second,
        take_second,
        send_chips,
        take_chips,
        send_sums,
        pass_sums,
        end,
    ]
    for tick in range(n + len(stages) - 1):
        for at, stage in enumerate(stages):
            if 0 <= tick - at < n:
                stage(tick - at)


def reduce_all(products):
    reps, chips = lax.axis_size("rep"), lax.axis_size("shard") // 2
    depth = max(left.shape[0] for left, _, _ in products if left is not None)
    if reps != 4 or any(
        (given[0].shape[1] if left is None else left.shape[1] // reps) // chips % 16
        for left, given, _ in products
    ):
        results = []
        for left, given, _ in products:
            if left is None:
                whole = given[0].reshape(-1, given[0].shape[2])
            else:
                whole = jnp.concatenate(
                    [matmul_left(left, right).astype(BF16) for right in given], axis=1
                )
            part = lax.psum_scatter(whole, "rep", scatter_dimension=0, tiled=True)
            count = lax.axis_size("shard")
            part = lax.psum_scatter(
                part,
                "shard",
                scatter_dimension=0,
                tiled=True,
                axis_index_groups=[list(range(core, count, 2)) for core in (0, 1)],
            )
            results.append(lax.all_gather(part, "rep", axis=0, tiled=True))
        return results
    lefts, rights, givens, chunks, outs = [], [], [], [], []
    subs = [
        (given[0].shape[1] if left is None else left.shape[1] // reps) // chips
        for left, given, _ in products
    ]
    small = min(subs)
    for (left, parts, wide), sub in zip(products, subs):
        total = sum(part.shape[-1] for part in parts)
        outs.append(jax.ShapeDtypeStruct((reps * sub, total), BF16))
        first_right = len(rights)
        if left is not None:
            lefts.append(left.T.reshape(reps, chips * sub, depth))
            rights.extend(parts)
        else:
            givens.extend(parts)
        before = 0
        mine = []
        for i, part in enumerate(parts):
            row = []
            for first in range(0, part.shape[-1], wide):
                row.append(
                    dict(
                        left=len(lefts) - 1,
                        given=len(givens) - 1 if left is None else None,
                        right=first_right + i,
                        first=first,
                        wide=min(wide, part.shape[-1] - first),
                        sub=sub,
                        out=len(outs) - 1,
                        place=before + first,
                        big=sub > small,
                        load=False,
                    )
                )
            mine.append(row)
            before += part.shape[-1]
        mine = [chunk for group in zip(*mine) for chunk in group]
        mine[0]["load"] = sub > small
        chunks += mine
    for i, chunk in enumerate(chunks):
        chunk["flip"] = i % 2
    n = len(chunks)
    rows = max(subs) * chips
    wide = max(chunk["wide"] for chunk in chunks)
    hbm = pl.BlockSpec(memory_space=pl.ANY)
    vmem = pl.BlockSpec(memory_space=pltpu.VMEM)
    big = {chunk["left"] for chunk in chunks if chunk["big"]}

    def landing(blocks, sub_only=False):
        return [
            jax.ShapeDtypeStruct(
                (blocks, c["sub"] if sub_only else chips * c["sub"], c["wide"]), BF16
            )
            for c in chunks
        ]

    shapes = outs + landing(2) + landing(1) + landing(chips - 1, True)
    results = pl.pallas_call(
        functools.partial(
            reduce_kernel, chunks, (len(lefts), len(rights), len(givens), len(outs)), chips
        ),
        in_specs=[hbm if i in big else vmem for i in range(len(lefts))]
        + [hbm] * len(rights)
        + [vmem] * len(givens),
        out_specs=[hbm] * len(shapes),
        out_shape=shapes,
        scratch_shapes=[
            pltpu.VMEM((6, depth, wide), BF16),
            pltpu.VMEM((reps, rows, depth), BF16),
            pltpu.VMEM((3, 2, rows, wide), BF16),
            pltpu.VMEM((4, 2, rows, wide), BF16),
            pltpu.VMEM((3, 1, rows, wide), BF16),
            pltpu.VMEM((2, 1, rows, wide), BF16),
            pltpu.VMEM((3, rows, wide), BF16),
            pltpu.VMEM((2, chips - 1, max(subs), wide), BF16),
            pltpu.VMEM((3, max(subs), wide), BF16),
            pltpu.SemaphoreType.DMA((n, 2)),
            pltpu.SemaphoreType.DMA((n, 2)),
            pltpu.SemaphoreType.DMA((n, chips - 1)),
            pltpu.SemaphoreType.DMA((n, chips - 1)),
            pltpu.SemaphoreType.DMA((n, 8)),
            pltpu.SemaphoreType.DMA((n, 8)),
            pltpu.SemaphoreType.DMA((n, 6)),
        ],
        compiler_params=pltpu.CompilerParams(
            collective_id=1, has_side_effects=True, vmem_limit_bytes=62 * 1024 * 1024
        ),
    )(*lefts, *rights, *givens)
    return results[: len(outs)]


def reduce_chips(grads):
    return sum_rep(sum_chips(grads))


def own_rows(rows):
    part = rows.shape[0] // 2
    first, second = rows[:part], rows[part:]
    keep = by_core(first, second)
    got = swap_cores(by_core(second, first))
    return by_core(keep, got), by_core(got, keep)


def scan_kernel(reverse, coef_ref, drive_ref, cum_ref, out_ref):
    rows, lanes = coef_ref.shape[1], coef_ref.shape[2]
    groups = rows // 8
    place = lax.broadcasted_iota(jnp.int32, (8, lanes), 0)

    def step(turn, carry):
        carry_cum, carry_out = carry
        group = groups - 1 - turn if reverse else turn
        where = pl.ds(pl.multiple_of(group * 8, 8), 8)
        a = coef_ref[0, where, :]
        b = drive_ref[0, where, :]
        for k in (1, 2, 4):
            by = 8 - k if reverse else k
            inside = place < 8 - k if reverse else place >= k
            a_before = jnp.where(inside, pltpu.roll(a, by, 0), 1.0)
            b_before = jnp.where(inside, pltpu.roll(b, by, 0), 0.0)
            b = a * b_before + b
            a = a * a_before
        out = b + a * carry_out
        cum = a * carry_cum
        out_ref[0, where, :] = out
        cum_ref[0, where, :] = cum
        last = 0 if reverse else 7
        return (
            jnp.broadcast_to(cum[last : last + 1], (8, lanes)),
            jnp.broadcast_to(out[last : last + 1], (8, lanes)),
        )

    lax.fori_loop(
        0, groups, step, (jnp.ones((8, lanes), F32), jnp.zeros((8, lanes), F32))
    )


def linear_scan(coef, drive, reverse):
    batch, rows, width = coef.shape
    lanes = min(512, width)
    spec = pl.BlockSpec((1, rows, lanes), lambda b, i: (b, 0, i))
    shape = jax.ShapeDtypeStruct(coef.shape, F32)
    return pl.pallas_call(
        functools.partial(scan_kernel, reverse),
        grid=(batch, width // lanes),
        in_specs=[spec, spec],
        out_specs=[spec, spec],
        out_shape=[shape, shape],
        compiler_params=pltpu.CompilerParams(vmem_limit_bytes=48 * 1024 * 1024),
    )(coef, drive)


def carried_in(prod, part, reverse):
    size = lax.axis_size("rep")
    pair = jnp.stack([prod, part])
    total = jnp.zeros_like(part)
    through = jnp.ones_like(prod)
    place = lax.axis_index("rep")
    ahead = size - 1 - place if reverse else place
    for distance in range(1, size):
        got = shift_rep(pair, -distance if reverse else distance)
        total = total + through * got[1]
        through = jnp.where(ahead >= distance, through * got[0], through)
    return total


def window_scores(query_heads, key_win, start_row, behind):
    row_count = query_heads.shape[0]
    score_scale = 1.0 / math.sqrt(query_heads.shape[2])
    raw_scores = (
        jnp.einsum("thd,kd->htk", query_heads, key_win, preferred_element_type=F32) * score_scale
    )
    row_pos = start_row + jnp.arange(row_count, dtype=jnp.int32)[:, None]
    col_pos = start_row - behind + jnp.arange(key_win.shape[0], dtype=jnp.int32)[None, :]
    allowed = (col_pos <= row_pos) & (col_pos > row_pos - WINDOW) & (col_pos >= 0)
    return jnp.where(allowed[None], raw_scores, -1e30)


def with_sibling(x):
    return jnp.concatenate([x, swap_cores(x)], axis=0)


def sum_parts(parts):
    rows = parts.shape[0] // 2
    return parts[:rows] + swap_cores(parts[rows:])


def mlp_forward(resid, norm_gain, in_w, down_w):
    normed = with_sibling(rms_norm(resid, norm_gain).astype(BF16))
    middle = in_w.shape[1] // 2
    both = matmul(normed, in_w)
    gate_pre, up_pre = both[:, :middle], both[:, middle:]
    hidden = mlp_middle(gate_pre, up_pre).astype(BF16)
    return resid + sum_parts(matmul(hidden, down_w)), (normed, gate_pre, up_pre, hidden)


def mlp_backward(resid, norm_gain, in_w, down_w, kept_vals, back_out):
    normed, gate_pre, up_pre, hidden = kept_vals
    out_low = with_sibling(back_out.astype(BF16))
    back_hidden = rounded(matmul_right(out_low, down_w))
    back_gate, back_up = jax.vjp(mlp_middle, gate_pre, up_pre)[1](back_hidden)
    gate_low = back_gate.astype(BF16)
    up_low = back_up.astype(BF16)
    back_normed = sum_parts(matmul_right(jnp.concatenate([gate_low, up_low], axis=1), in_w))
    back_resid, grad_gain = jax.vjp(rms_norm, resid, norm_gain)[1](back_normed)
    return (back_out + back_resid, (grad_gain, (normed, gate_low), (normed, up_low), (hidden, out_low)))


def on_device(
    tokens_in,
    lengths,
    cotangent,
    attn_norm,
    query_proj,
    key_proj,
    value_proj,
    attn_out,
    first_norm,
    first_gate,
    first_up,
    first_down,
    mixer_norm,
    branch_proj,
    gated_proj,
    conv_taps,
    rate_gate,
    input_gate,
    decay_rate,
    mixer_out,
    second_norm,
    second_gate,
    second_up,
    second_down,
):
    row_count = tokens_in.shape[1]
    width = tokens_in.shape[2]
    shards = lax.axis_size("shard")
    reps = lax.axis_size("rep")
    chips = shards // 2
    core = my_core()
    start_row = lax.axis_index("rep") * row_count
    positions = start_row + jnp.arange(row_count, dtype=jnp.int32)
    valid_mask = (positions < lengths[0]).astype(F32)[:, None]

    piece = width // chips // reps
    spot = lax.broadcasted_iota(jnp.int32, (width, width), 1)
    natural = (
        lax.rem(spot // piece, chips) * (piece * reps)
        + (spot // (piece * chips)) * piece
        + lax.rem(spot, piece)
    )
    to_order = (lax.broadcasted_iota(jnp.int32, (width, width), 0) == natural).astype(BF16)

    def ordered(x):
        return matmul(x, to_order)

    def unordered(x):
        return matmul_right(x, to_order)

    head_size = key_proj.shape[1]
    half = query_proj.shape[1] // 2
    gain_columns = jnp.stack([attn_norm, first_norm, mixer_norm, second_norm], axis=1)
    gain_columns = jnp.pad(gain_columns, ((0, 0), (0, 128 - 4)))
    qkv_halves = (
        jnp.concatenate([query_proj[:, :half], key_proj, gain_columns], axis=1),
        jnp.concatenate([query_proj[:, half:], value_proj, gain_columns], axis=1),
    )
    out_ordered = ordered(attn_out).astype(BF16)
    out_halves = out_ordered[:, : width // 2], out_ordered[:, width // 2 :]
    qkv_width = half + head_size
    ff_unit = first_down.shape[0]
    lru_unit = mixer_out.shape[0]

    def both_halves(first, second, unit, parts):
        pairs = zip(column_halves(first, unit, parts), column_halves(second, unit, parts))
        return tuple(jnp.concatenate(pair, axis=1) for pair in pairs)

    block_width = rate_gate.shape[1]
    tap_count = conv_taps.shape[1]
    spare = block_width - tap_count - 1
    attn_wide, first_in_w, first_down_w, lru_in_w, mix_wide, second_in_w, second_down_w = gather_all(
        (
            chip_rows(tuple(jnp.concatenate(both, axis=1) for both in zip(qkv_halves, out_halves))),
            chip_rows(both_halves(first_gate, first_up, ff_unit, reps)),
            ordered(first_down).astype(BF16),
            chip_rows(both_halves(branch_proj, gated_proj, lru_unit, 1)),
            jnp.concatenate(
                [
                    rate_gate,
                    input_gate,
                    conv_taps,
                    decay_rate[:, None],
                    jnp.zeros((lru_unit, spare), BF16),
                    ordered(mixer_out).astype(BF16),
                ],
                axis=1,
            ),
            chip_rows(both_halves(second_gate, second_up, ff_unit, reps)),
            ordered(second_down).astype(BF16),
        ),
        (True, True, True, True, False, True, True),
        (1792, 1536, 1536, 1024, 1920, 1536, 1536),
    )
    qkv_own = attn_wide[:, :qkv_width]
    gains = attn_wide[:, qkv_width : qkv_width + 128].astype(F32)
    gain_attn, gain_first, gain_mix, gain_second = (gains[:, i] for i in range(4))
    attn_own = attn_wide[:, qkv_width + 128 :]
    qkv_sib = swap_cores(qkv_own)
    attn_sib = swap_cores(attn_own)

    small_w = mix_wide[:, : 3 * block_width]
    mix_w = mix_wide[:, 3 * block_width :]

    inputs = ordered(tokens_in.reshape(row_count, width))
    attn_normed = rms_norm(inputs, gain_attn).astype(BF16)
    qkv_mine = matmul(attn_normed, qkv_own).astype(BF16)
    qkv_other = matmul(attn_normed, qkv_sib).astype(BF16)
    qkv_first, qkv_second = by_core(qkv_mine, qkv_other), by_core(qkv_other, qkv_mine)
    query_rows = jnp.concatenate([qkv_first[:, :half], qkv_second[:, :half]], axis=1)
    kv_rows = jnp.concatenate([qkv_first[:, half:], qkv_second[:, half:]], axis=1)
    blocks_behind = -(-WINDOW // row_count)
    behind = blocks_behind * row_count
    kv_win = jnp.concatenate(
        [shift_rep(kv_rows, by) for by in range(blocks_behind, 0, -1) if by < reps]
        + [kv_rows],
        axis=0,
    )
    behind = kv_win.shape[0] - row_count
    key_win, value_win = kv_win[:, :head_size], kv_win[:, head_size:]
    head_count = query_rows.shape[1] // head_size
    query_heads = query_rows.reshape(row_count, head_count, head_size)
    scores = window_scores(query_heads, key_win, start_row, behind)
    row_peak = jnp.max(scores, axis=-1, keepdims=True)
    exp_scores = jnp.exp(scores - row_peak)
    exp_total = jnp.sum(exp_scores, axis=-1, keepdims=True)
    log_total = row_peak + jnp.log(exp_total)
    probs_low = (exp_scores / exp_total).astype(BF16)
    attended = jnp.einsum("htk,kd->thd", probs_low, value_win, preferred_element_type=F32)
    attended_low = ordered(attended.reshape(row_count, width).astype(BF16)).astype(BF16)
    out_mine = matmul(attended_low, attn_own)
    out_other = matmul(attended_low, attn_sib)
    resid_one = inputs + jnp.concatenate(
        [by_core(out_mine, out_other), by_core(out_other, out_mine)], axis=1
    )

    middle, first_kept = mlp_forward(resid_one, gain_first, first_in_w, first_down_w)

    rate_blocks = small_w[:, :block_width].reshape(-1, block_width, block_width)
    input_blocks = small_w[:, block_width : 2 * block_width].reshape(-1, block_width, block_width)
    conv_w = small_w[:, 2 * block_width : 2 * block_width + tap_count].astype(F32)
    decay_w = small_w[:, 2 * block_width + tap_count].astype(F32)
    mix_normed = with_sibling(rms_norm(middle, gain_mix).astype(BF16))
    lru_width = lru_in_w.shape[1] // 2
    block_count = lru_width // block_width
    branch_gated = matmul(mix_normed, lru_in_w).reshape(2, row_count, 2 * lru_width)
    branch, gated_pre = branch_gated[:, :, :lru_width], branch_gated[:, :, lru_width:]
    tail_rows = shift_rep(branch[:, row_count - (tap_count - 1) :], 1)
    extended = jnp.concatenate([tail_rows, branch], axis=1)

    def earlier(offset):
        return extended[:, tap_count - 1 - offset : tap_count - 1 - offset + row_count]

    conv_out = sum(conv_w[:, offset] * earlier(offset) for offset in range(tap_count))
    conv_low = conv_out.astype(BF16).reshape(2 * row_count, block_count, block_width)

    def through_blocks(values, blocks, how):
        return jnp.einsum(how, values, blocks, preferred_element_type=F32)

    rate_pre = through_blocks(conv_low, rate_blocks, "tbi,bij->tbj").reshape(branch.shape)
    input_pre = through_blocks(conv_low, input_blocks, "tbi,bij->tbj").reshape(branch.shape)
    lru_coef, lru_drive = lru_gates(rate_pre, input_pre, decay_w, conv_out)
    cum_coef, local_state = linear_scan(lru_coef, lru_drive, False)
    start_state = carried_in(cum_coef[:, -1], local_state[:, -1], False)
    lru_state = local_state + cum_coef * start_state[:, None]
    gated_act = gelu_tanh(gated_pre)
    mix_low = (lru_state * gated_act).astype(BF16).reshape(2 * row_count, lru_width)
    resid_two = middle + sum_parts(matmul(mix_low, mix_w))

    final_rows, second_kept = mlp_forward(
        resid_two, gain_second, second_in_w, second_down_w
    )
    out_tokens = unordered(final_rows.astype(BF16)).astype(BF16).reshape(1, row_count, width)
    back_final = ordered(cotangent.reshape(row_count, width)) * valid_mask
    back_two, second_grads = mlp_backward(
        resid_two,
        gain_second,
        second_in_w,
        second_down_w,
        second_kept,
        back_final,
    )

    mix_back_low = with_sibling(back_two.astype(BF16))
    grad_mix_out = matmul_left(mix_low, mix_back_low).astype(BF16)
    back_mixed = rounded(matmul_right(mix_back_low, mix_w)).reshape(branch.shape)
    back_state = back_mixed * gated_act
    gelu_pull = jax.vjp(gelu_tanh, gated_pre)[1]
    gated_back_low = (
        gelu_pull(back_mixed * lru_state)[0].astype(BF16).reshape(2 * row_count, lru_width)
    )
    coef_next = jnp.concatenate([lru_coef[:, 1:], jnp.ones_like(lru_coef[:, :1])], axis=1)
    later_prod, local_adjoint = linear_scan(coef_next, back_state, True)
    carry_in = carried_in(cum_coef[:, -1], lru_coef[:, 0] * local_adjoint[:, 0], True)
    adjoint = local_adjoint + later_prod * carry_in[:, None]
    prev_state = jnp.concatenate([start_state[:, None], lru_state[:, :-1]], axis=1)
    gates_pull = jax.vjp(lru_gates, rate_pre, input_pre, decay_w, conv_out)[1]
    back_rate, back_input, grad_decay, back_conv_direct = gates_pull(
        (adjoint * prev_state, adjoint)
    )
    rate_back_low = back_rate.astype(BF16).reshape(conv_low.shape)
    input_back_low = back_input.astype(BF16).reshape(conv_low.shape)
    grad_rate = through_blocks(conv_low, rate_back_low, "tbi,tbj->bij")
    grad_input = through_blocks(conv_low, input_back_low, "tbi,tbj->bij")
    gate_back_conv = through_blocks(rate_back_low, rate_blocks, "tbj,bij->tbi") + through_blocks(
        input_back_low, input_blocks, "tbj,bij->tbi"
    )
    back_conv = back_conv_direct + gate_back_conv.reshape(branch.shape)
    grad_taps = jnp.stack(
        [jnp.sum(back_conv * earlier(offset), axis=(0, 1)) for offset in range(tap_count)], axis=1
    )
    next_rows = shift_rep(back_conv[:, : tap_count - 1], -1)
    back_extended = jnp.concatenate([back_conv, next_rows], axis=1)
    branch_back_low = (
        sum(
            conv_w[:, offset] * back_extended[:, offset : offset + row_count]
            for offset in range(tap_count)
        )
        .astype(BF16)
        .reshape(2 * row_count, lru_width)
    )
    back_mix_normed = sum_parts(
        matmul_right(jnp.concatenate([branch_back_low, gated_back_low], axis=1), lru_in_w)
    )
    back_middle_norm, grad_mix_gain = jax.vjp(rms_norm, middle, gain_mix)[1](back_mix_normed)
    back_middle = back_two + back_middle_norm
    grad_small = jnp.concatenate(
        [
            grad_rate.reshape(lru_width, block_width).astype(BF16),
            grad_input.reshape(lru_width, block_width).astype(BF16),
            grad_taps.astype(BF16),
            grad_decay[:, None].astype(BF16),
            jnp.zeros((lru_width, spare), BF16),
        ],
        axis=1,
    )

    back_one, first_grads = mlp_backward(
        resid_one, gain_first, first_in_w, first_down_w, first_kept, back_middle
    )

    attn_back_low = back_one.astype(BF16)
    back_halves = attn_back_low[:, : width // 2], attn_back_low[:, width // 2 :]
    back_mine, back_other = by_core(*back_halves), by_core(back_halves[1], back_halves[0])
    attended_both = with_sibling(attended_low)
    out_right = jnp.concatenate([back_mine, swap_cores(back_other)], axis=0)
    back_attended = matmul_right(back_mine, attn_own) + matmul_right(back_other, attn_sib)
    back_attended = (
        unordered(back_attended.astype(BF16))
        .astype(BF16)
        .reshape(row_count, head_count, head_size)
    )
    attn_probs = jnp.exp(window_scores(query_heads, key_win, start_row, behind) - log_total)
    probs_again = attn_probs.astype(BF16)
    back_probs = jnp.einsum("thd,kd->htk", back_attended, value_win, preferred_element_type=F32)
    prob_dot = jnp.sum(attn_probs * back_probs, axis=-1, keepdims=True)
    scores_back_low = (attn_probs * (back_probs - prob_dot)).astype(BF16)
    score_scale = 1.0 / math.sqrt(head_size)
    back_query = (
        jnp.einsum("htk,kd->thd", scores_back_low, key_win, preferred_element_type=F32)
        * score_scale
    )
    back_key_win = (
        jnp.einsum("htk,thd->kd", scores_back_low, query_heads, preferred_element_type=F32)
        * score_scale
    )
    back_value_win = jnp.einsum(
        "htk,thd->kd", probs_again, back_attended, preferred_element_type=F32
    )
    back_kv_win = jnp.concatenate([back_key_win, back_value_win], axis=1)
    back_kv = back_kv_win[behind:]
    for by in range(1, behind // row_count + 1):
        begin = behind - by * row_count
        back_kv = back_kv + shift_rep(back_kv_win[begin : begin + row_count], -by)
    back_kv = back_kv.astype(BF16)
    back_query = back_query.reshape(row_count, width).astype(BF16)
    back_first = jnp.concatenate([back_query[:, :half], back_kv[:, :head_size]], axis=1)
    back_second = jnp.concatenate([back_query[:, half:], back_kv[:, head_size:]], axis=1)
    qkv_back_mine = by_core(back_first, back_second)
    qkv_back_other = by_core(back_second, back_first)
    back_attn_normed = matmul_right(qkv_back_mine, qkv_own) + matmul_right(qkv_back_other, qkv_sib)
    back_inputs_norm, grad_attn_gain = jax.vjp(rms_norm, inputs, gain_attn)[1](back_attn_normed)
    input_grad = (
        unordered((back_one + back_inputs_norm).astype(BF16))
        .astype(BF16)
        .reshape(1, row_count, width)
    )

    mix_reduced = reduce_chips([grad_small, grad_mix_out])
    grad_mixer_out = unordered(mix_reduced[:, 3 * block_width :])
    small = mix_reduced[:, : 3 * block_width].astype(F32)

    gain_given = jnp.stack([grad_attn_gain, first_grads[0], grad_mix_gain, second_grads[0]])
    gain_given = jnp.pad(gain_given, ((0, 124), (0, 0))).astype(BF16).T.reshape(reps, -1, 128)
    qkv_right = jnp.concatenate([qkv_back_mine, swap_cores(qkv_back_other)], axis=0)
    second_in, second_down_rows, lru_in, first_in, first_down_rows, qkv_rows, out_rows, gain_rows = (
        reduce_all(
            [
                (second_grads[1][0], [second_grads[1][1], second_grads[2][1]], 768),
                (second_grads[3][0], [second_grads[3][1]], 512),
                (mix_normed, [branch_back_low, gated_back_low], 512),
                (first_grads[1][0], [first_grads[1][1], first_grads[2][1]], 768),
                (first_grads[3][0], [first_grads[3][1]], 512),
                (with_sibling(attn_normed), [qkv_right], 512),
                (with_sibling(attended_low), [out_right], 768),
                (None, [gain_given], 128),
            ]
        )
    )

    def in_reduced(reduced, unit, parts):
        rows = own_rows(reduced)
        middle = rows[0].shape[1] // 2
        return tuple(
            joined_columns(*(half[:, columns] for half in rows), unit, parts).astype(F32)
            for columns in (slice(0, middle), slice(middle, None))
        )

    grad_second_gate, grad_second_up = in_reduced(second_in, ff_unit, reps)
    grad_second_down = unordered(second_down_rows)
    grad_branch_proj, grad_gated_proj = in_reduced(lru_in, lru_unit, 1)
    grad_first_gate, grad_first_up = in_reduced(first_in, ff_unit, reps)
    grad_first_down = unordered(first_down_rows)
    qkv_first, qkv_second = own_rows(qkv_rows)
    grad_query = jnp.concatenate([qkv_first[:, :half], qkv_second[:, :half]], axis=1).astype(F32)
    grad_key = qkv_first[:, half:].astype(F32)
    grad_value = qkv_second[:, half:].astype(F32)
    grad_out_proj = unordered(jnp.concatenate(own_rows(out_rows), axis=1))
    gain_first_, gain_second_ = own_rows(gain_rows)
    gain_grads = (gain_first_.astype(F32) + gain_second_.astype(F32)).T
    return (
        out_tokens,
        input_grad,
        gain_grads[0],
        grad_query,
        grad_key,
        grad_value,
        grad_out_proj,
        gain_grads[1],
        grad_first_gate,
        grad_first_up,
        grad_first_down,
        gain_grads[2],
        grad_branch_proj,
        grad_gated_proj,
        small[:, 2 * block_width : 2 * block_width + tap_count],
        small[:, :block_width],
        small[:, block_width : 2 * block_width],
        small[:, 2 * block_width + tap_count],
        grad_mixer_out,
        gain_grads[3],
        grad_second_gate,
        grad_second_up,
        grad_second_down,
    )


def solution(mesh):
    rows = P("shard", None)
    vector = P("shard")
    tokens = P("shard", "rep", None)
    weights = (
        vector,
        rows,
        rows,
        rows,
        rows,
        vector,
        rows,
        rows,
        rows,
        vector,
        rows,
        rows,
        rows,
        rows,
        rows,
        vector,
        rows,
        vector,
        rows,
        rows,
        rows,
    )
    return jax.shard_map(
        on_device,
        mesh=mesh,
        in_specs=(tokens, vector, tokens) + weights,
        out_specs=(tokens, tokens) + weights,
        check_vma=False,
    )
```

time: 4900 us -> 1960 us (0.40)
  waiting for transfers between devices: 3170 us -> 91.6 us
  Pallas kernels: 0 us -> 1000 us
  local copies, waits for them, and re-layouts: 712 us -> 227 us
  blocking collectives: 207 us -> 0 us
  matrix products: 532 us -> 362 us
    reduce_scatter x17 -> x0, waiting for transfers between devices: 2260 us -> none  [the longest x1 278 us: on_device(): lax.psum_scatter(rec_grads[9], 'shard', scatter_dimension=0, tiled=True)]
    pallas_call x0 -> x4, Pallas kernels: none -> 1000 us  [the longest x1 624 us: reduce_all(): pl.pallas_call(functools.partial(reduce_kernel, chunks, (len(lefts), len(...]
    psum x1 -> x0, waiting for transfers between devices: 472 us -> none  [on_device(): lax.psum((attn_parts[0], attn_parts[1], attn_parts[2], attn_parts[3], att...]
    all_gather x11 -> x0, waiting for transfers between devices: 422 us -> none  [the longest x1 119 us: on_device(): lax.all_gather(second_down, 'shard', axis=0, tiled=True)]
    slice x131 -> x47, local copies, waits for them, and re-layouts: 385 us -> 52.9 us  [the longest x8 16.3 us: column_halves(): w[:, at:at + sub]]
    pad x64 -> x0, local copies, waits for them, and re-layouts: 163 us -> none  [linear_scan(): return lax.associative_scan(compose, (lru_coef, lru_drive), axis=0)]
    all_gather x11 -> x0, blocking collectives: 137 us -> none  [the longest x3 23.4 us: carried_in(): gathered = jax.tree.map(lambda a: lax.all_gather(a, axis), part)]
    dot_general x13 -> x1, matrix products: 135 us -> 5.98 us  [matmul_left(): lax.dot_general(first_op, second_op, (((0,), (0,)), ((), ())), preferred_...]
  transfers between devices with their start and end apart: 32 -> 47, of which waited for: 21 -> 14; matrix products, arithmetic and copies ran while one was open for 15% -> 23% of each run, Pallas kernels for 0% -> 1%
where the time goes in v1:
time: 1960 us
  Pallas kernels  1000 us (51%)
  matrix products  362 us (18%)
  local copies, waits for them, and re-layouts  227 us (12%)
  other arithmetic  224 us (11%)
  waiting for transfers between devices  91.6 us (5%)
  starting transfers between devices  42.9 us (2%)
    pallas_call x1, Pallas kernels, reduce_all(): pl.pallas_call(functools.partial(reduce_kernel, chunks, (len(lefts), len(...  624 us
    pallas_call x1, Pallas kernels, gather_all(): pl.pallas_call(functools.partial(gather_kernel, chunks, len(arrays), chip...  359 us
    dot_general x16, matrix products, matmul_right(): lax.dot_general(first_op, second_op, (((1,), (1,)), ((), ())), preferred_...  149 us
    dot_general x17, matrix products, matmul(): return jnp.dot(first_op, second_op, preferred_element_type=F32)  105 us
    ppermute x3, waiting for transfers between devices, shift_chip(): lax.ppermute(x, 'shard', [(i, (i + 2 * by) % count) for i in range(count)])  41.3 us
  transfers between devices with their start and end apart: 47, of which 14 were waited for; matrix products, arithmetic and copies ran while one was open for 23% of the time, Pallas kernels for 1%

profile of v1, /device:TPU:0, one launch (start us, length us, event | category | flops | bytes accessed | tf_op | source)
XLA Modules:
  0.0 1956.0 jit_solution(3407464719688238447)
XLA Ops:
  83.8 358.7 %shard_map.407 = (bf16[1536,1792]{1,0:T(8,128)(2,1)}, bf16[1536,4608]{1,0:T(8,128)(2,1)}, bf16[2304,1536]{1,0:T(8,128)(2,1)}, bf16[1536,2048]{1,0:T(8,128)(2,1)}...) custom-call(bf16[384,1792]{1,0:T(8,128)(2,1)S(1)} %pad_maximum_fusion.21.refs_0_, ...), custom_call_target="tpu_custom_call" | custom-call | tf_op jit(solution)/shard_map/pallas_call | solution.py:377
  468.0 15.4 fusion.216
  483.4 14.7 fusion.3
  498.1 15.1 fusion.108
  527.4 17.8 fusion.97
  545.2 14.1 fusion.218
  601.9 7.3 copy.208
  620.5 7.2 copy.209
  627.8 10.9 fusion.130
  638.7 8.9 shard_map.408
  666.9 7.3 multiply_convert_fusion.2
  692.8 17.8 fusion.93
  711.7 22.7 %fusion.24 = (bf16[1024,2304]{1,0:T(8,128)(2,1)}, bf16[1024,2304]{1,0:T(8,128)(2,1)}, bf16[1024,2304]{1,0:T(8,128)(2,1)}) fusion(f32[1024,4608]{1,0:T(8,128)} %fusion.93, bf16[2304,1536]{1,0:T(8,128)(2,1)} %get-tuple-element.50, bf16[512,1536]{1,0:T(8,128)(2,1)} %copy-done.84, bf16[512,1536]{1,0:T(8,128)(2,1)S(1)} %get-tuple-element.521), kind=kOutput, calls=%fused_computation.41 | convolution fusion | flops 7320109056 | bytes 43253760 | tf_op jit(solution)/shard_map/dot_general | solution.py:50
  734.4 19.3 fusion.30
  797.0 9.9 shard_map.409
  818.2 10.4 multiply_reduce_fusion
  848.6 7.2 copy.210
  855.8 13.3 multiply_reduce_fusion.1
  870.6 10.6 fusion.283
  952.3 9.9 fusion.219
  964.7 41.3 %collective-permute-done.40 = bf16[256,1920]{1,0:T(8,128)(2,1)} collective-permute-done((bf16[256,1920]{1,0:T(8,128)(2,1)}, bf16[256,1920]{1,0:T(8,128)(2,1)}, u32[]{:S(2)}, u32[]{:S(2)}) %collective-permute-start.40) | collective-permute-done | bytes 983072 | tf_op jit(solution)/shard_map/ppermute | solution.py:79
  1012.2 21.6 %fusion.17 = (bf16[1024,2304]{1,0:T(8,128)(2,1)}, bf16[1024,2304]{1,0:T(8,128)(2,1)}) fusion(f32[1024,4608]{1,0:T(8,128)} %fusion.97, bf16[2304,1536]{1,0:T(8,128)(2,1)} %get-tuple-element.44, bf16[512,1536]{1,0:T(8,128)(2,1)} %collective-permute-done.26, bf16[512,1536]{1,0:T(8,128)(2,1)S(1)} %get-tuple-element.160), kind=kOutput, calls=%fused_computation.34 | convolution fusion | flops 7315390464 | bytes 38535168 | tf_op jit(solution)/shard_map/dot_general | solution.py:50
  1033.8 18.9 fusion.34
  1085.1 7.4 fusion.84
  1098.3 7.3 collective-permute-done.45
  1129.6 8.5 convolution_convert_fusion.6
  1140.0 28.2 %fusion = (f32[12,512]{1,0:T(8,128)S(1)}, f32[1536,512,12]{1,0,2:T(8,128)}) fusion(f32[12,512,1536]{1,2,0:T(8,128)} %get-tuple-element.520, f32[12,512]{1,0:T(8,128)S(1)} %copy-done.85, bf16[512,12,128]{0,2,1:T(8,128)(2,1)S(1)} %bitcast.249, bf16[1536,256]{1,0:T(8,128)(2,1)S(1)} %copy-done.57), kind=kOutput, calls=%fused_computation.2 | convolution fusion | flops 2444224512 | bytes 77520896 | tf_op jit(solution)/shard_map/thd,kd->htk/dot_general | solution.py:1180
  1168.1 14.4 fusion.87
  1182.5 31.5 %fusion.2 = bf16[12,512,1536]{1,2,0:T(8,128)(2,1)} fusion(f32[1536,512,12]{1,0,2:T(8,128)} %get-tuple-element.524, f32[12,512,1536]{1,2,0:T(8,128)} %get-tuple-element.520, f32[12,512]{1,0:T(8,128)S(1)} %get-tuple-element.523, f32[12,512]{1,0:T(8,128)S(1)} %copy-done.85), kind=kLoop, calls=%fused_computation.4 | loop fusion | flops 37748736 | bytes 94420992 | tf_op jit(solution)/shard_map/convert_element_type | solution.py:1182
  1214.0 9.1 fusion.90
  1250.7 8.5 fusion.85
  1264.1 623.9 %shard_map.410 = (bf16[384,4608]{1,0:T(8,128)(2,1)}, bf16[576,1536]{1,0:T(8,128)(2,1)}, bf16[384,2048]{1,0:T(8,128)(2,1)}, bf16[384,4608]{1,0:T(8,128)(2,1)}, bf...) custom-call(bf16[4,384,1024]{2,1,0:T(8,128)(2,1)} %bitcast.261, ...), custom_call_target="tpu_custom_call" | custom-call | tf_op jit(solution)/shard_map/pallas_call | solution.py:775
  (744 shorter events, 529.5 us)
Async XLA Ops:
  21.0 56.4 %collective-permute-start.3 = (bf16[192,4608]{1,0:T(8,128)(2,1)}, bf16[192,4608]{1,0:T(8,128)(2,1)}, u32[]{:S(2)}, u32[]{:S(2)}) collective-permute-start(bf16[192,4608]{1,0:T(8,128)(2,1)} %broadcast_select_fusion.10), channel_id=1, source_target_pairs={{0,1},{1,0},{2,3},{3,2},{4,5},{5,4},{6,7},{7,6},{8,9},{9,8},{10,11... | collective-permute-start | bytes 5308424 | tf_op jit(solution)/shard_map/ppermute | solution.py:69
  43.5 35.9 %collective-permute-start.1 = (bf16[192,4608]{1,0:T(8,128)(2,1)}, bf16[192,4608]{1,0:T(8,128)(2,1)}, u32[]{:S(2)}, u32[]{:S(2)}) collective-permute-start(bf16[192,4608]{1,0:T(8,128)(2,1)} %broadcast_select_fusion.14), channel_id=1, source_target_pairs={{0,1},{1,0},{2,3},{3,2},{4,5},{5,4},{6,7},{7,6},{8,9},{9,8},{10,11... | collective-permute-start | bytes 5308424 | tf_op jit(solution)/shard_map/ppermute | solution.py:69
  45.7 30.0 %collective-permute-start.2 = (bf16[192,2048]{1,0:T(8,128)(2,1)}, bf16[192,2048]{1,0:T(8,128)(2,1)}, u32[]{:S(2)}, u32[]{:S(2)}) collective-permute-start(bf16[192,2048]{1,0:T(8,128)(2,1)} %broadcast_select_fusion.26), channel_id=1, source_target_pairs={{0,1},{1,0},{2,3},{3,2},{4,5},{5,4},{6,7},{7,6},{8,9},{9,8},{10,11... | collective-permute-start | bytes 2359304 | tf_op jit(solution)/shard_map/ppermute | solution.py:69
  54.2 19.5 collective-permute-start
  447.6 72.1 %collective-permute-start.7 = (bf16[1536,768]{1,0:T(8,128)(2,1)}, bf16[1536,768]{1,0:T(8,128)(2,1)}, u32[]{:S(2)}, u32[]{:S(2)}) collective-permute-start(bf16[1536,768]{1,0:T(8,128)(2,1)} %slice.1506), channel_id=1, source_target_pairs={{0,1},{1,0},{2,3},{3,2},{4,5},{5,4},{6,7},{7,6},{8,9},{9,8},{10,11... | collective-permute-start | bytes 7077896 | tf_op jit(solution)/shard_map/ppermute | solution.py:69
  453.8 14.1 collective-permute-start.5
  456.3 11.6 collective-permute-start.6
  654.6 10.8 collective-permute-start.12
  692.6 18.0 collective-permute-start.18
  755.1 15.0 collective-permute-start.30
  766.5 17.8 collective-permute-start.20
  778.3 122.7 %collective-permute-start.31 = (bf16[512,1536]{1,0:T(8,128)(2,1)S(1)}, bf16[512,1536]{1,0:T(8,128)(2,1)}, u32[]{:S(2)}, u32[]{:S(2)}) collective-permute-start(bf16[512,1536]{1,0:T(8,128)(2,1)S(1)} %copy-done.50), channel_id=1, source_target_pairs={{0,1},{1,0},{2,3},{3,2},{4,5},{5,4},{6,7},{7,6},{8,9},{9,8},{10,11... | collective-permute-start | bytes 4718600 | tf_op jit(solution)/shard_map/ppermute | solution.py:69
  807.8 10.3 collective-permute-start.21
  869.1 12.0 collective-permute-start.24
  894.4 49.0 %collective-permute-start.25 = (f32[512,1536]{1,0:T(8,128)}, f32[512,1536]{1,0:T(8,128)}, u32[]{:S(2)}, u32[]{:S(2)}) collective-permute-start(f32[512,1536]{1,0:T(8,128)} %slice.1798), channel_id=1, source_target_pairs={{0,1},{1,0},{2,3},{3,2},{4,5},{5,4},{6,7},{7,6},{8,9},{9,8},{10,11... | collective-permute-start | bytes 9437192 | tf_op jit(solution)/shard_map/ppermute | solution.py:69
  937.6 27.2 %collective-permute-start.39 = (bf16[256,1920]{1,0:T(8,128)(2,1)}, bf16[256,1920]{1,0:T(8,128)(2,1)S(1)}, u32[]{:S(2)}, u32[]{:S(2)}) collective-permute-start(bf16[256,1920]{1,0:T(8,128)(2,1)} %pad_maximum_fusion.22), channel_id=1, source_target_pairs={{0,2},{1,3},{2,4},{3,5},{4,6},{5,7},{6,0},{7,1},{8,10},{9,11},{10,... | collective-permute-start | bytes 2949128 | tf_op jit(solution)/shard_map/ppermute | solution.py:79
  938.6 67.5 %collective-permute-start.40 = (bf16[256,1920]{1,0:T(8,128)(2,1)}, bf16[256,1920]{1,0:T(8,128)(2,1)}, u32[]{:S(2)}, u32[]{:S(2)}) collective-permute-start(bf16[256,1920]{1,0:T(8,128)(2,1)} %pad_maximum_fusion.23), channel_id=1, source_target_pairs={{0,4},{1,5},{2,6},{3,7},{4,0},{5,1},{6,2},{7,3},{8,12},{9,13},{10,... | collective-permute-start | bytes 2949128 | tf_op jit(solution)/shard_map/ppermute | solution.py:79
  940.6 65.5 %collective-permute-start.41 = (bf16[256,1920]{1,0:T(8,128)(2,1)}, bf16[256,1920]{1,0:T(8,128)(2,1)}, u32[]{:S(2)}, u32[]{:S(2)}) collective-permute-start(bf16[256,1920]{1,0:T(8,128)(2,1)} %pad_maximum_fusion.24), channel_id=1, source_target_pairs={{0,6},{1,7},{2,0},{3,1},{4,2},{5,3},{6,4},{7,5},{8,14},{9,15},{10,... | collective-permute-start | bytes 2949128 | tf_op jit(solution)/shard_map/ppermute | solution.py:79
  952.3 59.9 %collective-permute-start.26 = (bf16[512,1536]{1,0:T(8,128)(2,1)S(1)}, bf16[512,1536]{1,0:T(8,128)(2,1)}, u32[]{:S(2)}, u32[]{:S(2)}) collective-permute-start(bf16[512,1536]{1,0:T(8,128)(2,1)S(1)} %get-tuple-element.160), channel_id=1, source_target_pairs={{0,1},{1,0},{2,3},{3,2},{4,5},{5,4},{6,7},{7,6},{8,9},{9,8},{10,11... | collective-permute-start | bytes 4718600 | tf_op jit(solution)/shard_map/ppermute | solution.py:69
  964.2 120.9 %collective-permute-start.17 = (f32[512,1536]{1,0:T(8,128)}, f32[512,1536]{1,0:T(8,128)}, u32[]{:S(2)}, u32[]{:S(2)}) collective-permute-start(f32[512,1536]{1,0:T(8,128)} %slice.1781), channel_id=1, source_target_pairs={{0,1},{1,0},{2,3},{3,2},{4,5},{5,4},{6,7},{7,6},{8,9},{9,8},{10,11... | collective-permute-start | bytes 9437192 | tf_op jit(solution)/shard_map/ppermute | solution.py:69
  1009.5 70.7 %collective-permute-start.42 = (bf16[256,960]{1,0:T(8,128)(2,1)}, bf16[256,960]{1,0:T(8,128)(2,1)S(1)}, u32[]{:S(2)}, u32[]{:S(2)}) collective-permute-start(bf16[256,960]{1,0:T(8,128)(2,1)} %get-tuple-element.478), channel_id=1, source_target_pairs={{0,8},{8,0},{16,24},{24,16},{1,9},{9,1},{17,25},{25,17},{2,10},{10... | collective-permute-start | bytes 1474568 | tf_op jit(solution)/shard_map/ppermute | solution.py:125
  1012.2 68.9 %collective-permute-start.44 = (bf16[256,960]{1,0:T(8,128)(2,1)}, bf16[256,960]{1,0:T(8,128)(2,1)}, u32[]{:S(2)}, u32[]{:S(2)}) collective-permute-start(bf16[256,960]{1,0:T(8,128)(2,1)} %get-tuple-element.477), channel_id=1, source_target_pairs={{0,16},{8,24},{16,0},{24,8},{1,17},{9,25},{17,1},{25,9},{2,18},{10... | collective-permute-start | bytes 1474568 | tf_op jit(solution)/shard_map/ppermute | solution.py:125
  1057.2 58.5 %collective-permute-start.27 = (f32[512,1536]{1,0:T(8,128)}, f32[512,1536]{1,0:T(8,128)}, u32[]{:S(2)}, u32[]{:S(2)}) collective-permute-start(f32[512,1536]{1,0:T(8,128)} %slice.1800), channel_id=1, source_target_pairs={{0,1},{1,0},{2,3},{3,2},{4,5},{5,4},{6,7},{7,6},{8,9},{9,8},{10,11... | collective-permute-start | bytes 9437192 | tf_op jit(solution)/shard_map/ppermute | solution.py:69
  1083.0 13.6 collective-permute-start.43
  1092.5 13.1 collective-permute-start.45
  1224.2 14.6 collective-permute-start.28
  1225.8 14.3 collective-permute-start.29
  1230.1 29.1 %collective-permute-start.33 = (bf16[512,768]{1,0:T(8,128)(2,1)}, bf16[512,768]{1,0:T(8,128)(2,1)}, u32[]{:S(2)}, u32[]{:S(2)}) collective-permute-start(bf16[512,768]{1,0:T(8,128)(2,1)} %get-tuple-element.471), channel_id=1, source_target_pairs={{0,1},{1,0},{2,3},{3,2},{4,5},{5,4},{6,7},{7,6},{8,9},{9,8},{10,11... | collective-permute-start | bytes 2359304 | tf_op jit(solution)/shard_map/ppermute | solution.py:69
  1245.6 15.9 collective-permute-start.32
  1890.4 23.6 %collective-permute-start.46 = (bf16[192,4608]{1,0:T(8,128)(2,1)S(1)}, bf16[192,4608]{1,0:T(8,128)(2,1)S(1)}, u32[]{:S(2)}, u32[]{:S(2)}) collective-permute-start(bf16[192,4608]{1,0:T(8,128)(2,1)S(1)} %broadcast_select_fusion.2), channel_id=1, source_target_pairs={{0,1},{1,0},{2,3},{3,2},{4,5},{5,4},{6,7},{7,6},{8,9},{9,8},{10,11... | collective-permute-start | bytes 5308424 | tf_op jit(solution)/shard_map/ppermute | solution.py:69
  1890.6 20.3 %collective-permute-start.38 = (bf16[192,2048]{1,0:T(8,128)(2,1)S(1)}, bf16[192,2048]{1,0:T(8,128)(2,1)S(1)}, u32[]{:S(2)}, u32[]{:S(2)}) collective-permute-start(bf16[192,2048]{1,0:T(8,128)(2,1)S(1)} %broadcast_select_fusion.22), channel_id=1, source_target_pairs={{0,1},{1,0},{2,3},{3,2},{4,5},{5,4},{6,7},{7,6},{8,9},{9,8},{10,11... | collective-permute-start | bytes 2359304 | tf_op jit(solution)/shard_map/ppermute | solution.py:69
  1891.8 28.5 %collective-permute-start.37 = (bf16[192,4608]{1,0:T(8,128)(2,1)S(1)}, bf16[192,4608]{1,0:T(8,128)(2,1)S(1)}, u32[]{:S(2)}, u32[]{:S(2)}) collective-permute-start(bf16[192,4608]{1,0:T(8,128)(2,1)S(1)} %broadcast_select_fusion.6), channel_id=1, source_target_pairs={{0,1},{1,0},{2,3},{3,2},{4,5},{5,4},{6,7},{7,6},{8,9},{9,8},{10,11... | collective-permute-start | bytes 5308424 | tf_op jit(solution)/shard_map/ppermute | solution.py:69
  (208 other events, 2101.2 us)

commit v2 on v1

--- a/solution.py
+++ b/solution.py
@@ -29,13 +29,6 @@
     return gelu_tanh(gate_pre) * up_pre
 
 
-def lru_gates(rate_pre, input_pre, decay_w, conv_out):
-    log_coef = -8.0 * jax.nn.sigmoid(rate_pre) * decay_w
-    lru_coef = jnp.exp(log_coef)
-    lru_drive = jnp.sqrt(-jnp.expm1(2.0 * log_coef)) * jax.nn.sigmoid(input_pre) * conv_out
-    return (lru_coef, lru_drive)
-
-
 def matmul(first_op, second_op):
     return jnp.dot(first_op, second_op, preferred_element_type=F32)
 
@@ -92,37 +85,74 @@
     )
 
 
-def column_halves(w, unit, parts=1):
-    sub, places = unit_pieces(w.shape[1], unit, parts)
-    return tuple(
-        jnp.concatenate([w[:, at : at + sub] for at in places[core]], axis=1) for core in (0, 1)
-    )
-
-
-def joined_columns(first, second, unit, parts=1):
-    sub, places = unit_pieces(2 * first.shape[1], unit, parts)
-    pieces = {}
-    for half, starts in zip((first, second), places):
-        for i, at in enumerate(starts):
-            pieces[at] = half[:, i * sub : (i + 1) * sub]
-    return jnp.concatenate([pieces[at] for at in sorted(pieces)], axis=1)
-
-
-def chip_rows(halves):
-    own = by_core(halves[0], halves[1])
-    other = swap_cores(by_core(halves[1], halves[0]))
-    return jnp.concatenate([by_core(own, other), by_core(other, own)], axis=0)
-
-
-def rep_masks(flip):
-    size = lax.axis_size("rep")
-    masks = [1 << i for i in range(size.bit_length() - 1)]
-    return masks[::-1] if flip else masks
-
-
-def swap_rep(x, mask):
-    size = lax.axis_size("rep")
-    return lax.ppermute(x, "rep", [(i, i ^ mask) for i in range(size)])
+def split_kernel(sub, places, core_ref, *refs):
+    ins, (mine, other) = refs[:-2], refs[-2:]
+
+    def run(core):
+        for k, out in ((core, mine), (1 - core, other)):
+            column = 0
+            for ref in ins:
+                for at in places[k]:
+                    out[:, column : column + sub] = ref[:, at : at + sub]
+                    column += sub
+
+    for core in (0, 1):
+        pl.when(core_ref[0] == core)(functools.partial(run, core))
+
+
+def split_columns(arrays, unit, parts=1):
+    sub, places = unit_pieces(arrays[0].shape[1], unit, parts)
+    rows, width = arrays[0].shape
+    total = width * len(arrays) // 2
+    tile = 48 if rows % 48 == 0 else rows
+    shape = jax.ShapeDtypeStruct((rows, total), arrays[0].dtype)
+    out = pl.BlockSpec((tile, total), lambda i, core: (i, 0))
+    return pl.pallas_call(
+        functools.partial(split_kernel, sub, places),
+        grid_spec=pltpu.PrefetchScalarGridSpec(
+            num_scalar_prefetch=1,
+            grid=(rows // tile,),
+            in_specs=[pl.BlockSpec((tile, width), lambda i, core: (i, 0))] * len(arrays),
+            out_specs=[out, out],
+        ),
+        out_shape=[shape, shape],
+    )(my_core().astype(jnp.int32).reshape(1), *arrays)
+
+
+def join_kernel(sub, places, core_ref, mine, other, *outs):
+    def run(core):
+        for k, ref in ((core, mine), (1 - core, other)):
+            column = 0
+            for out in outs:
+                for at in places[k]:
+                    out[:, at : at + sub] = ref[:, column : column + sub].astype(out.dtype)
+                    column += sub
+
+    for core in (0, 1):
+        pl.when(core_ref[0] == core)(functools.partial(run, core))
+
+
+def join_columns(mine, other, count, unit, parts=1):
+    rows, total = mine.shape
+    width = 2 * total // count
+    sub, places = unit_pieces(width, unit, parts)
+    tile = 48 if rows % 48 == 0 else rows
+    half = pl.BlockSpec((tile, total), lambda i, core: (i, 0))
+    return pl.pallas_call(
+        functools.partial(join_kernel, sub, places),
+        grid_spec=pltpu.PrefetchScalarGridSpec(
+            num_scalar_prefetch=1,
+            grid=(rows // tile,),
+            in_specs=[half, half],
+            out_specs=[pl.BlockSpec((tile, width), lambda i, core: (i, 0))] * count,
+        ),
+        out_shape=[jax.ShapeDtypeStruct((rows, width), F32)] * count,
+    )(my_core().astype(jnp.int32).reshape(1), mine, other)
+
+
+def chip_rows(mine, other):
+    got = swap_cores(other)
+    return jnp.concatenate([by_core(mine, got), by_core(got, mine)], axis=0)
 
 
 MESH_ID = pl.DeviceIdType.MESH
@@ -350,23 +380,31 @@
                 stage(tick - at * LAG)
 
 
+def chip_groups():
+    count = lax.axis_size("shard")
+    return [list(range(core, count, 2)) for core in (0, 1)]
+
+
+def gather_plain(array, split):
+    if split:
+        part = array.shape[0] // lax.axis_size("rep")
+        array = lax.dynamic_slice_in_dim(array, lax.axis_index("rep") * part, part, 0)
+    array = lax.all_gather(array, "shard", axis=0, tiled=True, axis_index_groups=chip_groups())
+    return lax.all_gather(array, "rep", axis=0, tiled=True) if split else array
+
+
+def reduce_plain(whole):
+    part = lax.psum_scatter(whole, "rep", scatter_dimension=0, tiled=True)
+    part = lax.psum_scatter(
+        part, "shard", scatter_dimension=0, tiled=True, axis_index_groups=chip_groups()
+    )
+    return lax.all_gather(part, "rep", axis=0, tiled=True)
+
+
 def gather_all(arrays, splits, widths):
     reps, chips = lax.axis_size("rep"), lax.axis_size("shard") // 2
     if any(split and array.shape[0] // reps % 16 for array, split in zip(arrays, splits)):
-        results = []
-        for array, split in zip(arrays, splits):
-            if split:
-                part = array.shape[0] // reps
-                array = lax.dynamic_slice_in_dim(array, lax.axis_index("rep") * part, part, 0)
-            array = lax.all_gather(
-                array,
-                "shard",
-                axis=0,
-                tiled=True,
-                axis_index_groups=[list(range(core, 2 * chips, 2)) for core in (0, 1)],
-            )
-            results.append(lax.all_gather(array, "rep", axis=0, tiled=True) if split else array)
-        return results
+        return [gather_plain(array, split) for array, split in zip(arrays, splits)]
     chunks = []
     for i, (array, split, wide) in enumerate(zip(arrays, splits, widths)):
         sub = array.shape[0] // reps if split else array.shape[0]
@@ -391,34 +429,10 @@
         compiler_params=pltpu.CompilerParams(
             collective_id=0, has_side_effects=True, vmem_limit_bytes=40 * 1024 * 1024
         ),
+        cost_estimate=pl.CostEstimate(
+            flops=0, bytes_accessed=sum(70 * a.size for a in arrays), transcendentals=0
+        ),
     )(*arrays)
-
-
-def sum_chips(parts):
-    chips = lax.axis_size("shard") // 2
-    chip = my_chip()
-    sub = parts[0].shape[0] // chips
-
-    def rows_of(by):
-        at = lax.rem(chip + by, chips) * sub
-        return jnp.concatenate(
-            [lax.dynamic_slice_in_dim(part, at, sub, 0) for part in parts], axis=1
-        )
-
-    total = rows_of(0).astype(F32)
-    for by in range(1, chips):
-        total = total + shift_chip(rows_of(by), by).astype(F32)
-    return total.astype(BF16)
-
-
-def sum_rep(x):
-    middle = x.shape[1] // 2
-    halves = [x[:, :middle], x[:, middle:]]
-    for flip in (0, 1):
-        for mask in rep_masks(flip):
-            here = halves[flip]
-            halves[flip] = (here.astype(F32) + swap_rep(here, mask).astype(F32)).astype(BF16)
-    return jnp.concatenate(halves, axis=1)
 
 
 def reduce_kernel(chunks, counts, chips, *refs):
@@ -520,10 +534,12 @@
             if k["given"] is not None:
                 total = givens[k["given"]][at, :, columns].astype(F32)
             else:
-                left = big_left if k["big"] else lefts[k["left"]]
-                total = jnp.dot(
-                    left[at], right_buf[c % 6, :, columns], preferred_element_type=F32
-                )
+                right = right_buf[c % 6, :, columns]
+                if k["big"]:
+                    total = jnp.dot(big_left[at], right, preferred_element_type=F32)
+                else:
+                    left = lefts[k["left"]][:, pl.ds(pl.multiple_of(at * rows, 128), rows)]
+                    total = matmul_left(left, right)
             for ref, index in arrivals:
                 total = total + ref[index + (pl.ds(0, rows), columns)].astype(F32)
             target[0][target[1] + (pl.ds(0, rows), columns)] = total.astype(BF16)
@@ -704,29 +720,20 @@
                 whole = jnp.concatenate(
                     [matmul_left(left, right).astype(BF16) for right in given], axis=1
                 )
-            part = lax.psum_scatter(whole, "rep", scatter_dimension=0, tiled=True)
-            count = lax.axis_size("shard")
-            part = lax.psum_scatter(
-                part,
-                "shard",
-                scatter_dimension=0,
-                tiled=True,
-                axis_index_groups=[list(range(core, count, 2)) for core in (0, 1)],
-            )
-            results.append(lax.all_gather(part, "rep", axis=0, tiled=True))
+            results.append(reduce_plain(whole))
         return results
     lefts, rights, givens, chunks, outs = [], [], [], [], []
     subs = [
         (given[0].shape[1] if left is None else left.shape[1] // reps) // chips
         for left, given, _ in products
     ]
-    small = min(subs)
+    largest = max(subs)
     for (left, parts, wide), sub in zip(products, subs):
         total = sum(part.shape[-1] for part in parts)
         outs.append(jax.ShapeDtypeStruct((reps * sub, total), BF16))
         first_right = len(rights)
         if left is not None:
-            lefts.append(left.T.reshape(reps, chips * sub, depth))
+            lefts.append(left.T.reshape(reps, chips * sub, depth) if sub == largest else left)
             rights.extend(parts)
         else:
             givens.extend(parts)
@@ -745,14 +752,14 @@
                         sub=sub,
                         out=len(outs) - 1,
                         place=before + first,
-                        big=sub > small,
+                        big=sub == largest,
                         load=False,
                     )
                 )
             mine.append(row)
             before += part.shape[-1]
         mine = [chunk for group in zip(*mine) for chunk in group]
-        mine[0]["load"] = sub > small
+        mine[0]["load"] = sub == largest
         chunks += mine
     for i, chunk in enumerate(chunks):
         chunk["flip"] = i % 2
@@ -802,68 +809,237 @@
         compiler_params=pltpu.CompilerParams(
             collective_id=1, has_side_effects=True, vmem_limit_bytes=62 * 1024 * 1024
         ),
+        cost_estimate=pl.CostEstimate(
+            flops=0,
+            bytes_accessed=sum(128 * shape.size for shape in outs),
+            transcendentals=0,
+        ),
     )(*lefts, *rights, *givens)
     return results[: len(outs)]
 
 
-def reduce_chips(grads):
-    return sum_rep(sum_chips(grads))
-
-
 def own_rows(rows):
     part = rows.shape[0] // 2
-    first, second = rows[:part], rows[part:]
-    keep = by_core(first, second)
-    got = swap_cores(by_core(second, first))
-    return by_core(keep, got), by_core(got, keep)
-
-
-def scan_kernel(reverse, coef_ref, drive_ref, cum_ref, out_ref):
-    rows, lanes = coef_ref.shape[1], coef_ref.shape[2]
+    core = my_core()
+    mine = lax.dynamic_slice_in_dim(rows, core * part, part, 0)
+    return mine, swap_cores(lax.dynamic_slice_in_dim(rows, (1 - core) * part, part, 0))
+
+
+ROOT = math.sqrt(2.0 / math.pi)
+
+
+def gelu_parts(v):
+    inner = jnp.tanh(ROOT * (v + 0.044715 * v * v * v))
+    value = 0.5 * v * (1.0 + inner)
+    slope = 0.5 * (1.0 + inner) + 0.5 * v * (1.0 - inner * inner) * ROOT * (
+        1.0 + 3.0 * 0.044715 * v * v
+    )
+    return value, slope
+
+
+def one_minus_exp(v):
+    series = 1.0 + v / 8.0
+    for order in (7.0, 6.0, 5.0, 4.0, 3.0, 2.0):
+        series = 1.0 + v * series * (1.0 / order)
+    return -v * series
+
+
+def sigmoid(v):
+    return 1.0 / (1.0 + jnp.exp(-v))
+
+
+def scan_rows(a, b, a_ref, b_ref, cum_ref, out_ref, reverse):
+    rows, lanes = a.shape
+    place = lax.rem(lax.broadcasted_iota(jnp.int32, (rows, lanes), 0), 8)
+    for k in (1, 2, 4):
+        by = rows - k if reverse else k
+        inside = place < 8 - k if reverse else place >= k
+        a_before = jnp.where(inside, pltpu.roll(a, by, 0), 1.0)
+        b_before = jnp.where(inside, pltpu.roll(b, by, 0), 0.0)
+        b = a * b_before + b
+        a = a * a_before
+    a_ref[...] = a
+    b_ref[...] = b
     groups = rows // 8
-    place = lax.broadcasted_iota(jnp.int32, (8, lanes), 0)
+    last = 0 if reverse else 7
 
     def step(turn, carry):
         carry_cum, carry_out = carry
         group = groups - 1 - turn if reverse else turn
         where = pl.ds(pl.multiple_of(group * 8, 8), 8)
-        a = coef_ref[0, where, :]
-        b = drive_ref[0, where, :]
-        for k in (1, 2, 4):
-            by = 8 - k if reverse else k
-            inside = place < 8 - k if reverse else place >= k
-            a_before = jnp.where(inside, pltpu.roll(a, by, 0), 1.0)
-            b_before = jnp.where(inside, pltpu.roll(b, by, 0), 0.0)
-            b = a * b_before + b
-            a = a * a_before
-        out = b + a * carry_out
-        cum = a * carry_cum
+        out = b_ref[where, :] + a_ref[where, :] * carry_out
+        cum = a_ref[where, :] * carry_cum
         out_ref[0, where, :] = out
         cum_ref[0, where, :] = cum
-        last = 0 if reverse else 7
         return (
             jnp.broadcast_to(cum[last : last + 1], (8, lanes)),
             jnp.broadcast_to(out[last : last + 1], (8, lanes)),
         )
 
     lax.fori_loop(
-        0, groups, step, (jnp.ones((8, lanes), F32), jnp.zeros((8, lanes), F32))
-    )
-
-
-def linear_scan(coef, drive, reverse):
-    batch, rows, width = coef.shape
-    lanes = min(512, width)
-    spec = pl.BlockSpec((1, rows, lanes), lambda b, i: (b, 0, i))
-    shape = jax.ShapeDtypeStruct(coef.shape, F32)
+        0, groups, step, (jnp.ones((8, lanes), F32), jnp.zeros((8, lanes), F32)), unroll=4
+    )
+
+
+def shifted_rows(x, tail, by):
+    return pltpu.roll(jnp.concatenate([tail, x], axis=0), by, 0)[8:] if by else x
+
+
+def conv_rows(branch, tail, taps):
+    return sum(taps[j : j + 1] * shifted_rows(branch, tail, j) for j in range(taps.shape[0]))
+
+
+def by_blocks(low, weights, block, contract=0):
+    parts = []
+    for i in range(low.shape[1] // block):
+        parts.append(
+            lax.dot_general(
+                low[:, i * block : (i + 1) * block],
+                weights[i * block : (i + 1) * block],
+                (((1,), (contract,)), ((), ())),
+                preferred_element_type=F32,
+            )
+        )
+    return jnp.concatenate(parts, axis=1)
+
+
+def lru_forward_kernel(
+    block, branch_ref, tail_ref, rate_ref, input_ref, taps_ref, decay_ref,
+    coef_ref, cum_ref, state_ref, a_ref, b_ref,
+):
+    conv = conv_rows(branch_ref[0], tail_ref[0], taps_ref[...])
+    low = conv.astype(BF16)
+    log_coef = -8.0 * sigmoid(by_blocks(low, rate_ref[...], block)) * decay_ref[...]
+    coef = jnp.exp(log_coef)
+    gate = sigmoid(by_blocks(low, input_ref[...], block))
+    drive = jnp.sqrt(one_minus_exp(2.0 * log_coef)) * gate * conv
+    coef_ref[0] = coef
+    scan_rows(coef, drive, a_ref, b_ref, cum_ref, state_ref, False)
+
+
+def lru_adjoint_kernel(
+    gated_ref, coef_ref, cum_ref, local_ref, start_ref, back_ref,
+    later_ref, adjoint_ref, gated_back_ref, a_ref, b_ref,
+):
+    value, slope = gelu_parts(gated_ref[0])
+    back = back_ref[0].astype(F32)
+    state = local_ref[0] + cum_ref[0] * start_ref[0][:1]
+    gated_back_ref[0] = (back * state * slope).astype(BF16)
+    coef = coef_ref[0]
+    rows = coef.shape[0]
+    last = lax.broadcasted_iota(jnp.int32, coef.shape, 0) == rows - 1
+    coef_next = jnp.where(last, 1.0, pltpu.roll(coef, rows - 1, 0))
+    scan_rows(coef_next, back * value, a_ref, b_ref, later_ref, adjoint_ref, True)
+
+
+def lru_backward_kernel(
+    block, branch_ref, tail_ref, rate_ref, input_ref, taps_ref, decay_ref,
+    cum_ref, local_ref, start_ref, later_ref, adjoint_ref, carry_ref,
+    branch_back_ref, first_ref, last_ref, rate_grad_ref, input_grad_ref, taps_grad_ref, decay_grad_ref,
+):
+    branch, tail, taps, decay = branch_ref[0], tail_ref[0], taps_ref[...], decay_ref[...]
+    rows = branch.shape[0]
+    conv = conv_rows(branch, tail, taps)
+    low = conv.astype(BF16)
+    rate = sigmoid(by_blocks(low, rate_ref[...], block))
+    gate = sigmoid(by_blocks(low, input_ref[...], block))
+    log_coef = -8.0 * rate * decay
+    coef = jnp.exp(log_coef)
+    root = jnp.sqrt(one_minus_exp(2.0 * log_coef))
+    start = start_ref[0][:1]
+    state = local_ref[0] + cum_ref[0] * start
+    first = lax.broadcasted_iota(jnp.int32, state.shape, 0) == 0
+    before = jnp.where(first, start, pltpu.roll(state, 1, 0))
+    adjoint = adjoint_ref[0] + later_ref[0] * carry_ref[0][:1]
+    back_root = adjoint * gate * conv
+    back_log = (adjoint * before - back_root * coef / root) * coef
+    back_rate = back_log * (-8.0 * decay) * rate * (1.0 - rate)
+    back_gate = adjoint * root * conv * gate * (1.0 - gate)
+    rate_low, gate_low = back_rate.astype(BF16), back_gate.astype(BF16)
+    back_conv = (
+        adjoint * root * gate
+        + by_blocks(rate_low, rate_ref[...], block, 1)
+        + by_blocks(gate_low, input_ref[...], block, 1)
+    )
+
+    def block_grads(back):
+        return jnp.concatenate(
+            [
+                lax.dot_general(
+                    low[:, i : i + block],
+                    back[:, i : i + block],
+                    (((0,), (0,)), ((), ())),
+                    preferred_element_type=F32,
+                )
+                for i in range(0, low.shape[1], block)
+            ],
+            axis=0,
+        )
+
+    taps_grad = jnp.concatenate(
+        [
+            jnp.sum(back_conv * shifted_rows(branch, tail, j), axis=0, keepdims=True)
+            for j in range(taps.shape[0])
+        ],
+        axis=0,
+    )
+    grads = (
+        (rate_grad_ref, block_grads(rate_low)),
+        (input_grad_ref, block_grads(gate_low)),
+        (taps_grad_ref, taps_grad),
+        (decay_grad_ref, jnp.sum(back_log * (-8.0 * rate), axis=0, keepdims=True)),
+    )
+
+    @pl.when(pl.program_id(1) == 0)
+    def _():
+        for ref, grad in grads:
+            ref[...] = grad
+
+    @pl.when(pl.program_id(1) > 0)
+    def _():
+        for ref, grad in grads:
+            ref[...] += grad
+
+    extended = jnp.concatenate([back_conv, jnp.zeros((8, branch.shape[1]), F32)], axis=0)
+    branch_back = sum(
+        taps[j : j + 1] * (pltpu.roll(extended, rows + 8 - j, 0)[:rows] if j else back_conv)
+        for j in range(taps.shape[0])
+    )
+    branch_back_ref[0] = branch_back.astype(BF16)
+    first_ref[0] = back_conv[:8]
+    last_ref[0] = branch_back[rows - 8 :]
+
+
+def lru_call(kernel, arrays, outs, rows, scratch=()):
+    lanes = 256
+    kinds = {
+        "first": ((1, rows, lanes), lambda i, b: (b, 0, i)),
+        "second": ((1, rows, lanes), None),
+        "edge": ((1, 8, lanes), lambda i, b: (b, 0, i)),
+        "weight": ((lanes, 128), lambda i, b: (i, 0)),
+        "taps": ((4, lanes), lambda i, b: (0, i)),
+        "row": ((1, lanes), lambda i, b: (0, i)),
+    }
+    width = max(a.shape[-1] for a, kind in outs if kind == "first")
+
+    def spec(kind):
+        shape, place = kinds[kind]
+        if kind == "second":
+            place = lambda i, b: (b, 0, i + width // lanes)
+        return pl.BlockSpec(shape, place)
+
     return pl.pallas_call(
-        functools.partial(scan_kernel, reverse),
-        grid=(batch, width // lanes),
-        in_specs=[spec, spec],
-        out_specs=[spec, spec],
-        out_shape=[shape, shape],
-        compiler_params=pltpu.CompilerParams(vmem_limit_bytes=48 * 1024 * 1024),
-    )(coef, drive)
+        kernel,
+        grid=(width // lanes, 2),
+        in_specs=[spec(kind) for _, kind in arrays],
+        out_specs=[spec(kind) for _, kind in outs],
+        out_shape=[a for a, _ in outs],
+        scratch_shapes=list(scratch),
+        compiler_params=pltpu.CompilerParams(vmem_limit_bytes=56 * 1024 * 1024),
+        cost_estimate=pl.CostEstimate(
+            flops=0, bytes_accessed=16 * rows * width * 4, transcendentals=0
+        ),
+    )(*[a for a, _ in arrays])
 
 
 def carried_in(prod, part, reverse):
@@ -880,16 +1056,87 @@
     return total
 
 
-def window_scores(query_heads, key_win, start_row, behind):
-    row_count = query_heads.shape[0]
-    score_scale = 1.0 / math.sqrt(query_heads.shape[2])
-    raw_scores = (
-        jnp.einsum("thd,kd->htk", query_heads, key_win, preferred_element_type=F32) * score_scale
-    )
-    row_pos = start_row + jnp.arange(row_count, dtype=jnp.int32)[:, None]
-    col_pos = start_row - behind + jnp.arange(key_win.shape[0], dtype=jnp.int32)[None, :]
-    allowed = (col_pos <= row_pos) & (col_pos > row_pos - WINDOW) & (col_pos >= 0)
-    return jnp.where(allowed[None], raw_scores, -1e30)
+def block_probs(query, keys, lowest):
+    scores = lax.dot_general(
+        query, keys, (((1,), (1,)), ((), ())), preferred_element_type=F32
+    ) * (1.0 / math.sqrt(query.shape[1]))
+    row = lax.broadcasted_iota(jnp.int32, scores.shape, 0)
+    column = lax.broadcasted_iota(jnp.int32, scores.shape, 1)
+    allowed = (column > row) & (column <= row + WINDOW) & (column >= lowest)
+    scores = jnp.where(allowed, scores, -1e30)
+    powers = jnp.exp(scores - jnp.max(scores, axis=1, keepdims=True))
+    return powers * (1.0 / jnp.sum(powers, axis=1, keepdims=True))
+
+
+def attention_kernel(start_ref, query_ref, kv_ref, out_ref):
+    rows, size = query_ref.shape
+    block = min(256, rows)
+    for first in range(0, rows, block):
+        keys = kv_ref[first : first + block + WINDOW, :size]
+        values = kv_ref[first : first + block + WINDOW, size:]
+        probs = block_probs(
+            query_ref[first : first + block, :], keys, WINDOW - first - start_ref[0]
+        )
+        out_ref[first : first + block, :] = jnp.dot(
+            probs.astype(BF16), values, preferred_element_type=F32
+        ).astype(BF16)
+
+
+def attention_back_kernel(start_ref, query_ref, back_ref, kv_ref, query_back_ref, kv_back_ref):
+    rows, size = query_ref.shape
+    block = min(256, rows)
+    scale = 1.0 / math.sqrt(size)
+
+    @pl.when(pl.program_id(0) == 0)
+    def _():
+        kv_back_ref[...] = jnp.zeros_like(kv_back_ref)
+
+    for first in range(0, rows, block):
+        here = slice(first, first + block + WINDOW)
+        keys, values = kv_ref[here, :size], kv_ref[here, size:]
+        query = query_ref[first : first + block, :]
+        back = back_ref[first : first + block, :]
+        probs = block_probs(query, keys, WINDOW - first - start_ref[0])
+        back_probs = lax.dot_general(
+            back, values, (((1,), (1,)), ((), ())), preferred_element_type=F32
+        )
+        prob_dot = jnp.sum(probs * back_probs, axis=1, keepdims=True)
+        back_scores = (probs * (back_probs - prob_dot)).astype(BF16)
+        query_back_ref[first : first + block, :] = (
+            jnp.dot(back_scores, keys, preferred_element_type=F32) * scale
+        ).astype(BF16)
+        kv_back_ref[here, :size] += (
+            lax.dot_general(
+                back_scores, query, (((0,), (0,)), ((), ())), preferred_element_type=F32
+            )
+            * scale
+        )
+        kv_back_ref[here, size:] += lax.dot_general(
+            probs.astype(BF16), back, (((0,), (0,)), ((), ())), preferred_element_type=F32
+        )
+
+
+def attention_call(kernel, start, by_head, kv, outs):
+    rows, width = by_head[0].shape
+    size = kv.shape[1] // 2
+    head = pl.BlockSpec((rows, size), lambda h, start: (0, h))
+    whole = pl.BlockSpec(kv.shape, lambda h, start: (0, 0))
+    return pl.pallas_call(
+        kernel,
+        grid_spec=pltpu.PrefetchScalarGridSpec(
+            num_scalar_prefetch=1,
+            grid=(width // size,),
+            in_specs=[head] * len(by_head) + [whole],
+            out_specs=[head, whole][: len(outs)],
+        ),
+        out_shape=outs,
+        compiler_params=pltpu.CompilerParams(vmem_limit_bytes=56 * 1024 * 1024),
+        cost_estimate=pl.CostEstimate(
+            flops=12 * rows * width * WINDOW,
+            bytes_accessed=64 * 1024 * 1024,
+            transcendentals=0,
+        ),
+    )(jnp.reshape(start, (1,)), *by_head, kv)
 
 
 def with_sibling(x):
@@ -983,23 +1230,23 @@
     )
     out_ordered = ordered(attn_out).astype(BF16)
     out_halves = out_ordered[:, : width // 2], out_ordered[:, width // 2 :]
+    attn_halves = tuple(jnp.concatenate(both, axis=1) for both in zip(qkv_halves, out_halves))
     qkv_width = half + head_size
     ff_unit = first_down.shape[0]
     lru_unit = mixer_out.shape[0]
 
-    def both_halves(first, second, unit, parts):
-        pairs = zip(column_halves(first, unit, parts), column_halves(second, unit, parts))
-        return tuple(jnp.concatenate(pair, axis=1) for pair in pairs)
-
     block_width = rate_gate.shape[1]
     tap_count = conv_taps.shape[1]
     spare = block_width - tap_count - 1
-    attn_wide, first_in_w, first_down_w, lru_in_w, mix_wide, second_in_w, second_down_w = gather_all(
+    second_chip = chip_rows(*split_columns((second_gate, second_up), ff_unit, reps))
+    attn_halves, second_chip = lax.optimization_barrier((attn_halves, second_chip))
+    second_in_w = gather_plain(second_chip, True)
+    attn_wide, first_in_w, first_down_w, lru_in_w, mix_wide, second_down_w = gather_all(
         (
-            chip_rows(tuple(jnp.concatenate(both, axis=1) for both in zip(qkv_halves, out_halves))),
-            chip_rows(both_halves(first_gate, first_up, ff_unit, reps)),
+            chip_rows(by_core(*attn_halves), by_core(*attn_halves[::-1])),
+            chip_rows(*split_columns((first_gate, first_up), ff_unit, reps)),
             ordered(first_down).astype(BF16),
-            chip_rows(both_halves(branch_proj, gated_proj, lru_unit, 1)),
+            chip_rows(*split_columns((branch_proj, gated_proj), lru_unit)),
             jnp.concatenate(
                 [
                     rate_gate,
@@ -1011,11 +1258,10 @@
                 ],
                 axis=1,
             ),
-            chip_rows(both_halves(second_gate, second_up, ff_unit, reps)),
             ordered(second_down).astype(BF16),
         ),
-        (True, True, True, True, False, True, True),
-        (1792, 1536, 1536, 1024, 1920, 1536, 1536),
+        (True, True, True, True, False, True),
+        (1792, 1536, 1536, 1024, 1920, 1536),
     )
     qkv_own = attn_wide[:, :qkv_width]
     gains = attn_wide[:, qkv_width : qkv_width + 128].astype(F32)
@@ -1042,17 +1288,14 @@
         axis=0,
     )
     behind = kv_win.shape[0] - row_count
-    key_win, value_win = kv_win[:, :head_size], kv_win[:, head_size:]
-    head_count = query_rows.shape[1] // head_size
-    query_heads = query_rows.reshape(row_count, head_count, head_size)
-    scores = window_scores(query_heads, key_win, start_row, behind)
-    row_peak = jnp.max(scores, axis=-1, keepdims=True)
-    exp_scores = jnp.exp(scores - row_peak)
-    exp_total = jnp.sum(exp_scores, axis=-1, keepdims=True)
-    log_total = row_peak + jnp.log(exp_total)
-    probs_low = (exp_scores / exp_total).astype(BF16)
-    attended = jnp.einsum("htk,kd->thd", probs_low, value_win, preferred_element_type=F32)
-    attended_low = ordered(attended.reshape(row_count, width).astype(BF16)).astype(BF16)
+    (attended,) = attention_call(
+        attention_kernel,
+        start_row,
+        [query_rows],
+        kv_win,
+        [jax.ShapeDtypeStruct((row_count, width), BF16)],
+    )
+    attended_low = ordered(attended).astype(BF16)
     out_mine = matmul(attended_low, attn_own)
     out_other = matmul(attended_low, attn_sib)
     resid_one = inputs + jnp.concatenate(
@@ -1061,35 +1304,38 @@
 
     middle, first_kept = mlp_forward(resid_one, gain_first, first_in_w, first_down_w)
 
-    rate_blocks = small_w[:, :block_width].reshape(-1, block_width, block_width)
-    input_blocks = small_w[:, block_width : 2 * block_width].reshape(-1, block_width, block_width)
-    conv_w = small_w[:, 2 * block_width : 2 * block_width + tap_count].astype(F32)
-    decay_w = small_w[:, 2 * block_width + tap_count].astype(F32)
+    conv_w = small_w[:, 2 * block_width : 2 * block_width + tap_count].astype(F32).T
+    decay_w = small_w[:, 2 * block_width + tap_count].astype(F32)[None]
+    rate_w = small_w[:, :block_width]
+    input_w = small_w[:, block_width : 2 * block_width]
     mix_normed = with_sibling(rms_norm(middle, gain_mix).astype(BF16))
     lru_width = lru_in_w.shape[1] // 2
-    block_count = lru_width // block_width
     branch_gated = matmul(mix_normed, lru_in_w).reshape(2, row_count, 2 * lru_width)
-    branch, gated_pre = branch_gated[:, :, :lru_width], branch_gated[:, :, lru_width:]
-    tail_rows = shift_rep(branch[:, row_count - (tap_count - 1) :], 1)
-    extended = jnp.concatenate([tail_rows, branch], axis=1)
-
-    def earlier(offset):
-        return extended[:, tap_count - 1 - offset : tap_count - 1 - offset + row_count]
-
-    conv_out = sum(conv_w[:, offset] * earlier(offset) for offset in range(tap_count))
-    conv_low = conv_out.astype(BF16).reshape(2 * row_count, block_count, block_width)
-
-    def through_blocks(values, blocks, how):
-        return jnp.einsum(how, values, blocks, preferred_element_type=F32)
-
-    rate_pre = through_blocks(conv_low, rate_blocks, "tbi,bij->tbj").reshape(branch.shape)
-    input_pre = through_blocks(conv_low, input_blocks, "tbi,bij->tbj").reshape(branch.shape)
-    lru_coef, lru_drive = lru_gates(rate_pre, input_pre, decay_w, conv_out)
-    cum_coef, local_state = linear_scan(lru_coef, lru_drive, False)
+    tail_rows = shift_rep(branch_gated[:, row_count - 8 :, :lru_width], 1)
+    lru_inputs = [
+        (branch_gated, "first"),
+        (tail_rows, "edge"),
+        (rate_w, "weight"),
+        (input_w, "weight"),
+        (conv_w, "taps"),
+        (decay_w, "row"),
+    ]
+    wide = (jax.ShapeDtypeStruct((2, row_count, lru_width), F32), "first")
+    wide_low = (jax.ShapeDtypeStruct((2, row_count, lru_width), BF16), "first")
+    edge = (jax.ShapeDtypeStruct((2, 8, lru_width), F32), "edge")
+    scans = [pltpu.VMEM((row_count, 256), F32)] * 2
+    lru_coef, cum_coef, local_state = lru_call(
+        functools.partial(lru_forward_kernel, block_width),
+        lru_inputs,
+        [wide, wide, wide],
+        row_count,
+        scans,
+    )
     start_state = carried_in(cum_coef[:, -1], local_state[:, -1], False)
-    lru_state = local_state + cum_coef * start_state[:, None]
-    gated_act = gelu_tanh(gated_pre)
-    mix_low = (lru_state * gated_act).astype(BF16).reshape(2 * row_count, lru_width)
+    start_edge = jnp.broadcast_to(start_state[:, None], edge[0].shape)
+    gated_act = gelu_tanh(branch_gated[:, :, lru_width:])
+    mix_low = ((local_state + cum_coef * start_state[:, None]) * gated_act).astype(BF16)
+    mix_low = mix_low.reshape(2 * row_count, lru_width)
     resid_two = middle + sum_parts(matmul(mix_low, mix_w))
 
     final_rows, second_kept = mlp_forward(
@@ -1106,55 +1352,80 @@
         back_final,
     )
 
+    down_part = lax.psum_scatter(
+        matmul_left(*second_grads[3]).astype(BF16), "rep", scatter_dimension=0, tiled=True
+    )
+    in_part = lax.psum_scatter(
+        matmul_left(
+            second_grads[1][0],
+            jnp.concatenate([second_grads[1][1], second_grads[2][1]], axis=1),
+        ).astype(BF16),
+        "rep",
+        scatter_dimension=0,
+        tiled=True,
+    )
+
     mix_back_low = with_sibling(back_two.astype(BF16))
-    grad_mix_out = matmul_left(mix_low, mix_back_low).astype(BF16)
-    back_mixed = rounded(matmul_right(mix_back_low, mix_w)).reshape(branch.shape)
-    back_state = back_mixed * gated_act
-    gelu_pull = jax.vjp(gelu_tanh, gated_pre)[1]
-    gated_back_low = (
-        gelu_pull(back_mixed * lru_state)[0].astype(BF16).reshape(2 * row_count, lru_width)
-    )
-    coef_next = jnp.concatenate([lru_coef[:, 1:], jnp.ones_like(lru_coef[:, :1])], axis=1)
-    later_prod, local_adjoint = linear_scan(coef_next, back_state, True)
+    back_mixed = matmul_right(mix_back_low, mix_w).astype(BF16).reshape(wide[0].shape)
+    later_prod, local_adjoint, gated_back_low = lru_call(
+        lru_adjoint_kernel,
+        [
+            (branch_gated, "second"),
+            (lru_coef, "first"),
+            (cum_coef, "first"),
+            (local_state, "first"),
+            (start_edge, "edge"),
+            (back_mixed, "first"),
+        ],
+        [wide, wide, wide_low],
+        row_count,
+        scans,
+    )
+    gated_back_low = gated_back_low.reshape(2 * row_count, lru_width)
     carry_in = carried_in(cum_coef[:, -1], lru_coef[:, 0] * local_adjoint[:, 0], True)
-    adjoint = local_adjoint + later_prod * carry_in[:, None]
-    prev_state = jnp.concatenate([start_state[:, None], lru_state[:, :-1]], axis=1)
-    gates_pull = jax.vjp(lru_gates, rate_pre, input_pre, decay_w, conv_out)[1]
-    back_rate, back_input, grad_decay, back_conv_direct = gates_pull(
-        (adjoint * prev_state, adjoint)
-    )
-    rate_back_low = back_rate.astype(BF16).reshape(conv_low.shape)
-    input_back_low = back_input.astype(BF16).reshape(conv_low.shape)
-    grad_rate = through_blocks(conv_low, rate_back_low, "tbi,tbj->bij")
-    grad_input = through_blocks(conv_low, input_back_low, "tbi,tbj->bij")
-    gate_back_conv = through_blocks(rate_back_low, rate_blocks, "tbj,bij->tbi") + through_blocks(
-        input_back_low, input_blocks, "tbj,bij->tbi"
-    )
-    back_conv = back_conv_direct + gate_back_conv.reshape(branch.shape)
-    grad_taps = jnp.stack(
-        [jnp.sum(back_conv * earlier(offset), axis=(0, 1)) for offset in range(tap_count)], axis=1
-    )
-    next_rows = shift_rep(back_conv[:, : tap_count - 1], -1)
-    back_extended = jnp.concatenate([back_conv, next_rows], axis=1)
-    branch_back_low = (
-        sum(
-            conv_w[:, offset] * back_extended[:, offset : offset + row_count]
-            for offset in range(tap_count)
-        )
-        .astype(BF16)
-        .reshape(2 * row_count, lru_width)
-    )
+    carry_edge = jnp.broadcast_to(carry_in[:, None], edge[0].shape)
+    branch_back, first_rows, last_rows, grad_rate, grad_input, grad_taps, grad_decay = lru_call(
+        functools.partial(lru_backward_kernel, block_width),
+        lru_inputs
+        + [
+            (cum_coef, "first"),
+            (local_state, "first"),
+            (start_edge, "edge"),
+            (later_prod, "first"),
+            (local_adjoint, "first"),
+            (carry_edge, "edge"),
+        ],
+        [
+            wide_low,
+            edge,
+            edge,
+            (jax.ShapeDtypeStruct((lru_width, block_width), F32), "weight"),
+            (jax.ShapeDtypeStruct((lru_width, block_width), F32), "weight"),
+            (jax.ShapeDtypeStruct((tap_count, lru_width), F32), "taps"),
+            (jax.ShapeDtypeStruct((1, lru_width), F32), "row"),
+        ],
+        row_count,
+    )
+    spill = jnp.concatenate([jnp.zeros_like(first_rows), shift_rep(first_rows, -1)], axis=1)
+    for j in range(1, tap_count):
+        last_rows = last_rows + conv_w[j] * spill[:, j : j + 8]
+    branch_back_low = lax.dynamic_update_slice_in_dim(
+        branch_back, last_rows.astype(BF16), row_count - 8, 1
+    ).reshape(2 * row_count, lru_width)
     back_mix_normed = sum_parts(
         matmul_right(jnp.concatenate([branch_back_low, gated_back_low], axis=1), lru_in_w)
     )
     back_middle_norm, grad_mix_gain = jax.vjp(rms_norm, middle, gain_mix)[1](back_mix_normed)
-    back_middle = back_two + back_middle_norm
+    back_middle, down_part = lax.optimization_barrier((back_two + back_middle_norm, down_part))
+    down_part = lax.psum_scatter(
+        down_part, "shard", scatter_dimension=0, tiled=True, axis_index_groups=chip_groups()
+    )
     grad_small = jnp.concatenate(
         [
-            grad_rate.reshape(lru_width, block_width).astype(BF16),
-            grad_input.reshape(lru_width, block_width).astype(BF16),
-            grad_taps.astype(BF16),
-            grad_decay[:, None].astype(BF16),
+            grad_rate.astype(BF16),
+            grad_input.astype(BF16),
+            grad_taps.T.astype(BF16),
+            grad_decay.T.astype(BF16),
             jnp.zeros((lru_width, spare), BF16),
         ],
         axis=1,
@@ -1164,41 +1435,31 @@
         resid_one, gain_first, first_in_w, first_down_w, first_kept, back_middle
     )
 
-    attn_back_low = back_one.astype(BF16)
+    attn_back_low, in_part = lax.optimization_barrier((back_one.astype(BF16), in_part))
+    in_part = lax.psum_scatter(
+        in_part, "shard", scatter_dimension=0, tiled=True, axis_index_groups=chip_groups()
+    )
     back_halves = attn_back_low[:, : width // 2], attn_back_low[:, width // 2 :]
     back_mine, back_other = by_core(*back_halves), by_core(back_halves[1], back_halves[0])
     attended_both = with_sibling(attended_low)
     out_right = jnp.concatenate([back_mine, swap_cores(back_other)], axis=0)
     back_attended = matmul_right(back_mine, attn_own) + matmul_right(back_other, attn_sib)
-    back_attended = (
-        unordered(back_attended.astype(BF16))
-        .astype(BF16)
-        .reshape(row_count, head_count, head_size)
-    )
-    attn_probs = jnp.exp(window_scores(query_heads, key_win, start_row, behind) - log_total)
-    probs_again = attn_probs.astype(BF16)
-    back_probs = jnp.einsum("thd,kd->htk", back_attended, value_win, preferred_element_type=F32)
-    prob_dot = jnp.sum(attn_probs * back_probs, axis=-1, keepdims=True)
-    scores_back_low = (attn_probs * (back_probs - prob_dot)).astype(BF16)
-    score_scale = 1.0 / math.sqrt(head_size)
-    back_query = (
-        jnp.einsum("htk,kd->thd", scores_back_low, key_win, preferred_element_type=F32)
-        * score_scale
-    )
-    back_key_win = (
-        jnp.einsum("htk,thd->kd", scores_back_low, query_heads, preferred_element_type=F32)
-        * score_scale
-    )
-    back_value_win = jnp.einsum(
-        "htk,thd->kd", probs_again, back_attended, preferred_element_type=F32
-    )
-    back_kv_win = jnp.concatenate([back_key_win, back_value_win], axis=1)
+    back_attended = unordered(back_attended.astype(BF16)).astype(BF16)
+    back_query, back_kv_win = attention_call(
+        attention_back_kernel,
+        start_row,
+        [query_rows, back_attended],
+        kv_win,
+        [
+            jax.ShapeDtypeStruct((row_count, width), BF16),
+            jax.ShapeDtypeStruct(kv_win.shape, F32),
+        ],
+    )
     back_kv = back_kv_win[behind:]
     for by in range(1, behind // row_count + 1):
         begin = behind - by * row_count
         back_kv = back_kv + shift_rep(back_kv_win[begin : begin + row_count], -by)
     back_kv = back_kv.astype(BF16)
-    back_query = back_query.reshape(row_count, width).astype(BF16)
     back_first = jnp.concatenate([back_query[:, :half], back_kv[:, :head_size]], axis=1)
     back_second = jnp.concatenate([back_query[:, half:], back_kv[:, head_size:]], axis=1)
     qkv_back_mine = by_core(back_first, back_second)
@@ -1211,48 +1472,57 @@
         .reshape(1, row_count, width)
     )
 
-    mix_reduced = reduce_chips([grad_small, grad_mix_out])
-    grad_mixer_out = unordered(mix_reduced[:, 3 * block_width :])
-    small = mix_reduced[:, : 3 * block_width].astype(F32)
-
     gain_given = jnp.stack([grad_attn_gain, first_grads[0], grad_mix_gain, second_grads[0]])
     gain_given = jnp.pad(gain_given, ((0, 124), (0, 0))).astype(BF16).T.reshape(reps, -1, 128)
     qkv_right = jnp.concatenate([qkv_back_mine, swap_cores(qkv_back_other)], axis=0)
-    second_in, second_down_rows, lru_in, first_in, first_down_rows, qkv_rows, out_rows, gain_rows = (
+    second_in = lax.all_gather(in_part, "rep", axis=0, tiled=True)
+    second_down_rows = lax.all_gather(down_part, "rep", axis=0, tiled=True)
+    second_in, second_down_rows, gain_given = lax.optimization_barrier(
+        (second_in, second_down_rows, gain_given)
+    )
+
+    def by_reps(x):
+        parts = x.reshape(chips, reps, -1, x.shape[1]).transpose(1, 0, 2, 3)
+        return parts.reshape(reps, -1, x.shape[1])
+
+    lru_in, first_in, first_down_rows, qkv_rows, out_rows, gain_rows, mix_rows, small_rows = (
         reduce_all(
             [
-                (second_grads[1][0], [second_grads[1][1], second_grads[2][1]], 768),
-                (second_grads[3][0], [second_grads[3][1]], 512),
                 (mix_normed, [branch_back_low, gated_back_low], 512),
                 (first_grads[1][0], [first_grads[1][1], first_grads[2][1]], 768),
                 (first_grads[3][0], [first_grads[3][1]], 512),
                 (with_sibling(attn_normed), [qkv_right], 512),
                 (with_sibling(attended_low), [out_right], 768),
                 (None, [gain_given], 128),
+                (by_reps(mix_low.T).reshape(lru_width, -1).T, [mix_back_low], 768),
+                (None, [by_reps(grad_small)], 384),
             ]
         )
     )
 
-    def in_reduced(reduced, unit, parts):
-        rows = own_rows(reduced)
-        middle = rows[0].shape[1] // 2
-        return tuple(
-            joined_columns(*(half[:, columns] for half in rows), unit, parts).astype(F32)
-            for columns in (slice(0, middle), slice(middle, None))
-        )
+    grad_mixer_out = unordered(mix_rows)
+    small = small_rows.astype(F32)
+
+    def in_reduced(reduced, unit, parts=1):
+        return join_columns(*own_rows(reduced), 2, unit, parts)
 
     grad_second_gate, grad_second_up = in_reduced(second_in, ff_unit, reps)
     grad_second_down = unordered(second_down_rows)
-    grad_branch_proj, grad_gated_proj = in_reduced(lru_in, lru_unit, 1)
+    grad_branch_proj, grad_gated_proj = in_reduced(lru_in, lru_unit)
     grad_first_gate, grad_first_up = in_reduced(first_in, ff_unit, reps)
     grad_first_down = unordered(first_down_rows)
-    qkv_first, qkv_second = own_rows(qkv_rows)
-    grad_query = jnp.concatenate([qkv_first[:, :half], qkv_second[:, :half]], axis=1).astype(F32)
-    grad_key = qkv_first[:, half:].astype(F32)
-    grad_value = qkv_second[:, half:].astype(F32)
-    grad_out_proj = unordered(jnp.concatenate(own_rows(out_rows), axis=1))
-    gain_first_, gain_second_ = own_rows(gain_rows)
-    gain_grads = (gain_first_.astype(F32) + gain_second_.astype(F32)).T
+    qkv_mine, qkv_other = own_rows(qkv_rows)
+    grad_query = jnp.concatenate(
+        [by_core(qkv_mine, qkv_other)[:, :half], by_core(qkv_other, qkv_mine)[:, :half]], axis=1
+    ).astype(F32)
+    grad_key = by_core(qkv_mine, qkv_other)[:, half:].astype(F32)
+    grad_value = by_core(qkv_other, qkv_mine)[:, half:].astype(F32)
+    out_mine, out_other = own_rows(out_rows)
+    grad_out_proj = unordered(
+        jnp.concatenate([by_core(out_mine, out_other), by_core(out_other, out_mine)], axis=1)
+    )
+    gain_mine, gain_other = own_rows(gain_rows)
+    gain_grads = (gain_mine.astype(F32) + gain_other.astype(F32)).T
     return (
         out_tokens,
         input_grad,

time: 1960 us -> 1530 us (0.78)
  Pallas kernels: 1000 us -> 852 us
  local copies, waits for them, and re-layouts: 227 us -> 91.3 us
  other arithmetic: 224 us -> 89.7 us
  matrix products: 362 us -> 307 us
  waiting for transfers between devices: 91.6 us -> 126 us
    pallas_call x1, Pallas kernels: 624 us -> 427 us  [reduce_all(): pl.pallas_call(functools.partial(reduce_kernel, chunks, (len(lefts), len(...]
    pallas_call x2 -> x11, Pallas kernels: 18.9 us -> 155 us  [the longest x2 68.4 us: attention_call(): pl.pallas_call(kernel, grid_spec=pltpu.PrefetchScalarGridSpec(num_scalar_...]
    dot_general x12 -> x0, matrix products: 102 us -> none  [the longest x1 28.2 us: on_device(): jnp.einsum('thd,kd->htk', back_attended, value_win, preferred_element_typ...]
    pallas_call x1, Pallas kernels: 359 us -> 271 us  [gather_all(): pl.pallas_call(functools.partial(gather_kernel, chunks, len(arrays), chip...]
    convert_element_type x22 -> x11, other arithmetic: 77.8 us -> 16.9 us  [the longest x1 6.17 us: on_device(): ((local_state + cum_coef * start_state[:, None]) * gated_act).astype(BF16)]
    ppermute x7 -> x0, waiting for transfers between devices: 52.8 us -> none  [the longest x3 41.3 us: shift_chip(): lax.ppermute(x, 'shard', [(i, (i + 2 * by) % count) for i in range(count)])]
    concatenate x14 -> x5, local copies, waits for them, and re-layouts: 46.3 us -> 1.58 us  [on_device(): jnp.concatenate([grad_rate.astype(BF16), grad_input.astype(BF16), grad_ta...]
    reduce_scatter x0 -> x4, waiting for transfers between devices: none -> 43 us  [the longest x1 24.4 us: on_device(): lax.psum_scatter(in_part, 'shard', scatter_dimension=0, tiled=True, axis_...]
  transfers between devices with their start and end apart: 47 -> 48, of which waited for: 14 -> 23; matrix products, arithmetic and copies ran while one was open for 23% -> 28% of each run, Pallas kernels for 1% -> 9%
where the time goes in v2:
time: 1530 us; the launch traced here: 1520 us
  Pallas kernels  852 us (56%)
  matrix products  307 us (20%)
  waiting for transfers between devices  126 us (8%)
  local copies, waits for them, and re-layouts  91.3 us (6%)
  other arithmetic  89.7 us (6%)
  starting transfers between devices  32.6 us (2%)
  between operations  18.4 us (1%)
    pallas_call x1, Pallas kernels, reduce_all(): pl.pallas_call(functools.partial(reduce_kernel, chunks, (len(lefts), len(...  427 us
    pallas_call x1, Pallas kernels, gather_all(): pl.pallas_call(functools.partial(gather_kernel, chunks, len(arrays), chip...  271 us
    dot_general x16, matrix products, matmul_right(): lax.dot_general(first_op, second_op, (((1,), (1,)), ((), ())), preferred_...  151 us
    dot_general x17, matrix products, matmul(): return jnp.dot(first_op, second_op, preferred_element_type=F32)  122 us
    pallas_call x2, Pallas kernels, attention_call(): pl.pallas_call(kernel, grid_spec=pltpu.PrefetchScalarGridSpec(num_scalar_...  68.4 us
    pallas_call x3, Pallas kernels, lru_call(): pl.pallas_call(kernel, grid=(width // lanes, 2), in_specs=[spec(kind) for...  56.4 us
    ppermute x12, waiting for transfers between devices, shift_rep(): lax.ppermute(x, 'rep', [(i, i + by) for i in range(size) if 0 <= i + by <...  43.2 us
    ppermute x28, waiting for transfers between devices, swap_cores(): return lax.ppermute(x, 'shard', [(i, i ^ 1) for i in range(count)])  38.8 us
  transfers between devices with their start and end apart: 48, of which 23 were waited for; matrix products, arithmetic and copies ran while one was open for 28% of the time, Pallas kernels for 9%

profile of v2, /device:TPU:0, one launch (start us, length us, event | category | flops | bytes accessed | tf_op | source)
XLA Modules:
  0.0 1516.4 jit_solution(15965560769774330306)
XLA Ops:
  52.0 270.6 %shard_map.410 = (bf16[1536,1792]{1,0:T(8,128)(2,1)}, bf16[1536,4608]{1,0:T(8,128)(2,1)}, bf16[2304,1536]{1,0:T(8,128)(2,1)}, bf16[1536,2048]{1,0:T(8,128)(2,1)}...) custom-call(bf16[384,1792]{1,0:T(8,128)(2,1)S(1)} %pad_maximum_fusion.21.refs_0_, ...), custom_call_target="tpu_custom_call" | custom-call | bytes 385351680 | tf_op jit(solution)/shard_map/pallas_call | solution.py:415
  353.9 6.6 collective-permute-done.5
  361.4 23.8 %shard_map.411 = bf16[512,1536]{1,0:T(8,128)(2,1)} custom-call(s32[1]{0:T(128)} %bitcast.2.start_ref, bf16[512,1536]{1,0:T(8,128)(2,1)} %pad_maximum_fusion.19.query_ref, bf16[1536,256]{1,0:T(8,128)(2,1)} %maximum_maximum_fusion.kv_ref), custom_call_target="tpu_custom_call" | custom-call | flops 9663676416 | bytes 67108864 | tf_op jit(solution)/shard_map/pallas_call | solution.py:1124
  404.6 18.4 %fusion.128 = f32[1024,4608]{1,0:T(8,128)S(1)} fusion(bf16[1536,4608]{1,0:T(8,128)(2,1)} %get-tuple-element.83, bf16[512,1536]{1,0:T(8,128)(2,1)} %copy-done.49, bf16[512,1536]{1,0:T(8,128)(2,1)S(1)} %multiply_convert_fusion.4), kind=kOutput, calls=%fused_computation.298 | convolution fusion | flops 14501806080 | bytes 36175872 | tf_op jit(solution)/shard_map/dot_general | solution.py:33
  423.0 18.4 %fusion.144 = f32[1024,1536]{1,0:T(8,128)} fusion(bf16[2304,1536]{1,0:T(8,128)(2,1)} %get-tuple-element.84, f32[1024,4608]{1,0:T(8,128)S(1)} %fusion.128), kind=kOutput, calls=%fused_computation.310 | convolution fusion | flops 7271350272 | bytes 32243712 | tf_op jit(solution)/shard_map/dot_general | solution.py:33
  454.2 6.7 copy.88
  464.2 9.3 fusion.127
  482.8 18.9 %shard_map.412 = (f32[2,512,1024]{2,1,0:T(8,128)}, f32[2,512,1024]{2,1,0:T(8,128)}, f32[2,512,1024]{2,1,0:T(8,128)}) custom-call(f32[2,512,2048]{2,1,0:T(8,128)} %bitcast.166, f32[2,8,1024]{2,1,0:T(8,128)} %copy-done.62, bf16[1024,128]{1,0:T(8,128)(2,1)} %get-tuple-element.226.rate_ref, bf16[1024,128]{1,0:T(8,128)(2,1)} %get-tuple-element.225.input_ref, ...), custom_call_target="tpu_custom_call" | custom-call | bytes 33554432 | tf_op jit(solution)/shard_map/pallas_call | solution.py:1031
  510.5 6.4 collective-permute-start.12
  547.5 20.2 %fusion.60 = f32[1024,4608]{1,0:T(8,128)} fusion(bf16[1536,4608]{1,0:T(8,128)(2,1)} %all-gather.7.cloned.1.call-done, bf16[512,1536]{1,0:T(8,128)(2,1)S(1)} %collective-permute-done.16, bf16[512,1536]{1,0:T(8,128)(2,1)S(1)} %multiply_convert_fusion.2), kind=kOutput, calls=%fused_computation.133 | convolution fusion | flops 14501806080 | bytes 36175872 | tf_op jit(solution)/shard_map/dot_general | solution.py:33
  567.7 23.1 %fusion.15 = (bf16[1024,2304]{1,0:T(8,128)(2,1)}, bf16[1024,2304]{1,0:T(8,128)(2,1)}, bf16[1024,2304]{1,0:T(8,128)(2,1)}) fusion(f32[1024,4608]{1,0:T(8,128)} %fusion.60, bf16[2304,1536]{1,0:T(8,128)(2,1)} %get-tuple-element.90, bf16[512,1536]{1,0:T(8,128)(2,1)} %collective-permute-done.18, bf16[512,1536]{1,0:T(8,128)(2,1)} %get-tuple-element.272), kind=kOutput, calls=%fused_computation.29 | convolution fusion | flops 7320109056 | bytes 43253760 | tf_op jit(solution)/shard_map/dot_general | solution.py:43
  590.8 12.5 convolution_convert_fusion.1
  603.4 21.3 %convolution_convert_fusion = bf16[1536,4608]{1,0:T(8,128)(2,1)} fusion(bf16[1024,2304]{1,0:T(8,128)(2,1)} %get-tuple-element.223, bf16[1024,2304]{1,0:T(8,128)(2,1)} %get-tuple-element.222, bf16[512,1536]{1,0:T(8,128)(2,1)S(1)} %collective-permute-done.16, bf16[512,1536]{1,0:T(8,128)(2,1)S(1)} %multiply_convert_fusion.2), kind=kOutput, calls=%fused_computation | convolution fusion | flops 14527758336 | bytes 26738688 | tf_op jit(solution)/shard_map/dot_general | solution.py:37
  624.7 19.7 %fusion.25 = f32[1024,1536]{1,0:T(8,128)S(1)} fusion(bf16[1536,4608]{1,0:T(8,128)(2,1)} %all-gather.7.cloned.1.call-done, bf16[1024,2304]{1,0:T(8,128)(2,1)} %get-tuple-element.223, bf16[1024,2304]{1,0:T(8,128)(2,1)} %get-tuple-element.222), kind=kOutput, calls=%fused_computation.45 | convolution fusion | flops 14514388992 | bytes 29884416 | tf_op jit(solution)/shard_map/dot_general | solution.py:43
  665.8 16.3 %shard_map.413 = (f32[2,512,1024]{2,1,0:T(8,128)}, f32[2,512,1024]{2,1,0:T(8,128)}, bf16[2,512,1024]{2,1,0:T(8,128)(2,1)}) custom-call(f32[2,512,2048]{2,1,0:T(8,128)} %bitcast.168, f32[2,512,1024]{2,1,0:T(8,128)} %get-tuple-element.91.coef_ref, f32[2,512,1024]{2,1,0:T(8,128)} %get-tuple-element.88.cum_ref, f32[2,512,1024]{2,1,0:T(8,128)} %get-tuple-element.87.local_ref, ...), custom_call_target="tpu_custom_call" | custom-call | bytes 33554432 | tf_op jit(solution)/shard_map/pallas_call | solution.py:1031
  692.1 21.2 %shard_map.414 = (bf16[2,512,1024]{2,1,0:T(8,128)(2,1)}, f32[2,8,1024]{2,1,0:T(8,128)}, f32[2,8,1024]{2,1,0:T(8,128)}, f32[1024,128]{1,0:T(8,128)}, f32[1024,128...) custom-call(f32[2,512,2048]{2,1,0:T(8,128)} %bitcast.169, f32[2,8,1024]{2,1,0:T(8,128)} %copy-done.62, ...), custom_call_target="tpu_custom_call" | custom-call | bytes 33554432 | tf_op jit(solution)/shard_map/pallas_call | solution.py:1031
  714.6 7.3 collective-permute-done.24
  723.5 9.6 fusion.35
  748.3 20.5 %fusion.8 = (bf16[1024,2304]{1,0:T(8,128)(2,1)}, bf16[1024,2304]{1,0:T(8,128)(2,1)}) fusion(f32[1024,4608]{1,0:T(8,128)} %copy-done.16, bf16[2304,1536]{1,0:T(8,128)(2,1)} %get-tuple-element.84, bf16[512,1536]{1,0:T(8,128)(2,1)S(1)} %collective-permute-done.26, bf16[512,1536]{1,0:T(8,128)(2,1)S(1)} %convert_element_type.229), kind=kOutput, calls=%fused_computation.22 | convolution fusion | flops 7315390464 | bytes 38535168 | tf_op jit(solution)/shard_map/dot_general | solution.py:43
  768.7 19.3 %fusion.21 = f32[1024,1536]{1,0:T(8,128)S(1)} fusion(bf16[1536,4608]{1,0:T(8,128)(2,1)} %get-tuple-element.83, bf16[1024,2304]{1,0:T(8,128)(2,1)} %get-tuple-element.221.refs_9_, bf16[1024,2304]{1,0:T(8,128)(2,1)} %get-tuple-element.220.refs_8_), kind=kOutput, calls=%fused_computation.36 | convolution fusion | flops 14514388992 | bytes 29884416 | tf_op jit(solution)/shard_map/dot_general | solution.py:43
  808.2 9.2 reduce-scatter.7.cloned.1.call-done
  817.5 11.1 fusion.145
  838.1 10.4 fusion.197
  848.5 9.4 reduce-scatter.11.cloned.1.call-done
  861.4 7.1 copy.94
  882.9 8.4 fusion.56
  901.4 24.4 %reduce-scatter.9.cloned.1.call-done = bf16[96,4608]{1,0:T(8,128)(2,1)} async-done(((bf16[384,4608]{1,0:T(8,128)(2,1)}), bf16[96,4608]{1,0:T(8,128)(2,1)}) %reduce-scatter.9.cloned.1.call-update) | async-done | bytes 884752 | tf_op jit(solution)/shard_map/reduce_scatter | solution.py:1439
  925.8 8.5 convolution_convert_fusion.7.back_ref
  934.3 44.6 %shard_map.415 = (bf16[512,1536]{1,0:T(8,128)(2,1)}, f32[1536,256]{1,0:T(8,128)}) custom-call(s32[1]{0:T(128)} %bitcast.2.start_ref, bf16[512,1536]{1,0:T(8,128)(2,1)} %pad_maximum_fusion.19.query_ref, bf16[512,1536]{1,0:T(8,128)(2,1)} %convolution_convert_fusion.7.back_ref, bf16[1536,256]{1,0:T(8,128)(2,1)} %maximum_maximum_fusion.kv_ref), custom_call_target="tpu_custom_call" | custom-call | flops 9663676416 | bytes 67108864 | tf_op jit(solution)/shard_map/pallas_call | solution.py:1124
  985.1 16.9 %collective-permute-done.28 = f32[512,256]{1,0:T(8,128)S(1)} collective-permute-done((f32[512,256]{1,0:T(8,128)S(1)}, f32[512,256]{1,0:T(8,128)S(1)}, u32[]{:S(2)}, u32[]{:S(2)}) %collective-permute-start.28) | collective-permute-done | bytes 524320 | tf_op jit(solution)/shard_map/ppermute | solution.py:67
  1017.0 8.5 fusion.57
  1029.3 426.7 %shard_map.416 = (bf16[384,2048]{1,0:T(8,128)(2,1)}, bf16[384,4608]{1,0:T(8,128)(2,1)}, bf16[576,1536]{1,0:T(8,128)(2,1)}, bf16[384,896]{1,0:T(8,128)(2,1)}, bf1...) custom-call(bf16[1024,1536]{1,0:T(8,128)(2,1)} %pad_maximum_fusion.6, ...), custom_call_target="tpu_custom_call" | custom-call | bytes 591396864 | tf_op jit(solution)/shard_map/pallas_call | solution.py:782
  (476 shorter events, 342.7 us)
Async XLA Ops:
  7.2 393.3 %all-gather.5.cloned.1.call-start = ((), (), s32[]{:S(2)}) async-start(), calls=%async_computation.4 | async-start | bytes 4423680 | tf_op jit(solution)/shard_map/all_gather | solution.py:392
  12.6 33.0 %collective-permute-start = (bf16[192,4608]{1,0:T(8,128)(2,1)}, bf16[192,4608]{1,0:T(8,128)(2,1)}, u32[]{:S(2)}, u32[]{:S(2)}) collective-permute-start(bf16[192,4608]{1,0:T(8,128)(2,1)} %get-tuple-element.75), channel_id=1, source_target_pairs={{0,1},{1,0},{2,3},{3,2},{4,5},{5,4},{6,7},{7,6},{8,9},{9,8},{10,11... | collective-permute-start | bytes 5308424 | tf_op jit(solution)/shard_map/ppermute | solution.py:62
  18.2 31.5 %collective-permute-start.2 = (bf16[192,4608]{1,0:T(8,128)(2,1)}, bf16[192,4608]{1,0:T(8,128)(2,1)S(1)}, u32[]{:S(2)}, u32[]{:S(2)}) collective-permute-start(bf16[192,4608]{1,0:T(8,128)(2,1)} %get-tuple-element.79), channel_id=1, source_target_pairs={{0,1},{1,0},{2,3},{3,2},{4,5},{5,4},{6,7},{7,6},{8,9},{9,8},{10,11... | collective-permute-start | bytes 5308424 | tf_op jit(solution)/shard_map/ppermute | solution.py:62
  21.9 22.2 %collective-permute-start.3 = (bf16[192,2048]{1,0:T(8,128)(2,1)}, bf16[192,2048]{1,0:T(8,128)(2,1)}, u32[]{:S(2)}, u32[]{:S(2)}) collective-permute-start(bf16[192,2048]{1,0:T(8,128)(2,1)} %get-tuple-element.81), channel_id=1, source_target_pairs={{0,1},{1,0},{2,3},{3,2},{4,5},{5,4},{6,7},{7,6},{8,9},{9,8},{10,11... | collective-permute-start | bytes 2359304 | tf_op jit(solution)/shard_map/ppermute | solution.py:62
  326.4 16.7 %collective-permute-start.4 = (bf16[1536,896]{1,0:T(8,128)(2,1)}, bf16[1536,896]{1,0:T(8,128)(2,1)}, u32[]{:S(2)}, u32[]{:S(2)}) collective-permute-start(bf16[1536,896]{1,0:T(8,128)(2,1)} %slice.249), channel_id=1, source_target_pairs={{0,1},{1,0},{2,3},{3,2},{4,5},{5,4},{6,7},{7,6},{8,9},{9,8},{10,11... | collective-permute-start | bytes 8257544 | tf_op jit(solution)/shard_map/ppermute | solution.py:62
  332.9 214.6 %all-gather.7.cloned.1.call-start = ((), (), s32[]{:S(2)}) async-start(), calls=%async_computation.5 | async-start | bytes 17694720 | tf_op jit(solution)/shard_map/all_gather | solution.py:393
  336.2 57.7 %collective-permute-start.7 = (bf16[1536,768]{1,0:T(8,128)(2,1)}, bf16[1536,768]{1,0:T(8,128)(2,1)}, u32[]{:S(2)}, u32[]{:S(2)}) collective-permute-start(bf16[1536,768]{1,0:T(8,128)(2,1)} %slice.254), channel_id=1, source_target_pairs={{0,1},{1,0},{2,3},{3,2},{4,5},{5,4},{6,7},{7,6},{8,9},{9,8},{10,11... | collective-permute-start | bytes 7077896 | tf_op jit(solution)/shard_map/ppermute | solution.py:62
  346.7 13.7 collective-permute-start.5
  349.1 11.4 collective-permute-start.6
  400.5 342.2 %reduce-scatter.5.cloned.1.call-start = ((), (), s32[]{:S(2)}) async-start(), calls=%async_computation.6 | async-start | bytes 8847360 | tf_op jit(solution)/shard_map/reduce_scatter | solution.py:1355
  454.0 10.2 collective-permute-start.10
  510.5 11.6 collective-permute-start.12
  540.2 7.3 collective-permute-start.16
  547.4 20.3 %collective-permute-start.18 = (bf16[512,1536]{1,0:T(8,128)(2,1)}, bf16[512,1536]{1,0:T(8,128)(2,1)}, u32[]{:S(2)}, u32[]{:S(2)}) collective-permute-start(bf16[512,1536]{1,0:T(8,128)(2,1)} %get-tuple-element.272), channel_id=1, source_target_pairs={{0,1},{1,0},{2,3},{3,2},{4,5},{5,4},{6,7},{7,6},{8,9},{9,8},{10,11... | collective-permute-start | bytes 4718600 | tf_op jit(solution)/shard_map/ppermute | solution.py:62
  603.3 214.0 %reduce-scatter.7.cloned.1.call-start = ((), (), s32[]{:S(2)}) async-start(), calls=%async_computation.7 | async-start | bytes 17694720 | tf_op jit(solution)/shard_map/reduce_scatter | solution.py:1358
  624.7 233.3 %reduce-scatter.11.cloned.1.call-start = ((), (), s32[]{:S(2)}) async-start(), calls=%async_computation.10 | async-start | bytes 2211840 | tf_op jit(solution)/shard_map/reduce_scatter | solution.py:1420
  713.3 8.7 collective-permute-start.24
  791.6 134.1 %reduce-scatter.9.cloned.1.call-start = ((), (), s32[]{:S(2)}) async-start(), calls=%async_computation.8 | async-start | bytes 4423680 | tf_op jit(solution)/shard_map/reduce_scatter | solution.py:1439
  817.4 211.8 %all-gather.11.cloned.1.call-start = ((), (), s32[]{:S(2)}) async-start(), calls=%async_computation.11 | async-start | bytes 2211840 | tf_op jit(solution)/shard_map/all_gather | solution.py:1479
  817.5 15.3 %collective-permute-start.30 = (bf16[512,1536]{1,0:T(8,128)(2,1)S(1)}, bf16[512,1536]{1,0:T(8,128)(2,1)}, u32[]{:S(2)}, u32[]{:S(2)}) collective-permute-start(bf16[512,1536]{1,0:T(8,128)(2,1)S(1)} %copy-done.23), channel_id=1, source_target_pairs={{0,1},{1,0},{2,3},{3,2},{4,5},{5,4},{6,7},{7,6},{8,9},{9,8},{10,11... | collective-permute-start | bytes 4718600 | tf_op jit(solution)/shard_map/ppermute | solution.py:62
  832.3 50.6 %collective-permute-start.17 = (f32[512,1536]{1,0:T(8,128)}, f32[512,1536]{1,0:T(8,128)}, u32[]{:S(2)}, u32[]{:S(2)}) collective-permute-start(f32[512,1536]{1,0:T(8,128)} %slice.351), channel_id=1, source_target_pairs={{0,1},{1,0},{2,3},{3,2},{4,5},{5,4},{6,7},{7,6},{8,9},{9,8},{10,11... | collective-permute-start | bytes 9437192 | tf_op jit(solution)/shard_map/ppermute | solution.py:62
  836.1 21.9 %collective-permute-start.31 = (bf16[512,1536]{1,0:T(8,128)(2,1)}, bf16[512,1536]{1,0:T(8,128)(2,1)S(1)}, u32[]{:S(2)}, u32[]{:S(2)}) collective-permute-start(bf16[512,1536]{1,0:T(8,128)(2,1)} %convolution_convert_fusion.9), channel_id=1, source_target_pairs={{0,1},{1,0},{2,3},{3,2},{4,5},{5,4},{6,7},{7,6},{8,9},{9,8},{10,11... | collective-permute-start | bytes 4718600 | tf_op jit(solution)/shard_map/ppermute | solution.py:62
  858.0 171.3 %all-gather.9.cloned.1.call-start = ((), (), s32[]{:S(2)}) async-start(), calls=%async_computation.9 | async-start | bytes 4423680 | tf_op jit(solution)/shard_map/all_gather | solution.py:1478
  980.3 21.6 %collective-permute-start.28 = (f32[512,256]{1,0:T(8,128)S(1)}, f32[512,256]{1,0:T(8,128)S(1)}, u32[]{:S(2)}, u32[]{:S(2)}) collective-permute-start(f32[512,256]{1,0:T(8,128)S(1)} %get-tuple-element.247), channel_id=1, source_target_pairs={{8,0},{16,8},{24,16},{9,1},{17,9},{25,17},{10,2},{18,10},{26,18},{... | collective-permute-start | bytes 1572872 | tf_op jit(solution)/shard_map/ppermute | solution.py:67
  981.6 25.0 %collective-permute-start.29 = (f32[512,256]{1,0:T(8,128)S(1)}, f32[512,256]{1,0:T(8,128)S(1)}, u32[]{:S(2)}, u32[]{:S(2)}) collective-permute-start(f32[512,256]{1,0:T(8,128)S(1)} %get-tuple-element.248), channel_id=1, source_target_pairs={{16,0},{24,8},{17,1},{25,9},{18,2},{26,10},{19,3},{27,11},{20,4},{... | collective-permute-start | bytes 1572872 | tf_op jit(solution)/shard_map/ppermute | solution.py:67
  985.0 40.5 %collective-permute-start.33 = (bf16[512,768]{1,0:T(8,128)(2,1)}, bf16[512,768]{1,0:T(8,128)(2,1)S(1)}, u32[]{:S(2)}, u32[]{:S(2)}) collective-permute-start(bf16[512,768]{1,0:T(8,128)(2,1)} %get-tuple-element.249), channel_id=1, source_target_pairs={{0,1},{1,0},{2,3},{3,2},{4,5},{5,4},{6,7},{7,6},{8,9},{9,8},{10,11... | collective-permute-start | bytes 2359304 | tf_op jit(solution)/shard_map/ppermute | solution.py:62
  1008.2 18.5 %collective-permute-start.32 = (bf16[512,896]{1,0:T(8,128)(2,1)S(1)}, bf16[512,896]{1,0:T(8,128)(2,1)}, u32[]{:S(2)}, u32[]{:S(2)}) collective-permute-start(bf16[512,896]{1,0:T(8,128)(2,1)S(1)} %get-tuple-element.239), channel_id=1, source_target_pairs={{0,1},{1,0},{2,3},{3,2},{4,5},{5,4},{6,7},{7,6},{8,9},{9,8},{10,11... | collective-permute-start | bytes 2752520 | tf_op jit(solution)/shard_map/ppermute | solution.py:62
  1462.7 33.3 %collective-permute-start.39 = (bf16[192,4608]{1,0:T(8,128)(2,1)}, bf16[192,4608]{1,0:T(8,128)(2,1)S(1)}, u32[]{:S(2)}, u32[]{:S(2)}) collective-permute-start(bf16[192,4608]{1,0:T(8,128)(2,1)} %get-tuple-element.227), channel_id=1, source_target_pairs={{0,1},{1,0},{2,3},{3,2},{4,5},{5,4},{6,7},{7,6},{8,9},{9,8},{10,11... | collective-permute-start | bytes 5308424 | tf_op jit(solution)/shard_map/ppermute | solution.py:62
  1464.0 28.0 %collective-permute-start.38 = (bf16[192,2048]{1,0:T(8,128)(2,1)}, bf16[192,2048]{1,0:T(8,128)(2,1)}, u32[]{:S(2)}, u32[]{:S(2)}) collective-permute-start(bf16[192,2048]{1,0:T(8,128)(2,1)} %get-tuple-element.243), channel_id=1, source_target_pairs={{0,1},{1,0},{2,3},{3,2},{4,5},{5,4},{6,7},{7,6},{8,9},{9,8},{10,11... | collective-permute-start | bytes 2359304 | tf_op jit(solution)/shard_map/ppermute | solution.py:62
  1466.6 36.6 %collective-permute-start.37 = (bf16[192,4608]{1,0:T(8,128)(2,1)}, bf16[192,4608]{1,0:T(8,128)(2,1)}, u32[]{:S(2)}, u32[]{:S(2)}) collective-permute-start(bf16[192,4608]{1,0:T(8,128)(2,1)} %get-tuple-element.229), channel_id=1, source_target_pairs={{0,1},{1,0},{2,3},{3,2},{4,5},{5,4},{6,7},{7,6},{8,9},{9,8},{10,11... | collective-permute-start | bytes 5308424 | tf_op jit(solution)/shard_map/ppermute | solution.py:62
  1473.5 10.4 collective-permute-start.36
  1476.1 6.7 collective-permute-start.34
  (120 other events, 1007.9 us)
Sparse Core Ops, SparseCore 0:
  333.0 67.3 all-gather.4
  402.3 135.9 all-gather.6
  603.5 75.9 reduce-scatter.4
  682.5 134.8 reduce-scatter.6
  819.6 38.3 reduce-scatter.10
  860.2 65.4 reduce-scatter.8
  927.7 32.8 all-gather.10
  962.6 54.6 all-gather.8

commit v3 on v2

--- a/solution.py
+++ b/solution.py
@@ -489,7 +489,7 @@
         k = chunks[c]
         return pltpu.make_async_copy(
             rights[k["right"]].at[:, pl.ds(k["first"], k["wide"])],
-            right_buf.at[c % 6, :, pl.ds(0, k["wide"])],
+            right_buf.at[c % 8, :, pl.ds(0, k["wide"])],
             local.at[c, 0],
         )
 
@@ -500,7 +500,7 @@
         k, rows = chunks[c], rows_of(c)
         source, target = ((first_out, first_in), (second_out, second_in))[turn]
         return pltpu.make_async_remote_copy(
-            src_ref=source.at[c % 3, :, pl.ds(0, rows), pl.ds(0, k["wide"])],
+            src_ref=source.at[c % 4, :, pl.ds(0, rows), pl.ds(0, k["wide"])],
             dst_ref=target[c],
             send_sem=send.at[c, turn],
             recv_sem=recv.at[c, turn],
@@ -511,7 +511,7 @@
     def arrived_copy(c, turn):
         k, rows = chunks[c], rows_of(c)
         source = (first_in, second_in)[turn][c]
-        target = (first_loc.at[c % 4], second_loc.at[c % 2])[turn]
+        target = (first_loc.at[c % 5], second_loc.at[c % 2])[turn]
         return pltpu.make_async_copy(
             source, target.at[:, pl.ds(0, rows), pl.ds(0, k["wide"])], local.at[c, 2 + turn]
         )
@@ -534,7 +534,7 @@
             if k["given"] is not None:
                 total = givens[k["given"]][at, :, columns].astype(F32)
             else:
-                right = right_buf[c % 6, :, columns]
+                right = right_buf[c % 8, :, columns]
                 if k["big"]:
                     total = jnp.dot(big_left[at], right, preferred_element_type=F32)
                 else:
@@ -558,8 +558,8 @@
             if chunks[c]["load"]:
                 left_copy(c).wait()
         one, two = masks(c)
-        product(c, one, (first_out, (c % 3, 0)), [])
-        product(c, one ^ two, (first_out, (c % 3, 1)), [])
+        product(c, one, (first_out, (c % 4, 0)), [])
+        product(c, one ^ two, (first_out, (c % 4, 1)), [])
         exchange(c, 0).start()
 
     def take_first(c):
@@ -568,7 +568,7 @@
 
     def send_second(c):
         arrived_copy(c, 0).wait()
-        product(c, masks(c)[1], (second_out, (c % 3, 0)), [(first_loc, (c % 4, 1))])
+        product(c, masks(c)[1], (second_out, (c % 4, 0)), [(first_loc, (c % 5, 1))])
         exchange(c, 1).start()
         exchange(c, 0).wait_send()
 
@@ -592,7 +592,7 @@
     def send_chips(c):
         arrived_copy(c, 1).wait()
         product(
-            c, 0, (chip_out, (c % 3,)), [(first_loc, (c % 4, 0)), (second_loc, (c % 2, 0))]
+            c, 0, (chip_out, (c % 3,)), [(first_loc, (c % 5, 0)), (second_loc, (c % 2, 0))]
         )
         for by in range(1, chips):
             to_chip(c, by).start()
@@ -690,8 +690,10 @@
     stages = [
         load,
         send_first,
+        None,
         take_first,
         send_second,
+        None,
         take_second,
         send_chips,
         take_chips,
@@ -701,7 +703,7 @@
     ]
     for tick in range(n + len(stages) - 1):
         for at, stage in enumerate(stages):
-            if 0 <= tick - at < n:
+            if stage is not None and 0 <= tick - at < n:
                 stage(tick - at)
 
 
@@ -789,11 +791,11 @@
         out_specs=[hbm] * len(shapes),
         out_shape=shapes,
         scratch_shapes=[
-            pltpu.VMEM((6, depth, wide), BF16),
+            pltpu.VMEM((8, depth, wide), BF16),
             pltpu.VMEM((reps, rows, depth), BF16),
-            pltpu.VMEM((3, 2, rows, wide), BF16),
             pltpu.VMEM((4, 2, rows, wide), BF16),
-            pltpu.VMEM((3, 1, rows, wide), BF16),
+            pltpu.VMEM((5, 2, rows, wide), BF16),
+            pltpu.VMEM((4, 1, rows, wide), BF16),
             pltpu.VMEM((2, 1, rows, wide), BF16),
             pltpu.VMEM((3, rows, wide), BF16),
             pltpu.VMEM((2, chips - 1, max(subs), wide), BF16),
@@ -905,7 +907,7 @@
 
 def lru_forward_kernel(
     block, branch_ref, tail_ref, rate_ref, input_ref, taps_ref, decay_ref,
-    coef_ref, cum_ref, state_ref, a_ref, b_ref,
+    coef_ref, cum_ref, state_ref, cum_last_ref, state_last_ref, a_ref, b_ref,
 ):
     conv = conv_rows(branch_ref[0], tail_ref[0], taps_ref[...])
     low = conv.astype(BF16)
@@ -915,11 +917,14 @@
     drive = jnp.sqrt(one_minus_exp(2.0 * log_coef)) * gate * conv
     coef_ref[0] = coef
     scan_rows(coef, drive, a_ref, b_ref, cum_ref, state_ref, False)
+    rows = coef.shape[0]
+    cum_last_ref[0] = cum_ref[0, rows - 8 :, :]
+    state_last_ref[0] = state_ref[0, rows - 8 :, :]
 
 
 def lru_adjoint_kernel(
     gated_ref, coef_ref, cum_ref, local_ref, start_ref, back_ref,
-    later_ref, adjoint_ref, gated_back_ref, a_ref, b_ref,
+    later_ref, adjoint_ref, gated_back_ref, first_ref, a_ref, b_ref,
 ):
     value, slope = gelu_parts(gated_ref[0])
     back = back_ref[0].astype(F32)
@@ -930,6 +935,7 @@
     last = lax.broadcasted_iota(jnp.int32, coef.shape, 0) == rows - 1
     coef_next = jnp.where(last, 1.0, pltpu.roll(coef, rows - 1, 0))
     scan_rows(coef_next, back * value, a_ref, b_ref, later_ref, adjoint_ref, True)
+    first_ref[0] = coef[:8] * adjoint_ref[0, :8, :]
 
 
 def lru_backward_kernel(
@@ -1230,7 +1236,6 @@
     )
     out_ordered = ordered(attn_out).astype(BF16)
     out_halves = out_ordered[:, : width // 2], out_ordered[:, width // 2 :]
-    attn_halves = tuple(jnp.concatenate(both, axis=1) for both in zip(qkv_halves, out_halves))
     qkv_width = half + head_size
     ff_unit = first_down.shape[0]
     lru_unit = mixer_out.shape[0]
@@ -1239,11 +1244,12 @@
     tap_count = conv_taps.shape[1]
     spare = block_width - tap_count - 1
     second_chip = chip_rows(*split_columns((second_gate, second_up), ff_unit, reps))
-    attn_halves, second_chip = lax.optimization_barrier((attn_halves, second_chip))
+    qkv_halves, second_chip = lax.optimization_barrier((qkv_halves, second_chip))
     second_in_w = gather_plain(second_chip, True)
-    attn_wide, first_in_w, first_down_w, lru_in_w, mix_wide, second_down_w = gather_all(
+    qkv_own, attn_own, first_in_w, first_down_w, lru_in_w, small_w, mix_w, second_down_w = gather_all(
         (
-            chip_rows(by_core(*attn_halves), by_core(*attn_halves[::-1])),
+            chip_rows(by_core(*qkv_halves), by_core(*qkv_halves[::-1])),
+            chip_rows(by_core(*out_halves), by_core(*out_halves[::-1])),
             chip_rows(*split_columns((first_gate, first_up), ff_unit, reps)),
             ordered(first_down).astype(BF16),
             chip_rows(*split_columns((branch_proj, gated_proj), lru_unit)),
@@ -1254,24 +1260,19 @@
                     conv_taps,
                     decay_rate[:, None],
                     jnp.zeros((lru_unit, spare), BF16),
-                    ordered(mixer_out).astype(BF16),
                 ],
                 axis=1,
             ),
+            ordered(mixer_out).astype(BF16),
             ordered(second_down).astype(BF16),
         ),
-        (True, True, True, True, False, True),
-        (1792, 1536, 1536, 1024, 1920, 1536),
-    )
-    qkv_own = attn_wide[:, :qkv_width]
-    gains = attn_wide[:, qkv_width : qkv_width + 128].astype(F32)
+        (True, True, True, True, True, False, False, True),
+        (1024, 768, 1536, 1536, 1024, 384, 1536, 1536),
+    )
+    gains = qkv_own[:, qkv_width:].astype(F32)
     gain_attn, gain_first, gain_mix, gain_second = (gains[:, i] for i in range(4))
-    attn_own = attn_wide[:, qkv_width + 128 :]
     qkv_sib = swap_cores(qkv_own)
     attn_sib = swap_cores(attn_own)
-
-    small_w = mix_wide[:, : 3 * block_width]
-    mix_w = mix_wide[:, 3 * block_width :]
 
     inputs = ordered(tokens_in.reshape(row_count, width))
     attn_normed = rms_norm(inputs, gain_attn).astype(BF16)
@@ -1279,7 +1280,9 @@
     qkv_other = matmul(attn_normed, qkv_sib).astype(BF16)
     qkv_first, qkv_second = by_core(qkv_mine, qkv_other), by_core(qkv_other, qkv_mine)
     query_rows = jnp.concatenate([qkv_first[:, :half], qkv_second[:, :half]], axis=1)
-    kv_rows = jnp.concatenate([qkv_first[:, half:], qkv_second[:, half:]], axis=1)
+    kv_rows = jnp.concatenate(
+        [qkv_first[:, half:qkv_width], qkv_second[:, half:qkv_width]], axis=1
+    )
     blocks_behind = -(-WINDOW // row_count)
     behind = blocks_behind * row_count
     kv_win = jnp.concatenate(
@@ -1324,14 +1327,14 @@
     wide_low = (jax.ShapeDtypeStruct((2, row_count, lru_width), BF16), "first")
     edge = (jax.ShapeDtypeStruct((2, 8, lru_width), F32), "edge")
     scans = [pltpu.VMEM((row_count, 256), F32)] * 2
-    lru_coef, cum_coef, local_state = lru_call(
+    lru_coef, cum_coef, local_state, cum_last, state_last = lru_call(
         functools.partial(lru_forward_kernel, block_width),
         lru_inputs,
-        [wide, wide, wide],
+        [wide, wide, wide, edge, edge],
         row_count,
         scans,
     )
-    start_state = carried_in(cum_coef[:, -1], local_state[:, -1], False)
+    start_state = carried_in(cum_last[:, 7], state_last[:, 7], False)
     start_edge = jnp.broadcast_to(start_state[:, None], edge[0].shape)
     gated_act = gelu_tanh(branch_gated[:, :, lru_width:])
     mix_low = ((local_state + cum_coef * start_state[:, None]) * gated_act).astype(BF16)
@@ -1367,7 +1370,7 @@
 
     mix_back_low = with_sibling(back_two.astype(BF16))
     back_mixed = matmul_right(mix_back_low, mix_w).astype(BF16).reshape(wide[0].shape)
-    later_prod, local_adjoint, gated_back_low = lru_call(
+    later_prod, local_adjoint, gated_back_low, out_first = lru_call(
         lru_adjoint_kernel,
         [
             (branch_gated, "second"),
@@ -1377,12 +1380,12 @@
             (start_edge, "edge"),
             (back_mixed, "first"),
         ],
-        [wide, wide, wide_low],
+        [wide, wide, wide_low, edge],
         row_count,
         scans,
     )
     gated_back_low = gated_back_low.reshape(2 * row_count, lru_width)
-    carry_in = carried_in(cum_coef[:, -1], lru_coef[:, 0] * local_adjoint[:, 0], True)
+    carry_in = carried_in(cum_last[:, 7], out_first[:, 0], True)
     carry_edge = jnp.broadcast_to(carry_in[:, None], edge[0].shape)
     branch_back, first_rows, last_rows, grad_rate, grad_input, grad_taps, grad_decay = lru_call(
         functools.partial(lru_backward_kernel, block_width),
@@ -1464,7 +1467,10 @@
     back_second = jnp.concatenate([back_query[:, half:], back_kv[:, head_size:]], axis=1)
     qkv_back_mine = by_core(back_first, back_second)
     qkv_back_other = by_core(back_second, back_first)
-    back_attn_normed = matmul_right(qkv_back_mine, qkv_own) + matmul_right(qkv_back_other, qkv_sib)
+    gain_pad = ((0, 0), (0, 128))
+    back_attn_normed = matmul_right(jnp.pad(qkv_back_mine, gain_pad), qkv_own) + matmul_right(
+        jnp.pad(qkv_back_other, gain_pad), qkv_sib
+    )
     back_inputs_norm, grad_attn_gain = jax.vjp(rms_norm, inputs, gain_attn)[1](back_attn_normed)
     input_grad = (
         unordered((back_one + back_inputs_norm).astype(BF16))
@@ -1475,16 +1481,17 @@
     gain_given = jnp.stack([grad_attn_gain, first_grads[0], grad_mix_gain, second_grads[0]])
     gain_given = jnp.pad(gain_given, ((0, 124), (0, 0))).astype(BF16).T.reshape(reps, -1, 128)
     qkv_right = jnp.concatenate([qkv_back_mine, swap_cores(qkv_back_other)], axis=0)
-    second_in = lax.all_gather(in_part, "rep", axis=0, tiled=True)
-    second_down_rows = lax.all_gather(down_part, "rep", axis=0, tiled=True)
-    second_in, second_down_rows, gain_given = lax.optimization_barrier(
-        (second_in, second_down_rows, gain_given)
-    )
-
     def by_reps(x):
         parts = x.reshape(chips, reps, -1, x.shape[1]).transpose(1, 0, 2, 3)
         return parts.reshape(reps, -1, x.shape[1])
 
+    sub = lru_unit // reps
+    spot = lax.broadcasted_iota(jnp.int32, (lru_width, lru_width), 1)
+    source = (
+        lax.rem(spot // sub, chips) * lru_unit + (spot // (sub * chips)) * sub + lax.rem(spot, sub)
+    )
+    to_reps = lax.broadcasted_iota(jnp.int32, (lru_width, lru_width), 0) == source
+    mix_by_reps = matmul(mix_low, to_reps.astype(BF16)).astype(BF16)
     lru_in, first_in, first_down_rows, qkv_rows, out_rows, gain_rows, mix_rows, small_rows = (
         reduce_all(
             [
@@ -1494,12 +1501,15 @@
                 (with_sibling(attn_normed), [qkv_right], 512),
                 (with_sibling(attended_low), [out_right], 768),
                 (None, [gain_given], 128),
-                (by_reps(mix_low.T).reshape(lru_width, -1).T, [mix_back_low], 768),
+                (mix_by_reps, [mix_back_low], 768),
                 (None, [by_reps(grad_small)], 384),
             ]
         )
     )
 
+    lru_in, in_part, down_part = lax.optimization_barrier((lru_in, in_part, down_part))
+    second_in = lax.all_gather(in_part, "rep", axis=0, tiled=True)
+    second_down_rows = lax.all_gather(down_part, "rep", axis=0, tiled=True)
     grad_mixer_out = unordered(mix_rows)
     small = small_rows.astype(F32)
 

time: 1530 us -> 1490 us (0.974)
  local copies, waits for them, and re-layouts: 91.3 us -> 51.6 us
  waiting for transfers between devices: 126 us -> 102 us
    reduce_scatter x1, waiting for transfers between devices: 24.4 us -> 0.02 us  [on_device(): lax.psum_scatter(in_part, 'shard', scatter_dimension=0, tiled=True, axis_...]
    dot_general x17 -> x18, matrix products: 122 us -> 129 us  [matmul(): return jnp.dot(first_op, second_op, preferred_element_type=F32)]
    ppermute x28 -> x29, waiting for transfers between devices: 38.8 us -> 32.9 us  [swap_cores(): return lax.ppermute(x, 'shard', [(i, i ^ 1) for i in range(count)])]
  transfers between devices with their start and end apart: 48 -> 49, of which waited for: 23 -> 18; matrix products, arithmetic and copies ran while one was open for 28% -> 28% of each run, Pallas kernels for 9% -> 38%
where the time goes in v3:
time: 1490 us; the launch traced here: 1480 us
  Pallas kernels  860 us (58%)
  matrix products  314 us (21%)
  waiting for transfers between devices  102 us (7%)
  other arithmetic  87.9 us (6%)
  local copies, waits for them, and re-layouts  51.6 us (3%)
  starting transfers between devices  42 us (3%)
  between operations  19.2 us (1%)
    pallas_call x1, Pallas kernels, reduce_all(): pl.pallas_call(functools.partial(reduce_kernel, chunks, (len(lefts), len(...  422 us
    pallas_call x1, Pallas kernels, gather_all(): pl.pallas_call(functools.partial(gather_kernel, chunks, len(arrays), chip...  283 us
    dot_general x16, matrix products, matmul_right(): lax.dot_general(first_op, second_op, (((1,), (1,)), ((), ())), preferred_...  151 us
    dot_general x18, matrix products, matmul(): return jnp.dot(first_op, second_op, preferred_element_type=F32)  129 us
    pallas_call x2, Pallas kernels, attention_call(): pl.pallas_call(kernel, grid_spec=pltpu.PrefetchScalarGridSpec(num_scalar_...  67.5 us
    pallas_call x3, Pallas kernels, lru_call(): pl.pallas_call(kernel, grid=(width // lanes, 2), in_specs=[spec(kind) for...  56.3 us
    ppermute x12, starting transfers between devices, shift_rep(): lax.ppermute(x, 'rep', [(i, i + by) for i in range(size) if 0 <= i + by <...  35.3 us
    dot_general x2, matrix products, matmul_left(): lax.dot_general(first_op, second_op, (((0,), (0,)), ((), ())), preferred_...  34.1 us
  transfers between devices with their start and end apart: 49, of which 18 were waited for; matrix products, arithmetic and copies ran while one was open for 28% of the time, Pallas kernels for 38%

profile of v3, /device:TPU:0, one launch (start us, length us, event | category | flops | bytes accessed | tf_op | source)
XLA Modules:
  0.0 1475.9 jit_solution(3673744320950581600)
XLA Ops:
  53.1 283.1 %shard_map.410 = (bf16[1536,1024]{1,0:T(8,128)(2,1)S(1)}, bf16[1536,768]{1,0:T(8,128)(2,1)S(1)}, bf16[1536,4608]{1,0:T(8,128)(2,1)}, bf16[2304,1536]{1,0:T(8,128...) custom-call(bf16[384,1024]{1,0:T(8,128)(2,1)S(1)} %pad_maximum_fusio, ...), custom_call_target="tpu_custom_call" | custom-call | bytes 385351680 | tf_op jit(solution)/shard_map/pallas_call | solution.py:415
  355.8 15.1 %collective-permute-start.7 = (bf16[512,256]{1,0:T(8,128)(2,1)S(1)}, bf16[512,256]{1,0:T(8,128)(2,1)S(1)}, u32[]{:S(2)}, u32[]{:S(2)}) collective-permute-start(bf16[512,256]{1,0:T(8,128)(2,1)S(1)} %pad_maximum_fusion.25), channel_id=1, source_target_pairs={{0,8},{8,16},{16,24},{1,9},{9,17},{17,25},{2,10},{10,18},{18,26},{... | collective-permute-start | bytes 786440 | tf_op jit(solution)/shard_map/ppermute | solution.py:67
  373.3 23.3 %shard_map.411 = bf16[512,1536]{1,0:T(8,128)(2,1)} custom-call(s32[1]{0:T(128)} %bitcast.2.start_ref, bf16[512,1536]{1,0:T(8,128)(2,1)} %pad_maximum_fusion.19.query_ref, bf16[1536,256]{1,0:T(8,128)(2,1)} %maximum_maximum_fusion.kv_ref), custom_call_target="tpu_custom_call" | custom-call | flops 9663676416 | bytes 67108864 | tf_op jit(solution)/shard_map/pallas_call | solution.py:1130
  414.3 22.3 %fusion.154 = f32[1024,4608]{1,0:T(8,128)} fusion(bf16[1536,4608]{1,0:T(8,128)(2,1)} %get-tuple-element.89, bf16[512,1536]{1,0:T(8,128)(2,1)} %collective-permute-done.9, bf16[512,1536]{1,0:T(8,128)(2,1)} %multiply_convert_fusion.4), kind=kOutput, calls=%fused_computation.333 | convolution fusion | flops 14501806080 | bytes 36175872 | tf_op jit(solution)/shard_map/dot_general | solution.py:33
  436.6 13.9 fusion.170
  462.6 11.2 fusion.153
  480.2 18.7 %shard_map.412 = (f32[2,512,1024]{2,1,0:T(8,128)}, f32[2,512,1024]{2,1,0:T(8,128)}, f32[2,512,1024]{2,1,0:T(8,128)}, f32[2,8,1024]{2,1,0:T(8,128)}, f32[2,8,1024]{2,1,0:T(8,128)}) custom-call(f32[2,512,2048]{2,1,0:T(8,128)} %bitcast.8.branch_ref.gated_ref, f32[2,8,1024]{2,1,0:T(8,128)} %copy-done.61, bf16[1024,128]{1,0:T(8,128)(2,1)} %get-tuple-element.268.rate_ref, ...), custom_call_target="tpu_custom_call" | custom-call | bytes 33554432 | tf_op jit(solution)/shard_map/pallas_call | solution.py:1037
  535.0 12.1 all-gather.7.cloned.1.call-done
  547.1 21.1 %fusion.73 = f32[1024,4608]{1,0:T(8,128)} fusion(bf16[1536,4608]{1,0:T(8,128)(2,1)} %all-gather.7.cloned.1.call-done, bf16[512,1536]{1,0:T(8,128)(2,1)} %collective-permute-done.17, bf16[512,1536]{1,0:T(8,128)(2,1)} %copy-done.52), kind=kOutput, calls=%fused_computation.146 | convolution fusion | flops 14501806080 | bytes 36175872 | tf_op jit(solution)/shard_map/dot_general | solution.py:33
  568.2 22.8 %fusion.15 = (bf16[1024,2304]{1,0:T(8,128)(2,1)}, bf16[1024,2304]{1,0:T(8,128)(2,1)}, bf16[1024,2304]{1,0:T(8,128)(2,1)}) fusion(f32[1024,4608]{1,0:T(8,128)} %fusion.73, bf16[2304,1536]{1,0:T(8,128)(2,1)} %get-tuple-element.99, bf16[512,1536]{1,0:T(8,128)(2,1)} %collective-permute-done.19, bf16[512,1536]{1,0:T(8,128)(2,1)} %get-tuple-element.282), kind=kOutput, calls=%fused_computation.29 | convolution fusion | flops 7320109056 | bytes 43253760 | tf_op jit(solution)/shard_map/dot_general | solution.py:43
  591.0 12.5 convolution_convert_fusion.1
  603.6 21.6 %convolution_convert_fusion = bf16[1536,4608]{1,0:T(8,128)(2,1)} fusion(bf16[1024,2304]{1,0:T(8,128)(2,1)} %get-tuple-element.233, bf16[1024,2304]{1,0:T(8,128)(2,1)} %get-tuple-element.232, bf16[512,1536]{1,0:T(8,128)(2,1)} %collective-permute-done.17, bf16[512,1536]{1,0:T(8,128)(2,1)} %copy-done.52), kind=kOutput, calls=%fused_computation | convolution fusion | flops 14527758336 | bytes 26738688 | tf_op jit(solution)/shard_map/dot_general | solution.py:37
  625.2 19.5 %fusion.25 = f32[1024,1536]{1,0:T(8,128)S(1)} fusion(bf16[1536,4608]{1,0:T(8,128)(2,1)} %all-gather.7.cloned.1.call-done, bf16[1024,2304]{1,0:T(8,128)(2,1)} %get-tuple-element.233, bf16[1024,2304]{1,0:T(8,128)(2,1)} %get-tuple-element.232), kind=kOutput, calls=%fused_computation.49 | convolution fusion | flops 14514388992 | bytes 29884416 | tf_op jit(solution)/shard_map/dot_general | solution.py:43
  658.5 7.9 convolution_convert_fusion.12
  667.0 16.4 %shard_map.413 = (f32[2,512,1024]{2,1,0:T(8,128)}, f32[2,512,1024]{2,1,0:T(8,128)}, bf16[2,512,1024]{2,1,0:T(8,128)(2,1)}, f32[2,8,1024]{2,1,0:T(8,128)}) custom-call(f32[2,512,2048]{2,1,0:T(8,128)} %bitcast.8.branch_ref.gated_ref, f32[2,512,1024]{2,1,0:T(8,128)} %get-tuple-element.100.coef_ref, f32[2,512,1024]{2,1,0:T(8,128)} %get-tuple-element.94.cum_ref, ...), custom_call_target="tpu_custom_call" | custom-call | bytes 33554432 | tf_op jit(solution)/shard_map/pallas_call | solution.py:1037
  693.4 21.2 %shard_map.414 = (bf16[2,512,1024]{2,1,0:T(8,128)(2,1)}, f32[2,8,1024]{2,1,0:T(8,128)}, f32[2,8,1024]{2,1,0:T(8,128)}, f32[1024,128]{1,0:T(8,128)}, f32[1024,128...) custom-call(f32[2,512,2048]{2,1,0:T(8,128)} %bitcast.8.branch_ref.gated_ref, f32[2,8,1024]{2,1,0:T(8,128)} %copy-done.61, ...), custom_call_target="tpu_custom_call" | custom-call | bytes 33554432 | tf_op jit(solution)/shard_map/pallas_call | solution.py:1037
  715.9 7.2 collective-permute-done.25
  724.6 9.6 fusion.40
  735.1 7.4 collective-permute-done.26
  749.1 21.9 %fusion.8 = (bf16[1024,2304]{1,0:T(8,128)(2,1)}, bf16[1024,2304]{1,0:T(8,128)(2,1)}) fusion(f32[1024,4608]{1,0:T(8,128)} %fusion.154, bf16[2304,1536]{1,0:T(8,128)(2,1)} %get-tuple-element.90, bf16[512,1536]{1,0:T(8,128)(2,1)} %collective-permute-done.27, bf16[512,1536]{1,0:T(8,128)(2,1)} %copy-done.26), kind=kOutput, calls=%fused_computation.22 | convolution fusion | flops 7315390464 | bytes 38535168 | tf_op jit(solution)/shard_map/dot_general | solution.py:43
  771.1 19.3 %fusion.21 = f32[1024,1536]{1,0:T(8,128)S(1)} fusion(bf16[1536,4608]{1,0:T(8,128)(2,1)} %get-tuple-element.89, bf16[1024,2304]{1,0:T(8,128)(2,1)} %get-tuple-element.231.refs_9_, bf16[1024,2304]{1,0:T(8,128)(2,1)} %get-tuple-element.230.refs_8_), kind=kOutput, calls=%fused_computation.36 | convolution fusion | flops 14514388992 | bytes 29884416 | tf_op jit(solution)/shard_map/dot_general | solution.py:43
  794.2 11.1 fusion.230
  805.3 6.7 copy.91
  835.3 11.3 fusion.172
  861.9 8.5 convolution_convert_fusion.7.back_ref
  870.4 44.2 %shard_map.415 = (bf16[512,1536]{1,0:T(8,128)(2,1)}, f32[1536,256]{1,0:T(8,128)}) custom-call(s32[1]{0:T(128)} %bitcast.2.start_ref, bf16[512,1536]{1,0:T(8,128)(2,1)} %pad_maximum_fusion.19.query_ref, bf16[512,1536]{1,0:T(8,128)(2,1)} %convolution_convert_fusion.7.back_ref, bf16[1536,256]{1,0:T(8,128)(2,1)} %maximum_maximum_fusion.kv_ref), custom_call_target="tpu_custom_call" | custom-call | flops 9663676416 | bytes 67108864 | tf_op jit(solution)/shard_map/pallas_call | solution.py:1130
  922.7 10.0 collective-permute-done.29
  950.9 422.5 %shard_map.416 = (bf16[384,2048]{1,0:T(8,128)(2,1)}, bf16[384,4608]{1,0:T(8,128)(2,1)}, bf16[576,1536]{1,0:T(8,128)(2,1)}, bf16[384,896]{1,0:T(8,128)(2,1)}, bf1...) custom-call(bf16[1024,1536]{1,0:T(8,128)(2,1)} %pad_maximum_fusion.6, ...), custom_call_target="tpu_custom_call" | custom-call | bytes 591396864 | tf_op jit(solution)/shard_map/pallas_call | solution.py:784
  1373.6 8.4 fusion.58
  1407.0 13.9 all-gather.9.cloned.1.call-done
  1441.2 14.3 all-gather.11.cloned.1.call-done
  1455.5 7.1 fusion.176
  (484 shorter events, 290.8 us)
Async XLA Ops:
  7.2 403.4 %all-gather.5.cloned.1.call-start = ((), (), s32[]{:S(2)}) async-start(), calls=%async_computation.4 | async-start | bytes 4423680 | tf_op jit(solution)/shard_map/all_gather | solution.py:392
  12.6 31.4 %collective-permute-start = (bf16[192,4608]{1,0:T(8,128)(2,1)}, bf16[192,4608]{1,0:T(8,128)(2,1)}, u32[]{:S(2)}, u32[]{:S(2)}) collective-permute-start(bf16[192,4608]{1,0:T(8,128)(2,1)} %get-tuple-element.80), channel_id=1, source_target_pairs={{0,1},{1,0},{2,3},{3,2},{4,5},{5,4},{6,7},{7,6},{8,9},{9,8},{10,11... | collective-permute-start | bytes 5308424 | tf_op jit(solution)/shard_map/ppermute | solution.py:62
  17.2 24.1 %collective-permute-start.2 = (bf16[192,768]{1,0:T(8,128)(2,1)}, bf16[192,768]{1,0:T(8,128)(2,1)}, u32[]{:S(2)}, u32[]{:S(2)}) collective-permute-start(bf16[192,768]{1,0:T(8,128)(2,1)} %broadcast_select_fusion.24), channel_id=1, source_target_pairs={{0,1},{1,0},{2,3},{3,2},{4,5},{5,4},{6,7},{7,6},{8,9},{9,8},{10,11... | collective-permute-start | bytes 884744 | tf_op jit(solution)/shard_map/ppermute | solution.py:62
  22.4 24.3 %collective-permute-start.3 = (bf16[192,4608]{1,0:T(8,128)(2,1)}, bf16[192,4608]{1,0:T(8,128)(2,1)}, u32[]{:S(2)}, u32[]{:S(2)}) collective-permute-start(bf16[192,4608]{1,0:T(8,128)(2,1)} %get-tuple-element.84), channel_id=1, source_target_pairs={{0,1},{1,0},{2,3},{3,2},{4,5},{5,4},{6,7},{7,6},{8,9},{9,8},{10,11... | collective-permute-start | bytes 5308424 | tf_op jit(solution)/shard_map/ppermute | solution.py:62
  26.5 16.0 %collective-permute-start.4 = (bf16[192,2048]{1,0:T(8,128)(2,1)}, bf16[192,2048]{1,0:T(8,128)(2,1)}, u32[]{:S(2)}, u32[]{:S(2)}) collective-permute-start(bf16[192,2048]{1,0:T(8,128)(2,1)} %get-tuple-element.86), channel_id=1, source_target_pairs={{0,1},{1,0},{2,3},{3,2},{4,5},{5,4},{6,7},{7,6},{8,9},{9,8},{10,11... | collective-permute-start | bytes 2359304 | tf_op jit(solution)/shard_map/ppermute | solution.py:62
  336.3 12.6 collective-permute-start.5
  341.8 205.3 %all-gather.7.cloned.1.call-start = ((), (), s32[]{:S(2)}) async-start(), calls=%async_computation.5 | async-start | bytes 17694720 | tf_op jit(solution)/shard_map/all_gather | solution.py:393
  341.9 62.8 %collective-permute-start.8 = (bf16[1536,768]{1,0:T(8,128)(2,1)}, bf16[1536,768]{1,0:T(8,128)(2,1)}, u32[]{:S(2)}, u32[]{:S(2)}) collective-permute-start(bf16[1536,768]{1,0:T(8,128)(2,1)} %copy-done.8), channel_id=1, source_target_pairs={{0,1},{1,0},{2,3},{3,2},{4,5},{5,4},{6,7},{7,6},{8,9},{9,8},{10,11... | collective-permute-start | bytes 7077896 | tf_op jit(solution)/shard_map/ppermute | solution.py:62
  353.2 19.1 %collective-permute-start.6 = (bf16[512,256]{1,0:T(8,128)(2,1)S(1)}, bf16[512,256]{1,0:T(8,128)(2,1)S(1)}, u32[]{:S(2)}, u32[]{:S(2)}) collective-permute-start(bf16[512,256]{1,0:T(8,128)(2,1)S(1)} %pad_maximum_fusion.25), channel_id=1, source_target_pairs={{0,16},{8,24},{1,17},{9,25},{2,18},{10,26},{3,19},{11,27},{4,20},{... | collective-permute-start | bytes 786440 | tf_op jit(solution)/shard_map/ppermute | solution.py:67
  355.8 16.5 %collective-permute-start.7 = (bf16[512,256]{1,0:T(8,128)(2,1)S(1)}, bf16[512,256]{1,0:T(8,128)(2,1)S(1)}, u32[]{:S(2)}, u32[]{:S(2)}) collective-permute-start(bf16[512,256]{1,0:T(8,128)(2,1)S(1)} %pad_maximum_fusion.25), channel_id=1, source_target_pairs={{0,8},{8,16},{16,24},{1,9},{9,17},{17,25},{2,10},{10,18},{18,26},{... | collective-permute-start | bytes 786440 | tf_op jit(solution)/shard_map/ppermute | solution.py:67
  410.6 333.8 %reduce-scatter.5.cloned.1.call-start = ((), (), s32[]{:S(2)}) async-start(), calls=%async_computation.6 | async-start | bytes 8847360 | tf_op jit(solution)/shard_map/reduce_scatter | solution.py:1358
  534.9 33.3 %collective-permute-start.19 = (bf16[512,1536]{1,0:T(8,128)(2,1)}, bf16[512,1536]{1,0:T(8,128)(2,1)}, u32[]{:S(2)}, u32[]{:S(2)}) collective-permute-start(bf16[512,1536]{1,0:T(8,128)(2,1)} %get-tuple-element.282), channel_id=1, source_target_pairs={{0,1},{1,0},{2,3},{3,2},{4,5},{5,4},{6,7},{7,6},{8,9},{9,8},{10,11... | collective-permute-start | bytes 4718600 | tf_op jit(solution)/shard_map/ppermute | solution.py:62
  603.5 231.7 %reduce-scatter.7.cloned.1.call-start = ((), (), s32[]{:S(2)}) async-start(), calls=%async_computation.7 | async-start | bytes 17694720 | tf_op jit(solution)/shard_map/reduce_scatter | solution.py:1361
  625.1 748.2 %reduce-scatter.11.cloned.1.call-start = ((), (), s32[]{:S(2)}) async-start(), calls=%async_computation.9 | async-start | bytes 2211840 | tf_op jit(solution)/shard_map/reduce_scatter | solution.py:1423
  714.5 8.5 collective-permute-start.25
  734.6 10.3 collective-permute-start.31
  748.9 66.9 %collective-permute-start.32 = (bf16[512,1536]{1,0:T(8,128)(2,1)}, bf16[512,1536]{1,0:T(8,128)(2,1)}, u32[]{:S(2)}, u32[]{:S(2)}) collective-permute-start(bf16[512,1536]{1,0:T(8,128)(2,1)} %convolution_convert_fusion.9), channel_id=1, source_target_pairs={{0,1},{1,0},{2,3},{3,2},{4,5},{5,4},{6,7},{7,6},{8,9},{9,8},{10,11... | collective-permute-start | bytes 4718600 | tf_op jit(solution)/shard_map/ppermute | solution.py:62
  793.9 33.1 %collective-permute-start.28 = (f32[512,1536]{1,0:T(8,128)}, f32[512,1536]{1,0:T(8,128)}, u32[]{:S(2)}, u32[]{:S(2)}) collective-permute-start(f32[512,1536]{1,0:T(8,128)} %slice.344), channel_id=1, source_target_pairs={{0,1},{1,0},{2,3},{3,2},{4,5},{5,4},{6,7},{7,6},{8,9},{9,8},{10,11... | collective-permute-start | bytes 9437192 | tf_op jit(solution)/shard_map/ppermute | solution.py:62
  812.0 561.4 %reduce-scatter.9.cloned.1.call-start = ((), (), s32[]{:S(2)}) async-start(), calls=%async_computation.8 | async-start | bytes 4423680 | tf_op jit(solution)/shard_map/reduce_scatter | solution.py:1442
  835.2 585.7 %all-gather.9.cloned.1.call-start = ((), (), s32[]{:S(2)}) async-start(), calls=%async_computation.10 | async-start | bytes 4423680 | tf_op jit(solution)/shard_map/all_gather | solution.py:1511
  850.8 522.7 %collective-permute-start.18 = (f32[512,1536]{1,0:T(8,128)}, f32[512,1536]{1,0:T(8,128)}, u32[]{:S(2)}, u32[]{:S(2)}) collective-permute-start(f32[512,1536]{1,0:T(8,128)} %slice.330), channel_id=1, source_target_pairs={{0,1},{1,0},{2,3},{3,2},{4,5},{5,4},{6,7},{7,6},{8,9},{9,8},{10,11... | collective-permute-start | bytes 9437192 | tf_op jit(solution)/shard_map/ppermute | solution.py:62
  916.0 16.7 %collective-permute-start.29 = (f32[512,256]{1,0:T(8,128)S(1)}, f32[512,256]{1,0:T(8,128)S(1)}, u32[]{:S(2)}, u32[]{:S(2)}) collective-permute-start(f32[512,256]{1,0:T(8,128)S(1)} %get-tuple-element.253), channel_id=1, source_target_pairs={{8,0},{16,8},{24,16},{9,1},{17,9},{25,17},{10,2},{18,10},{26,18},{... | collective-permute-start | bytes 1572872 | tf_op jit(solution)/shard_map/ppermute | solution.py:67
  917.4 18.0 %collective-permute-start.30 = (f32[512,256]{1,0:T(8,128)S(1)}, f32[512,256]{1,0:T(8,128)S(1)}, u32[]{:S(2)}, u32[]{:S(2)}) collective-permute-start(f32[512,256]{1,0:T(8,128)S(1)} %get-tuple-element.254), channel_id=1, source_target_pairs={{16,0},{24,8},{17,1},{25,9},{18,2},{26,10},{19,3},{27,11},{20,4},{... | collective-permute-start | bytes 1572872 | tf_op jit(solution)/shard_map/ppermute | solution.py:67
  922.1 25.0 %collective-permute-start.34 = (bf16[512,768]{1,0:T(8,128)(2,1)}, bf16[512,768]{1,0:T(8,128)(2,1)}, u32[]{:S(2)}, u32[]{:S(2)}) collective-permute-start(bf16[512,768]{1,0:T(8,128)(2,1)} %get-tuple-element.255), channel_id=1, source_target_pairs={{0,1},{1,0},{2,3},{3,2},{4,5},{5,4},{6,7},{7,6},{8,9},{9,8},{10,11... | collective-permute-start | bytes 2359304 | tf_op jit(solution)/shard_map/ppermute | solution.py:62
  937.8 11.7 collective-permute-start.33
  1373.4 82.1 %all-gather.11.cloned.1.call-start = ((), (), s32[]{:S(2)}) async-start(), calls=%async_computation.11 | async-start | bytes 2211840 | tf_op jit(solution)/shard_map/all_gather | solution.py:1512
  1388.8 41.4 %collective-permute-start.38 = (bf16[192,4608]{1,0:T(8,128)(2,1)}, bf16[192,4608]{1,0:T(8,128)(2,1)}, u32[]{:S(2)}, u32[]{:S(2)}) collective-permute-start(bf16[192,4608]{1,0:T(8,128)(2,1)} %get-tuple-element.237), channel_id=1, source_target_pairs={{0,1},{1,0},{2,3},{3,2},{4,5},{5,4},{6,7},{7,6},{8,9},{9,8},{10,11... | collective-permute-start | bytes 5308424 | tf_op jit(solution)/shard_map/ppermute | solution.py:62
  1389.5 13.7 collective-permute-start.37
  1390.8 35.7 %collective-permute-start.36 = (bf16[192,896]{1,0:T(8,128)(2,1)}, bf16[192,896]{1,0:T(8,128)(2,1)}, u32[]{:S(2)}, u32[]{:S(2)}) collective-permute-start(bf16[192,896]{1,0:T(8,128)(2,1)} %constant_dynamic-slice_fusion.7), channel_id=1, source_target_pairs={{0,1},{1,0},{2,3},{3,2},{4,5},{5,4},{6,7},{7,6},{8,9},{9,8},{10,11... | collective-permute-start | bytes 1032200 | tf_op jit(solution)/shard_map/ppermute | solution.py:62
  1391.4 10.0 collective-permute-start.35
  1425.0 37.6 %collective-permute-start.40 = (bf16[192,4608]{1,0:T(8,128)(2,1)}, bf16[192,4608]{1,0:T(8,128)(2,1)}, u32[]{:S(2)}, u32[]{:S(2)}) collective-permute-start(bf16[192,4608]{1,0:T(8,128)(2,1)} %get-tuple-element.235), channel_id=1, source_target_pairs={{0,1},{1,0},{2,3},{3,2},{4,5},{5,4},{6,7},{7,6},{8,9},{9,8},{10,11... | collective-permute-start | bytes 5308424 | tf_op jit(solution)/shard_map/ppermute | solution.py:62
  1426.0 10.1 collective-permute-start.39
  (123 other events, 1586.3 us)
Sparse Core Ops, SparseCore 0:
  341.9 67.3 all-gather.4
  411.1 135.9 all-gather.6
  603.6 76.7 reduce-scatter.4
  683.4 135.2 reduce-scatter.6
  820.9 38.3 reduce-scatter.10
  861.6 65.4 reduce-scatter.8
  1373.6 47.2 all-gather.8
  1422.9 32.5 all-gather.10
